TPU v7x, 32 devices: a whole 2x2x4 slice. The times are simulated.
32 devices in a mesh: ctx: 4 (over y, x), fsdp: 8 (over z, core).
Axes of the slice: x: 2, y: 2, z: 4, core: 2. Of those that a mesh axis runs over, the one named last changes fastest.
Arguments:
- tokens: bfloat16 [8, 1024, 2048], P('fsdp', 'ctx'), may hold values from -6 to 6
- segments: int32 [8, 1024], P('fsdp', 'ctx'), may hold values from 0 to 510, as said below
- positions: int32 [8, 1024], P('fsdp', 'ctx'), may hold values from 0 to 1023, as said below
- ln1_gain: bfloat16 [2048], P('fsdp'), may hold values from 0.5 to 1.5
- ln1_bias: bfloat16 [2048], P('fsdp'), may hold values from -2 to 2
- ln2_gain: bfloat16 [2048], P('fsdp'), may hold values from 0.5 to 1.5
- ln2_bias: bfloat16 [2048], P('fsdp'), may hold values from -2 to 2
- qkv_weight: bfloat16 [2048, 6144], P('fsdp'), may hold values from -0.125 to 0.125
- qkv_bias: bfloat16 [6144], P('fsdp'), may hold values from -2 to 2
- dense_weight: bfloat16 [2048, 2048], P('fsdp'), may hold values from -0.5 to 0.5
- dense_bias: bfloat16 [2048], P('fsdp'), may hold values from -2 to 2
- fc_in_weight: bfloat16 [2048, 8192], P('fsdp'), may hold values from -0.125 to 0.125
- fc_in_bias: bfloat16 [8192], P('fsdp'), may hold values from -2 to 2
- fc_out_weight: bfloat16 [8192, 2048], P('fsdp'), may hold values from -0.0625 to 0.0625
- fc_out_bias: bfloat16 [2048], P('fsdp'), may hold values from -2 to 2
- cotangent: bfloat16 [8, 1024, 2048], P('fsdp', 'ctx'), may hold values from -6 to 6
Outputs:
- output: bfloat16 [8, 1024, 2048], P('fsdp', 'ctx')
- input_grad: float32 [8, 1024, 2048], P('fsdp', 'ctx')
- ln1_gain_grad: float32 [2048], P('fsdp')
- ln1_bias_grad: float32 [2048], P('fsdp')
- ln2_gain_grad: float32 [2048], P('fsdp')
- ln2_bias_grad: float32 [2048], P('fsdp')
- qkv_weight_grad: float32 [2048, 6144], P('fsdp')
- qkv_bias_grad: float32 [6144], P('fsdp')
- dense_weight_grad: float32 [2048, 2048], P('fsdp')
- dense_bias_grad: float32 [2048], P('fsdp')
- fc_in_weight_grad: float32 [2048, 8192], P('fsdp')
- fc_in_bias_grad: float32 [8192], P('fsdp')
- fc_out_weight_grad: float32 [8192, 2048], P('fsdp')
- fc_out_bias_grad: float32 [2048], P('fsdp')
Inputs may be any that keep to these rules, and one draw needn't show every extreme that they name: `segments`: within each sequence the document numbers start at 0, never fall and rise by at most one from a token to the next; one document of each sequence starts within its first 256 tokens and ends within its last 256 tokens. `positions`: 0 at the first token of each document, else one more than at the token before.
All inputs are finite; a program needn't handle non-finite values.
Results may differ from a plain program's by a relative error of at most 0.015.
Values may be sent and summed in bfloat16 or wider, within the bound.
No kernel may reach another device: no remote copies, remote signals or barrier semaphores. Data moves between devices by JAX's collectives and lax.ppermute only.
A program may use at most 576 MiB of HBM per device.

v0:
```python
import jax
import jax.numpy as jnp
from jax import lax
from jax.sharding import PartitionSpec as P

HEADS = 8


eps_norm = 1e-05


def layer_norm(values, gain_vec, shift_vec):
    row_mean = jnp.mean(values, axis=-1, keepdims=True)
    centred = values - row_mean
    spread = jnp.mean(centred * centred, axis=-1, keepdims=True)
    return centred * lax.rsqrt(spread + eps_norm) * gain_vec + shift_vec


def rotary_tables(position, rotary):
    frequency = 10000.0 ** (-jnp.arange(0, rotary, 2, dtype=jnp.float32) / rotary)
    angles = position.astype(jnp.float32)[:, None] * frequency[None, :]
    angles = jnp.concatenate([angles, angles], axis=-1)
    return (jnp.cos(angles), jnp.sin(angles))


def rotate(values, cosine, sine_table):
    rotary = cosine.shape[-1]
    half_rot = rotary // 2
    turned = jnp.concatenate([-values[..., half_rot:rotary], values[..., :half_rot]], axis=-1)
    rotated_head = values[..., :rotary] * cosine[:, None, :] + turned * sine_table[:, None, :]
    return jnp.concatenate([rotated_head, values[..., rotary:]], axis=-1)


def gelu_exact(tensor):
    return jax.nn.gelu(tensor, approximate=False)


def dot_right(left_side, right_side):
    return lax.dot_general(
        left_side, right_side, (((1,), (1,)), ((), ())), preferred_element_type=jnp.float32
    )


def dot_left(left_side, right_side):
    return lax.dot_general(
        left_side, right_side, (((0,), (0,)), ((), ())), preferred_element_type=jnp.float32
    )


def reduce_grads(weight_one, bias_one, weight_two, bias_two, gain_grad, shift_grad):
    shared = (
        lax.psum_scatter(
            weight_one.astype(jnp.bfloat16), "fsdp", scatter_dimension=0, tiled=True
        ).astype(jnp.float32),
        lax.psum_scatter(
            bias_one.astype(jnp.bfloat16), "fsdp", scatter_dimension=0, tiled=True
        ).astype(jnp.float32),
        lax.psum_scatter(
            weight_two.astype(jnp.bfloat16), "fsdp", scatter_dimension=0, tiled=True
        ).astype(jnp.float32),
        lax.psum_scatter(
            bias_two.astype(jnp.bfloat16), "fsdp", scatter_dimension=0, tiled=True
        ).astype(jnp.float32),
        lax.psum_scatter(
            gain_grad.astype(jnp.bfloat16), "fsdp", scatter_dimension=0, tiled=True
        ).astype(jnp.float32),
        lax.psum_scatter(
            shift_grad.astype(jnp.bfloat16), "fsdp", scatter_dimension=0, tiled=True
        ).astype(jnp.float32),
    )
    return (
        lax.psum(shared[0].astype(jnp.bfloat16), "ctx").astype(jnp.float32),
        lax.psum(shared[1].astype(jnp.bfloat16), "ctx").astype(jnp.float32),
        lax.psum(shared[2].astype(jnp.bfloat16), "ctx").astype(jnp.float32),
        lax.psum(shared[3].astype(jnp.bfloat16), "ctx").astype(jnp.float32),
        lax.psum(shared[4].astype(jnp.bfloat16), "ctx").astype(jnp.float32),
        lax.psum(shared[5].astype(jnp.bfloat16), "ctx").astype(jnp.float32),
    )


def local(
    tokens,
    segments,
    positions,
    ln1_gain,
    ln1_bias,
    ln2_gain,
    ln2_bias,
    qkv_weight,
    qkv_bias,
    dense_weight,
    dense_bias,
    fc_in_weight,
    fc_in_bias,
    fc_out_weight,
    fc_out_bias,
    cotangent,
):
    model_width = tokens.shape[-1]
    values = tokens.reshape(-1, model_width).astype(jnp.float32)
    row_count = values.shape[0]
    head_dim = model_width // HEADS
    score_scale = head_dim ** (-0.5)
    everyone = lax.all_gather(segments, "ctx", axis=1, tiled=True).reshape(-1)
    seq_length = everyone.shape[0]
    own_segment = segments.reshape(-1)
    query_index = lax.axis_index("ctx") * row_count + jnp.arange(row_count, dtype=jnp.int32)
    key_index = jnp.arange(seq_length, dtype=jnp.int32)
    allowed = (own_segment[:, None] == everyone[None, :]) & (
        key_index[None, :] <= query_index[:, None]
    )
    cosine, sine_table = rotary_tables(positions.reshape(-1), head_dim // 4)
    gathered = (
        lax.all_gather(ln1_gain, "fsdp", axis=0, tiled=True),
        lax.all_gather(ln1_bias, "fsdp", axis=0, tiled=True),
        lax.all_gather(ln2_gain, "fsdp", axis=0, tiled=True),
        lax.all_gather(ln2_bias, "fsdp", axis=0, tiled=True),
        lax.all_gather(qkv_weight, "fsdp", axis=0, tiled=True),
        lax.all_gather(qkv_bias, "fsdp", axis=0, tiled=True),
        lax.all_gather(dense_weight, "fsdp", axis=0, tiled=True),
        lax.all_gather(dense_bias, "fsdp", axis=0, tiled=True),
        lax.all_gather(fc_in_weight, "fsdp", axis=0, tiled=True),
        lax.all_gather(fc_in_bias, "fsdp", axis=0, tiled=True),
        lax.all_gather(fc_out_weight, "fsdp", axis=0, tiled=True),
        lax.all_gather(fc_out_bias, "fsdp", axis=0, tiled=True),
    )
    gain_one = gathered[0].astype(jnp.float32)
    shift_one = gathered[1].astype(jnp.float32)
    gain_two = gathered[2].astype(jnp.float32)
    shift_two = gathered[3].astype(jnp.float32)
    normed_one = layer_norm(values, gain_one, shift_one).astype(jnp.bfloat16)
    normed_two = layer_norm(values, gain_two, shift_two).astype(jnp.bfloat16)
    packed = jnp.dot(normed_one, gathered[4], preferred_element_type=jnp.float32) + gathered[
        5
    ].astype(jnp.float32)
    shaped = packed.reshape(row_count, 3, HEADS, head_dim)
    query_low = rotate(shaped[:, 0], cosine, sine_table).astype(jnp.bfloat16)
    key_low = (
        rotate(shaped[:, 1], cosine, sine_table)
        .astype(jnp.bfloat16)
        .reshape(row_count, model_width)
    )
    value_low = shaped[:, 2].astype(jnp.bfloat16).reshape(row_count, model_width)
    keys_all, values_all = (
        lax.all_gather(key_low, "ctx", axis=0, tiled=True),
        lax.all_gather(value_low, "ctx", axis=0, tiled=True),
    )

    def score_block(key_rows):
        raw_scores = jnp.einsum(
            "qhd,khd->hqk",
            query_low,
            key_rows.reshape(seq_length, HEADS, head_dim),
            preferred_element_type=jnp.float32,
        )
        return jnp.where(allowed[None], raw_scores * score_scale, -1e30)

    scores = score_block(keys_all)
    row_max = jnp.max(scores, axis=-1, keepdims=True)
    exp_scores = jnp.exp(scores - row_max)
    row_total = jnp.sum(exp_scores, axis=-1, keepdims=True)
    probs_low = (exp_scores / row_total).astype(jnp.bfloat16)
    log_total = row_max + jnp.log(row_total)
    mixed_heads = jnp.einsum(
        "hqk,khd->qhd",
        probs_low,
        values_all.reshape(seq_length, HEADS, head_dim),
        preferred_element_type=jnp.float32,
    )
    mixed_low = mixed_heads.reshape(row_count, model_width).astype(jnp.bfloat16)
    attn_out = jnp.dot(mixed_low, gathered[6], preferred_element_type=jnp.float32) + gathered[
        7
    ].astype(jnp.float32)
    hidden = jnp.dot(normed_two, gathered[8], preferred_element_type=jnp.float32) + gathered[
        9
    ].astype(jnp.float32)
    active_low = gelu_exact(hidden).astype(jnp.bfloat16)
    mlp_out = jnp.dot(active_low, gathered[10], preferred_element_type=jnp.float32) + gathered[
        11
    ].astype(jnp.float32)
    output = (values + attn_out + mlp_out).astype(jnp.bfloat16).reshape(tokens.shape)
    regathered = (
        lax.all_gather(ln1_gain, "fsdp", axis=0, tiled=True),
        lax.all_gather(ln1_bias, "fsdp", axis=0, tiled=True),
        lax.all_gather(ln2_gain, "fsdp", axis=0, tiled=True),
        lax.all_gather(ln2_bias, "fsdp", axis=0, tiled=True),
        lax.all_gather(qkv_weight, "fsdp", axis=0, tiled=True),
        lax.all_gather(qkv_bias, "fsdp", axis=0, tiled=True),
        lax.all_gather(dense_weight, "fsdp", axis=0, tiled=True),
        lax.all_gather(dense_bias, "fsdp", axis=0, tiled=True),
        lax.all_gather(fc_in_weight, "fsdp", axis=0, tiled=True),
        lax.all_gather(fc_in_bias, "fsdp", axis=0, tiled=True),
        lax.all_gather(fc_out_weight, "fsdp", axis=0, tiled=True),
        lax.all_gather(fc_out_bias, "fsdp", axis=0, tiled=True),
    )
    keys_back, values_back = (
        lax.all_gather(key_low, "ctx", axis=0, tiled=True),
        lax.all_gather(value_low, "ctx", axis=0, tiled=True),
    )
    grad_out = cotangent.reshape(row_count, model_width)
    grad_wide = grad_out.astype(jnp.float32)
    d_active = dot_right(grad_out, regathered[10])
    d_hidden_low = jax.vjp(gelu_exact, hidden)[1](d_active)[0].astype(jnp.bfloat16)
    d_second = dot_right(d_hidden_low, regathered[8])
    d_mixed_low = (
        dot_right(grad_out, regathered[6]).astype(jnp.bfloat16).reshape(row_count, HEADS, head_dim)
    )
    probs_again = jnp.exp(score_block(keys_back) - log_total)
    probs_again_low = probs_again.astype(jnp.bfloat16)
    grad_probs = jnp.einsum(
        "qhd,khd->hqk",
        d_mixed_low,
        values_back.reshape(seq_length, HEADS, head_dim),
        preferred_element_type=jnp.float32,
    )
    row_delta = jnp.sum(probs_again * grad_probs, axis=-1, keepdims=True)
    grad_scores = (probs_again * (grad_probs - row_delta) * score_scale).astype(jnp.bfloat16)
    d_query = jnp.einsum(
        "hqk,khd->qhd",
        grad_scores,
        keys_back.reshape(seq_length, HEADS, head_dim),
        preferred_element_type=jnp.float32,
    )
    d_key = jnp.einsum(
        "hqk,qhd->khd", grad_scores, query_low, preferred_element_type=jnp.float32
    ).reshape(row_count * lax.axis_size("ctx"), model_width)
    d_value = jnp.einsum(
        "hqk,qhd->khd", probs_again_low, d_mixed_low, preferred_element_type=jnp.float32
    ).reshape(row_count * lax.axis_size("ctx"), model_width)
    kv_grad = lax.psum_scatter(
        jnp.concatenate([d_key, d_value], axis=1).astype(jnp.bfloat16),
        "ctx",
        scatter_dimension=0,
        tiled=True,
    ).astype(jnp.float32)
    d_key_own = kv_grad[:, :model_width].reshape(row_count, HEADS, head_dim)
    d_packed = jnp.concatenate(
        [
            rotate(d_query, cosine, -sine_table).reshape(row_count, model_width),
            rotate(d_key_own, cosine, -sine_table).reshape(row_count, model_width),
            kv_grad[:, model_width:],
        ],
        axis=1,
    )
    d_packed_low = d_packed.astype(jnp.bfloat16)
    d_first = dot_right(d_packed_low, regathered[4])
    norm_back_one = jax.vjp(layer_norm, values, gain_one, shift_one)[1]
    d_values_one, d_gain_one, d_shift_one = norm_back_one(d_first)
    norm_back_two = jax.vjp(layer_norm, values, gain_two, shift_two)[1]
    d_values_two, d_gain_two, d_shift_two = norm_back_two(d_second)
    input_grad = (grad_wide + d_values_one + d_values_two).reshape(tokens.shape)
    grad_sum = jnp.sum(grad_wide, axis=0)
    mlp_grads = reduce_grads(
        dot_left(normed_two, d_hidden_low),
        jnp.sum(d_hidden_low.astype(jnp.float32), axis=0),
        dot_left(active_low, grad_out),
        grad_sum,
        d_gain_two,
        d_shift_two,
    )
    attn_grads = reduce_grads(
        dot_left(normed_one, d_packed_low),
        jnp.sum(d_packed_low.astype(jnp.float32), axis=0),
        dot_left(mixed_low, grad_out),
        grad_sum,
        d_gain_one,
        d_shift_one,
    )
    return (
        output,
        input_grad,
        attn_grads[4],
        attn_grads[5],
        mlp_grads[4],
        mlp_grads[5],
        attn_grads[0],
        attn_grads[1],
        attn_grads[2],
        attn_grads[3],
        mlp_grads[0],
        mlp_grads[1],
        mlp_grads[2],
        mlp_grads[3],
    )


def solution(mesh):
    placed = (
        P("fsdp", "ctx", None),
        P("fsdp", "ctx"),
        P("fsdp", "ctx"),
        P("fsdp"),
        P("fsdp"),
        P("fsdp"),
        P("fsdp"),
        P("fsdp", None),
        P("fsdp"),
        P("fsdp", None),
        P("fsdp"),
        P("fsdp", None),
        P("fsdp"),
        P("fsdp", None),
        P("fsdp"),
        P("fsdp", "ctx", None),
    )
    return jax.shard_map(
        local,
        mesh=mesh,
        in_specs=placed,
        out_specs=(
            P("fsdp", "ctx", None),
            P("fsdp", "ctx", None),
            P("fsdp"),
            P("fsdp"),
            P("fsdp"),
            P("fsdp"),
            P("fsdp", None),
            P("fsdp"),
            P("fsdp", None),
            P("fsdp"),
            P("fsdp", None),
            P("fsdp"),
            P("fsdp", None),
            P("fsdp"),
        ),
        check_vma=False,
    )
```

profile of v0, /device:TPU:0, one launch (start us, length us, event | category | flops | bytes accessed | tf_op | source)
XLA Modules:
  0.0 2394.3 jit_solution(9701126549895756625)
XLA Ops:
  11.4 13.4 all-gather.1
  24.8 8.9 all-gather
  33.7 28.6 %all-gather.2 = bf16[8,1,768]{2,1,0:T(2,128)(2,1)S(1)} all-gather(bf16[1,1,768]{2,1,0:T(2,128)(2,1)S(1)} %reshape.294), channel_id=1, replica_groups=mesh['ctx'=4,'fsdp'=8] {'fsdp'}, dimensions={0}, use_global_device_ids=true | all-gather | bytes 13824 | tf_op jit(solution)/shard_map/all_gather | solution.py:119
  66.9 165.6 %all-gather.14.cloned.1.call-done = bf16[2048,6144]{1,0:T(8,128)(2,1)} async-done(((bf16[256,6144]{1,0:T(8,128)(2,1)}), bf16[2048,6144]{1,0:T(8,128)(2,1)}) %all-gather.14.cloned.1.call-update) | async-done | bytes 25165840 | tf_op jit(solution)/shard_map/all_gather | solution.py:118
  232.5 12.8 convolution_add_fusion.1
  262.2 8.2 all_gather.58
  271.5 42.9 %all-gather.20.cloned.1.call-done = bf16[2048,2048]{1,0:T(8,128)(2,1)} async-done(((bf16[256,2048]{1,0:T(8,128)(2,1)}), bf16[2048,2048]{1,0:T(8,128)(2,1)}) %all-gather.20.cloned.1.call-update) | async-done | bytes 8388624 | tf_op jit(solution)/shard_map/all_gather | solution.py:120
  314.3 6.7 convolution_convert_fusion.4
  324.7 43.2 %all-gather.18.cloned.1.call-done = bf16[1024,2048]{0,1:T(8,128)(2,1)} async-done(((bf16[256,2048]{0,1:T(8,128)(2,1)}), bf16[1024,2048]{0,1:T(8,128)(2,1)}) %all-gather.18.cloned.1.call-update) | async-done | bytes 4194320 | tf_op jit(solution)/shard_map/all_gather | solution.py:145
  367.9 5.0 fusion.9
  379.1 43.7 %all-gather.16.cloned.1.call-done = bf16[1024,2048]{0,1:T(8,128)(2,1)} async-done(((bf16[256,2048]{0,1:T(8,128)(2,1)}), bf16[1024,2048]{0,1:T(8,128)(2,1)}) %all-gather.16.cloned.1.call-update) | async-done | bytes 4194320 | tf_op jit(solution)/shard_map/all_gather | solution.py:146
  422.8 7.0 fusion.126
  429.8 4.3 fusion.42
  434.1 26.6 %fusion.45 = bf16[8,256,1024]{2,1,0:T(8,128)(2,1)} fusion(f32[8,256,1024]{2,1,0:T(8,128)} %fusion.126, f32[8,256,1024]{2,1,0:T(8,128)} %copy-done.7, f32[8,256]{1,0:T(8,128)} %log_add_fusion, pred[256,1024]{1,0:T(8,128)(4,1)S(1)} %fusion.91, bf16[256,8,192]{2,0,1:T(8,128)(2,1)S(1)} %copy-done.17, bf16[256,8,64]{2,0,1:T(8,128)(2,1)} %get-tuple-element.58), kind=kOutput, calls=%fused_computation.55 | convolution fusion | flops 1101007872 | bytes 22290432 | tf_op jit(solution)/shard_map/hqk,qhd->khd/dot_general | solution.py:224
  460.7 7.7 pad_maximum_fusion
  469.8 17.2 fusion.75
  488.0 5.6 convolution_convert_fusion.3
  493.7 23.0 fusion.72
  520.0 34.9 %reduce-scatter.6.cloned.1.call-done = bf16[256,4096]{0,1:T(8,128)(2,1)} async-done(((bf16[1024,4096]{0,1:T(8,128)(2,1)}), bf16[256,4096]{0,1:T(8,128)(2,1)}) %reduce-scatter.6.cloned.1.call-update) | async-done | bytes 2097168 | tf_op jit(solution)/shard_map/reduce_scatter | solution.py:230
  561.8 3.7 fusion.79
  572.6 12.7 convolution_convert_fusion.2
  586.0 12.0 all-gather.5
  598.1 21.5 all-gather.4
  619.6 21.6 all_gather.66
  641.3 204.1 %all-gather.22.cloned.1.call-done = bf16[2048,8192]{1,0:T(8,128)(2,1)} async-done(((bf16[256,8192]{1,0:T(8,128)(2,1)}), bf16[2048,8192]{1,0:T(8,128)(2,1)}) %all-gather.22.cloned.1.call-update) | async-done | bytes 33554448 | tf_op jit(solution)/shard_map/all_gather | solution.py:122
  845.4 32.4 %multiply_convert_fusion.1 = (bf16[256,8192]{1,0:T(8,128)(2,1)}, f32[256,8192]{1,0:T(8,128)}) fusion(f32[8192]{0:T(1024)S(1)} %convert_element_type.201, bf16[2048,8192]{1,0:T(8,128)(2,1)} %all-gather.22.cloned.1.call-done, bf16[1,256,2048]{2,1,0:T(8,128)(2,1)S(1)} %copy-done, f32[2048]{0:T(1024)S(1)} %bitcast.178, f32[2048]{0:T(1024)S(1)} %bitcast.173, ...), kind=kOutput, calls=%fused_computation.13 | convolution fusion | flops 8731492352 | bytes 47237120 | tf_op jit(solution)/shard_map/dot_general | solution.py:174
  877.8 256.1 %all-gather.24.cloned.1.call-done = bf16[8192,2048]{1,0:T(8,128)(2,1)} async-done(((bf16[1024,2048]{1,0:T(8,128)(2,1)}), bf16[8192,2048]{1,0:T(8,128)(2,1)}) %all-gather.24.cloned.1.call-update) | async-done | bytes 33554448 | tf_op jit(solution)/shard_map/all_gather | solution.py:124
  1133.9 33.3 %fusion.125 = (bf16[8192]{0:T(1024)(128)(2,1)S(1)}, bf16[256,8192]{1,0:T(8,128)(2,1)}) fusion(f32[256,8192]{1,0:T(8,128)} %get-tuple-element.66, bf16[8192,2048]{1,0:T(8,128)(2,1)} %all-gather.24.cloned.1.call-done, bf16[1,256,2048]{2,1,0:T(8,128)(2,1)S(1)} %copy-done.2), kind=kOutput, calls=%fused_computation.162 | convolution fusion | flops 8743018496 | bytes 47202304 | tf_op jit(solution)/shard_map/dot_general | solution.py:39
  1167.2 16.5 convolution_convert_fusion.1
  1183.8 16.2 convolution_convert_fusion
  1200.3 23.8 reduce-scatter.10.cloned.1.call-done
  1224.2 248.0 %reduce-scatter.8.cloned.1.call-done = bf16[256,6144]{1,0:T(8,128)(2,1)} async-done(((bf16[2048,6144]{1,0:T(8,128)(2,1)}), bf16[256,6144]{1,0:T(8,128)(2,1)}) %reduce-scatter.8.cloned.1.call-update) | async-done | bytes 3145744 | tf_op jit(solution)/shard_map/reduce_scatter | solution.py:52
  1472.2 326.3 %reduce-scatter.12.cloned.1.call-done = bf16[256,8192]{1,0:T(8,128)(2,1)} async-done(((bf16[2048,8192]{1,0:T(8,128)(2,1)}), bf16[256,8192]{1,0:T(8,128)(2,1)}) %reduce-scatter.12.cloned.1.call-update) | async-done | bytes 4194320 | tf_op jit(solution)/shard_map/reduce_scatter | solution.py:52
  1798.5 326.3 %reduce-scatter.14.cloned.1.call-done = bf16[1024,2048]{1,0:T(8,128)(2,1)} async-done(((bf16[8192,2048]{1,0:T(8,128)(2,1)}), bf16[1024,2048]{1,0:T(8,128)(2,1)}) %reduce-scatter.14.cloned.1.call-update) | async-done | bytes 4194320 | tf_op jit(solution)/shard_map/reduce_scatter | solution.py:58
  2127.6 9.2 all-gather.6
  2136.8 9.6 all-gather.3
  2146.4 7.1 fusion.48
  2153.5 17.6 fusion.127
  2171.1 19.0 fusion.62
  2190.1 13.9 fusion.122
  2206.2 3.8 fusion.68
  2210.0 27.8 %all-reduce.7 = (bf16[2048]{0:T(1024)(128)(2,1)S(1)}, bf16[2048]{0:T(1024)(128)(2,1)S(1)}, bf16[2048]{0:T(1024)(128)(2,1)S(1)}, bf16[2048]{0:T(1024)(128)(2,1)S(...) all-reduce(bf16[2048]{0:T(1024)(128)(2,1)S(1)} %get-tuple-element.2, ...), channel_id=3, replica_groups=mesh['ctx'=4,'fsdp'=8] {'fsdp'}, use_global_device_ids=true, to_apply=%region_11.12.clone | all-reduce | flops 24576 | bytes 98304
  2238.3 9.8 all-reduce.8
  2251.6 4.9 add_bitcast_fusion
  2256.5 113.1 %all-reduce.12.cloned.1.call-done = (bf16[256,6144]{1,0:T(8,128)(2,1)}, bf16[256,2048]{1,0:T(8,128)(2,1)}, bf16[256,8192]{1,0:T(8,128)(2,1)}, bf16[1024,2048]{1,0:T(8,128)(2,1)}) async-done(((bf16[256,6144]{1,0:T(8,128)(2,1)}, bf16[256,2048]{1,0:T(8,128)(2,1)}, bf16[256,8192]{1,0:T(8,128)(2,1)}, bf16[1024,2048]{1,0:T(8,128)(2,1)}), (bf16[256,6144]{1,0:T(8,128)(2,1)}, bf16[256,2048]{1,0:T(8,128)(2,1)}, ...) | async-done | bytes 12582928 | tf_op jit(solution)/shard_map/psum | solution.py:72
  2372.5 5.3 convert_element_type.219
  2377.8 4.4 convert_element_type.225
  2382.2 4.4 convert_element_type.228
  (179 shorter events, 67.3 us)
Async XLA Ops:
  7.2 225.3 %all-gather.14.cloned.1.call-start = ((), (), s32[]{:S(2)}) async-start(), calls=%async_computation.5 | async-start | bytes 28311552 | tf_op jit(solution)/shard_map/all_gather | solution.py:118
  7.9 306.4 %all-gather.20.cloned.1.call-start = ((), (), s32[]{:S(2)}) async-start(), calls=%async_computation.8 | async-start | bytes 9437184 | tf_op jit(solution)/shard_map/all_gather | solution.py:120
  8.7 359.2 %all-gather.18.cloned.1.call-start = ((), (), s32[]{:S(2)}) async-start(), calls=%async_computation.7 | async-start | bytes 5242880 | tf_op jit(solution)/shard_map/all_gather | solution.py:145
  33.7 537.9 %copy-start.18 = (f32[8,1,256]{2,1,0:T(1,128)}, f32[8,1,256]{2,1,0:T(1,128)S(1)}, u32[]{:S(2)}) copy-start(f32[8,1,256]{2,1,0:T(1,128)S(1)} %convert_element_type.229) | copy-start | bytes 24580
  65.2 180.1 %copy-start.21 = (f32[256]{0:T(256)}, f32[256]{0:T(256)S(1)}, u32[]{:S(2)}) copy-start(f32[256]{0:T(256)S(1)} %broadcast_multiply_fusion.1) | copy-start | bytes 3076
  66.8 178.5 %copy-start.29 = (f32[256]{0:T(256)}, f32[256]{0:T(256)S(1)}, u32[]{:S(2)}) copy-start(f32[256]{0:T(256)S(1)} %fusion.69) | copy-start | bytes 3076
  66.9 178.5 %copy-start.23 = (f32[256]{0:T(256)}, f32[256]{0:T(256)S(1)}, u32[]{:S(2)}) copy-start(f32[256]{0:T(256)S(1)} %fusion.95) | copy-start | bytes 3076
  247.9 2.7 copy-start.1
  251.8 10.4 copy-start.32
  251.8 62.6 %copy-start.2 = (bf16[1,256,2048]{2,1,0:T(8,128)(2,1)S(1)}, bf16[1,256,2048]{2,1,0:T(8,128)(2,1)}, u32[]{:S(2)}) copy-start(bf16[1,256,2048]{2,1,0:T(8,128)(2,1)} %param.31) | copy-start | bytes 3145732
  257.0 165.8 %all-gather.16.cloned.1.call-start = ((), (), s32[]{:S(2)}) async-start(), calls=%async_computation.6 | async-start | bytes 5242880 | tf_op jit(solution)/shard_map/all_gather | solution.py:146
  262.2 292.8 %reduce-scatter.6.cloned.1.call-start = ((), (), s32[]{:S(2)}) async-start(), calls=%async_computation.11 | async-start | bytes 10485760 | tf_op jit(solution)/shard_map/reduce_scatter | solution.py:230
  367.9 54.9 %copy-start.10 = (bf16[256,2048]{0,1:T(8,128)(2,1)S(1)}, bf16[256,2048]{0,1:T(8,128)(2,1)}, u32[]{:S(2)}) copy-start(bf16[256,2048]{0,1:T(8,128)(2,1)} %copy.72) | copy-start | bytes 3145732
  372.9 3.4 copy-start.7
  372.9 49.9 %copy-start.25 = (f32[8,256]{1,0:T(8,128)}, f32[8,256]{1,0:T(8,128)S(1)}, u32[]{:S(2)}) copy-start(f32[8,256]{1,0:T(8,128)S(1)} %get-tuple-element.63) | copy-start | bytes 24580
  378.5 44.3 %copy-start.27 = (f32[8,256]{1,0:T(8,128)}, f32[8,256]{1,0:T(8,128)S(1)}, u32[]{:S(2)}) copy-start(f32[8,256]{1,0:T(8,128)S(1)} %fusion.8) | copy-start | bytes 24580
  422.7 7.1 copy-start.8
  422.7 7.1 copy-start.31
  429.8 4.3 copy-start.17
  468.4 1.4 copy-start.26
  468.4 1.4 copy-start.28
  468.4 377.0 %all-gather.22.cloned.1.call-start = ((), (), s32[]{:S(2)}) async-start(), calls=%async_computation.9 | async-start | bytes 37748736 | tf_op jit(solution)/shard_map/all_gather | solution.py:122
  469.0 664.9 %all-gather.24.cloned.1.call-start = ((), (), s32[]{:S(2)}) async-start(), calls=%async_computation.10 | async-start | bytes 37748736 | tf_op jit(solution)/shard_map/all_gather | solution.py:124
  469.7 754.4 %reduce-scatter.10.cloned.1.call-start = ((), (), s32[]{:S(2)}) async-start(), calls=%async_computation.13 | async-start | bytes 9437184 | tf_op jit(solution)/shard_map/reduce_scatter | solution.py:58
  493.6 978.6 %reduce-scatter.8.cloned.1.call-start = ((), (), s32[]{:S(2)}) async-start(), calls=%async_computation.12 | async-start | bytes 28311552 | tf_op jit(solution)/shard_map/reduce_scatter | solution.py:52
  516.7 41.0 %copy-start.9 = (f32[256,8,256]{2,0,1:T(8,128)}, f32[256,8,256]{2,0,1:T(8,128)S(1)}, u32[]{:S(2)}) copy-start(f32[256,8,256]{2,0,1:T(8,128)S(1)} %fusion.72) | copy-start | bytes 6291460
  520.0 41.8 %copy-start.20 = (f32[256,64]{1,0:T(8,128)S(1)}, f32[256,64]{1,0:T(8,128)}, u32[]{:S(2)}) copy-start(f32[256,64]{1,0:T(8,128)} %get-tuple-element.60) | copy-start | bytes 196612
  559.6 5.9 copy-start.16
  561.4 11.2 copy-start
  561.4 11.1 copy-start.22
  561.5 11.1 copy-start.24
  568.6 16.7 copy-start.3
  571.6 1.0 copy-start.5
  585.3 34.3 %copy-start.33 = (bf16[1024]{0:T(1024)(128)(2,1)S(1)}, bf16[1024]{0:T(1024)(128)(2,1)}, u32[]{:S(2)}) copy-start(bf16[1024]{0:T(1024)(128)(2,1)} %param.28) | copy-start | bytes 6148
  585.4 1213.1 %reduce-scatter.12.cloned.1.call-start = ((), (), s32[]{:S(2)}) async-start(), calls=%async_computation.14 | async-start | bytes 37748736 | tf_op jit(solution)/shard_map/reduce_scatter | solution.py:52
  1183.8 941.0 %reduce-scatter.14.cloned.1.call-start = ((), (), s32[]{:S(2)}) async-start(), calls=%async_computation.15 | async-start | bytes 37748736 | tf_op jit(solution)/shard_map/reduce_scatter | solution.py:58
  1200.1 924.7 %copy-start.39 = (u32[32]{0:T(128)S(1)}, u32[32]{0:T(128)}, u32[]{:S(2)}) copy-start(u32[32]{0:T(128)} %constant.104) | copy-start | bytes 388
  1200.1 927.3 %copy-start.37 = (bf16[256]{0:T(256)(128)(2,1)S(1)}, bf16[256]{0:T(256)(128)(2,1)}, u32[]{:S(2)}) copy-start(bf16[256]{0:T(256)(128)(2,1)} %param.26) | copy-start | bytes 1540
  1200.1 927.3 %copy-start.38 = (bf16[256]{0:T(256)(128)(2,1)S(1)}, bf16[256]{0:T(256)(128)(2,1)}, u32[]{:S(2)}) copy-start(bf16[256]{0:T(256)(128)(2,1)} %param.30) | copy-start | bytes 1540
  1200.1 946.3 %copy-start.12 = (bf16[8,256,256]{2,1,0:T(8,128)(2,1)S(1)}, bf16[8,256,256]{2,1,0:T(8,128)(2,1)}, u32[]{:S(2)}) copy-start(bf16[8,256,256]{2,1,0:T(8,128)(2,1)} %copy-done.11) | copy-start | bytes 3145732
  1200.1 1169.4 %all-reduce.12.cloned.1.call-start = ((), (), s32[]{:S(2)}) async-start(), calls=%async_computation.16 | async-start | bytes 25165824 | tf_op jit(solution)/shard_map/psum | solution.py:72
  2171.1 19.0 copy-start.4
  2171.1 19.0 copy-start.6
  2171.1 19.0 copy-start.19
  2190.1 14.0 copy-start.30
  2248.7 138.0 %copy-start.34 = (f32[256]{0:T(256)}, f32[256]{0:T(256)S(1)}, u32[]{:S(2)}) copy-start(f32[256]{0:T(256)S(1)} %convert_element_type.223) | copy-start | bytes 3076
  2369.5 8.3 copy-start.15
  2377.8 4.4 copy-start.14
  (4 other events, 3.3 us)
Sparse Core Ops, SparseCore 0:
  9.7 222.7 all-gather.13
  234.1 80.2 all-gather.19
  316.7 51.0 all-gather.17
  370.1 52.5 all-gather.15
  468.5 86.3 reduce-scatter.5
  556.5 288.8 all-gather.21
  847.1 286.8 all-gather.23
  1136.3 87.7 reduce-scatter.9
  1226.7 245.5 reduce-scatter.7
  1474.5 323.8 reduce-scatter.11
  1800.9 323.8 reduce-scatter.13
  2129.0 240.4 all-reduce.11
where the time goes:
time: 2400 us; the launch traced here: 2390 us
  waiting for transfers between devices  1830 us (76%)
  matrix products  277 us (12%)
  blocking collectives  171 us (7%)
  other arithmetic  60.6 us (3%)
  local copies, waits for them, and re-layouts  37.6 us (2%)
    reduce_scatter x2, waiting for transfers between devices, reduce_grads(): lax.psum_scatter(weight_one.astype(jnp.bfloat16), 'fsdp', scatter_dimensi...  574 us
    reduce_scatter x2, waiting for transfers between devices, reduce_grads(): lax.psum_scatter(weight_two.astype(jnp.bfloat16), 'fsdp', scatter_dimensi...  350 us
    all_gather x1, waiting for transfers between devices, local(): lax.all_gather(fc_out_weight, 'fsdp', axis=0, tiled=True)  256 us
    all_gather x1, waiting for transfers between devices, local(): lax.all_gather(fc_in_weight, 'fsdp', axis=0, tiled=True)  204 us
    all_gather x1, waiting for transfers between devices, local(): lax.all_gather(qkv_weight, 'fsdp', axis=0, tiled=True)  166 us
    psum x1, waiting for transfers between devices, reduce_grads(): lax.psum(shared[0].astype(jnp.bfloat16), 'ctx').astype(jnp.float32)  113 us
    dot_general x4, matrix products, dot_right(): lax.dot_general(left_side, right_side, (((1,), (1,)), ((), ())), preferre...  71.5 us
    dot_general x4, matrix products, dot_left(): lax.dot_general(left_side, right_side, (((0,), (0,)), ((), ())), preferre...  51.1 us
  transfers between devices with their start and end apart: 12, of which 12 were waited for; matrix products, arithmetic and copies ran while one was open for 13% of the time, Pallas kernels for 0%

commit v1 on v0

--- a/solution.py
+++ b/solution.py
@@ -284,6 +284,229 @@
     )
 
 
+def gather_vectors(vectors):
+    sizes = [v.shape[0] for v in vectors]
+    everything = lax.all_gather(jnp.concatenate(vectors), "fsdp", axis=0, tiled=False)
+    whole, start = [], 0
+    for size in sizes:
+        whole.append(everything[:, start : start + size].reshape(-1).astype(jnp.float32))
+        start += size
+    return whole
+
+
+def local_by_head(
+    tokens,
+    segments,
+    positions,
+    ln1_gain,
+    ln1_bias,
+    ln2_gain,
+    ln2_bias,
+    qkv_weight,
+    qkv_bias,
+    dense_weight,
+    dense_bias,
+    fc_in_weight,
+    fc_in_bias,
+    fc_out_weight,
+    fc_out_bias,
+    cotangent,
+):
+    width = tokens.shape[-1]
+    block = tokens.shape[1]
+    nf = lax.axis_size("fsdp")
+    nc = lax.axis_size("ctx")
+    me_c = lax.axis_index("ctx")
+    me_f = lax.axis_index("fsdp")
+    hd = width // HEADS
+    units = fc_in_weight.shape[1] // nf
+    group = nf * block
+    length = nc * block
+    mine = nf // nc
+    rows = width // nf
+    part = rows // nc
+    scale = hd ** (-0.5)
+    x_own = tokens.reshape(block, width)
+    g_own = cotangent.reshape(block, width)
+
+    gain_one, shift_one, gain_two, shift_two, qkv_b, dense_b, fc_out_b = gather_vectors(
+        [ln1_gain, ln1_bias, ln2_gain, ln2_bias, qkv_bias, dense_bias, fc_out_bias]
+    )
+    ints = lax.all_gather(
+        jnp.concatenate([segments, positions], axis=0), "fsdp", axis=0, tiled=False
+    )
+    position_all = ints[:, 1].reshape(group)
+    segment_all = lax.all_gather(ints[:, 0], "ctx", axis=1, tiled=True)
+    segment_mine = lax.dynamic_slice_in_dim(segment_all, me_c * mine, mine, 0)
+
+    joined = jnp.concatenate(
+        [
+            lax.dynamic_slice_in_dim(qkv_weight, me_c * part, part, 0)
+            .reshape(part, 3, nf, hd)
+            .transpose(2, 0, 1, 3)
+            .reshape(nf, part, 3 * hd),
+            lax.dynamic_slice_in_dim(fc_in_weight, me_c * part, part, 0)
+            .reshape(part, nf, units)
+            .transpose(1, 0, 2),
+        ],
+        axis=2,
+    )
+    quarter = lax.all_to_all(joined, "fsdp", 0, 0, tiled=True)
+    columns = lax.all_gather(quarter, "ctx", axis=1, tiled=True).reshape(width, 3 * hd + units)
+    w_qkv = columns[:, : 3 * hd]
+    w_in = columns[:, 3 * hd :]
+
+    x_all = lax.all_gather(x_own, "fsdp", axis=0, tiled=True)
+    g_all = lax.all_gather(g_own, "fsdp", axis=0, tiled=True)
+    values = x_all.astype(jnp.float32)
+    row_mean = jnp.mean(values, axis=-1, keepdims=True)
+    centred = values - row_mean
+    spread = jnp.mean(centred * centred, axis=-1, keepdims=True)
+    normal = centred * lax.rsqrt(spread + eps_norm)
+    first = (normal * gain_one + shift_one).astype(jnp.bfloat16)
+    second = (normal * gain_two + shift_two).astype(jnp.bfloat16)
+
+    head_bias = lax.dynamic_index_in_dim(qkv_b.reshape(3, nf, hd), me_f, 1, keepdims=False)
+    packed = jnp.dot(first, w_qkv, preferred_element_type=jnp.float32) + head_bias.reshape(-1)
+    cosine, sine_table = rotary_tables(position_all, hd // 4)
+    shaped = packed.reshape(group, 3, hd)
+    turned = rotate(shaped[:, :2], cosine, sine_table)
+    mixed = jnp.concatenate([turned, shaped[:, 2:]], axis=1).astype(jnp.bfloat16)
+    mixed = mixed.reshape(nf, block, 3 * hd)
+    mixed = lax.all_to_all(mixed, "ctx", 0, 1, tiled=True)
+    q, k, v = (mixed[..., i * hd : (i + 1) * hd] for i in range(3))
+
+    index = jnp.arange(length, dtype=jnp.int32)
+    allowed = (segment_mine[:, :, None] == segment_mine[:, None, :]) & (
+        index[None, None, :] <= index[None, :, None]
+    )
+    scores = jnp.einsum("sqd,skd->sqk", q, k, preferred_element_type=jnp.float32) * scale
+    scores = jnp.where(allowed, scores, -1e30)
+    row_max = jnp.max(scores, axis=-1, keepdims=True)
+    probs = jnp.exp(scores - row_max)
+    probs = probs / jnp.sum(probs, axis=-1, keepdims=True)
+    probs_low = probs.astype(jnp.bfloat16)
+    o = jnp.einsum("sqk,skd->sqd", probs_low, v, preferred_element_type=jnp.float32).astype(
+        jnp.bfloat16
+    )
+    o_back = lax.all_to_all(o, "ctx", 1, 0, tiled=True).reshape(group, hd)
+
+    hidden = jnp.dot(second, w_in, preferred_element_type=jnp.float32) + fc_in_bias.astype(
+        jnp.float32
+    )
+    active = gelu_exact(hidden).astype(jnp.bfloat16)
+    partial = jnp.dot(o_back, dense_weight, preferred_element_type=jnp.float32) + jnp.dot(
+        active, fc_out_weight, preferred_element_type=jnp.float32
+    )
+    summed = lax.psum_scatter(
+        partial.astype(jnp.bfloat16), "fsdp", scatter_dimension=0, tiled=True
+    ).astype(jnp.float32)
+    x_wide = x_own.astype(jnp.float32)
+    output = (x_wide + summed + dense_b + fc_out_b).astype(jnp.bfloat16).reshape(tokens.shape)
+
+    d_o = dot_right(g_all, dense_weight).astype(jnp.bfloat16).reshape(nf, block, hd)
+    d_o = lax.all_to_all(d_o, "ctx", 0, 1, tiled=True)
+    d_active = dot_right(g_all, fc_out_weight)
+    d_hidden = jax.vjp(gelu_exact, hidden)[1](d_active)[0].astype(jnp.bfloat16)
+    grad_fc_out = dot_left(active, g_all).astype(jnp.bfloat16)
+    grad_fc_in = dot_left(second, d_hidden).astype(jnp.bfloat16)
+    grad_dense = dot_left(o_back, g_all).astype(jnp.bfloat16)
+
+    d_probs = jnp.einsum("sqd,skd->sqk", d_o, v, preferred_element_type=jnp.float32)
+    delta = jnp.sum(probs * d_probs, axis=-1, keepdims=True)
+    d_scores = (probs * (d_probs - delta) * scale).astype(jnp.bfloat16)
+    d_q = jnp.einsum("sqk,skd->sqd", d_scores, k, preferred_element_type=jnp.float32)
+    d_k = jnp.einsum("sqk,sqd->skd", d_scores, q, preferred_element_type=jnp.float32)
+    d_v = jnp.einsum("sqk,sqd->skd", probs_low, d_o, preferred_element_type=jnp.float32)
+    d_mixed = jnp.concatenate([d_q, d_k, d_v], axis=-1).astype(jnp.bfloat16)
+    d_mixed = lax.all_to_all(d_mixed, "ctx", 1, 0, tiled=True).reshape(group, 3, hd)
+    d_mixed = d_mixed.astype(jnp.float32)
+    d_packed = jnp.concatenate(
+        [rotate(d_mixed[:, :2], cosine, -sine_table), d_mixed[:, 2:]], axis=1
+    ).reshape(group, 3 * hd)
+    d_packed = d_packed.astype(jnp.bfloat16)
+    grad_qkv = dot_left(first, d_packed).astype(jnp.bfloat16)
+
+    d_first = dot_right(d_packed, w_qkv)
+    d_second = dot_right(d_hidden, w_in)
+    d_normal = lax.psum_scatter(
+        (d_first * gain_one + d_second * gain_two).astype(jnp.bfloat16),
+        "fsdp",
+        scatter_dimension=0,
+        tiled=True,
+    ).astype(jnp.float32)
+    own_mean = jnp.mean(x_wide, axis=-1, keepdims=True)
+    own_centred = x_wide - own_mean
+    own_rstd = lax.rsqrt(jnp.mean(own_centred * own_centred, axis=-1, keepdims=True) + eps_norm)
+    own_normal = own_centred * own_rstd
+    d_x = own_rstd * (
+        d_normal
+        - jnp.mean(d_normal, axis=-1, keepdims=True)
+        - own_normal * jnp.mean(d_normal * own_normal, axis=-1, keepdims=True)
+    )
+    input_grad = (g_own.astype(jnp.float32) + d_x).reshape(tokens.shape)
+
+    def spread_out(values, parts):
+        whole = jnp.zeros((parts, nf, values.shape[0] // parts), jnp.float32)
+        return lax.dynamic_update_slice_in_dim(
+            whole, values.reshape(parts, 1, -1), me_f, 1
+        ).reshape(nf, -1)
+
+    small = jnp.concatenate(
+        [
+            jnp.sum(d_first * normal, axis=0).reshape(nf, -1),
+            jnp.sum(d_first, axis=0).reshape(nf, -1),
+            jnp.sum(d_second * normal, axis=0).reshape(nf, -1),
+            jnp.sum(d_second, axis=0).reshape(nf, -1),
+            spread_out(jnp.sum(d_packed.astype(jnp.float32), axis=0), 3),
+            spread_out(jnp.sum(d_hidden.astype(jnp.float32), axis=0), 1),
+        ],
+        axis=1,
+    )
+    small = lax.psum_scatter(small, "fsdp", scatter_dimension=0, tiled=True)
+    g_sum = lax.dynamic_slice_in_dim(jnp.sum(g_all.astype(jnp.float32), axis=0), me_f * rows, rows)
+    small = lax.psum(jnp.concatenate([small.reshape(-1), g_sum]), "ctx")
+    qkv_cols = 3 * width // nf
+    cuts, start = [], 0
+    for size in (rows, rows, rows, rows, qkv_cols, units, rows):
+        cuts.append(small[start : start + size])
+        start += size
+
+    def by_rows(grad):
+        cols = grad.shape[1]
+        mine_rows = lax.psum_scatter(
+            grad.reshape(nf, nc, part, cols), "ctx", scatter_dimension=1, tiled=True
+        ).reshape(nf, part, cols)
+        mine_rows = lax.all_to_all(mine_rows, "fsdp", 0, 0, tiled=True)
+        return lax.all_gather(mine_rows, "ctx", axis=1, tiled=True).astype(jnp.float32)
+
+    grad_fc_in = by_rows(grad_fc_in).transpose(1, 0, 2).reshape(fc_in_weight.shape)
+    grad_qkv = (
+        by_rows(grad_qkv)
+        .reshape(nf, rows, 3, hd)
+        .transpose(1, 2, 0, 3)
+        .reshape(qkv_weight.shape)
+    )
+    grad_fc_out = lax.psum(grad_fc_out, "ctx").astype(jnp.float32)
+    grad_dense = lax.psum(grad_dense, "ctx").astype(jnp.float32)
+    return (
+        output,
+        input_grad,
+        cuts[0],
+        cuts[1],
+        cuts[2],
+        cuts[3],
+        grad_qkv,
+        cuts[4],
+        grad_dense,
+        cuts[6],
+        grad_fc_in,
+        cuts[5],
+        grad_fc_out,
+        cuts[6],
+    )
+
+
 def solution(mesh):
     placed = (
         P("fsdp", "ctx", None),
@@ -303,8 +526,9 @@
         P("fsdp"),
         P("fsdp", "ctx", None),
     )
+    by_head = mesh.shape["fsdp"] == HEADS and HEADS % mesh.shape["ctx"] == 0
     return jax.shard_map(
-        local,
+        local_by_head if by_head else local,
         mesh=mesh,
         in_specs=placed,
         out_specs=(

time: 2400 us -> 1130 us (0.47)
  waiting for transfers between devices: 1830 us -> 548 us
  local copies, waits for them, and re-layouts: 37.6 us -> 109 us
  matrix products: 277 us -> 226 us
  blocking collectives: 171 us -> 133 us
    reduce_scatter x5 -> x2, waiting for transfers between devices: 959 us -> 157 us  [the longest x1 88 us: local_by_head(): lax.psum_scatter(partial.astype(jnp.bfloat16), 'fsdp', scatter_dimension=...]
    all_gather x6 -> x5, waiting for transfers between devices: 756 us -> 215 us  [the longest x1 76.2 us: local_by_head(): x_all = lax.all_gather(x_own, 'fsdp', axis=0, tiled=True)]
    all_gather x9 -> x3, blocking collectives: 133 us -> 36 us  [the longest x1 14.6 us: gather_vectors(): lax.all_gather(jnp.concatenate(vectors), 'fsdp', axis=0, tiled=False)]
    all_to_all x0 -> x2, blocking collectives: none -> 81.8 us  [the longest x1 49.6 us: local_by_head(): quarter = lax.all_to_all(joined, 'fsdp', 0, 0, tiled=True)]
    dot_general x10, matrix products: 154 us -> 117 us  [the longest x1 32.9 us: local_by_head(): jnp.dot(second, w_in, preferred_element_type=jnp.float32)]
    psum x1, waiting for transfers between devices: 113 us -> 144 us  [local_by_head(): grad_dense = lax.psum(grad_dense, 'ctx').astype(jnp.float32)]
    all_to_all x0 -> x5, waiting for transfers between devices: none -> 28.9 us  [the longest x1 13.9 us: local_by_head(): lax.all_to_all(d_mixed, 'ctx', 1, 0, tiled=True).reshape(group, 3, hd)]
    unnamed x1 -> x0, blocking collectives: 27.8 us -> none
  transfers between devices with their start and end apart: 12 -> 15, of which waited for: 12 -> 12; matrix products, arithmetic and copies ran while one was open for 13% -> 24% of each run, Pallas kernels for 0% -> 0%
where the time goes in v1:
time: 1130 us; the launch traced here: 1120 us
  waiting for transfers between devices  548 us (48%)
  matrix products  226 us (20%)
  blocking collectives  133 us (12%)
  local copies, waits for them, and re-layouts  109 us (10%)
  other arithmetic  69.8 us (6%)
  starting transfers between devices  20.3 us (2%)
  between operations  15.3 us (1%)
    psum x1, waiting for transfers between devices, local_by_head(): grad_dense = lax.psum(grad_dense, 'ctx').astype(jnp.float32)  144 us
    reduce_scatter x1, waiting for transfers between devices, local_by_head(): lax.psum_scatter(partial.astype(jnp.bfloat16), 'fsdp', scatter_dimension=...  88 us
    all_gather x1, waiting for transfers between devices, local_by_head(): x_all = lax.all_gather(x_own, 'fsdp', axis=0, tiled=True)  76.2 us
    reduce_scatter x1, waiting for transfers between devices, local_by_head(): lax.psum_scatter((d_first * gain_one + d_second * gain_two).astype(jnp.bf...  69.4 us
    dot_general x4, matrix products, dot_right(): lax.dot_general(left_side, right_side, (((1,), (1,)), ((), ())), preferre...  64.9 us
    all_gather x1, waiting for transfers between devices, local_by_head(): g_all = lax.all_gather(g_own, 'fsdp', axis=0, tiled=True)  54.8 us
    all_gather x2, waiting for transfers between devices, by_rows(): lax.all_gather(mine_rows, 'ctx', axis=1, tiled=True).astype(jnp.float32)  49.9 us
    all_to_all x1, blocking collectives, local_by_head(): quarter = lax.all_to_all(joined, 'fsdp', 0, 0, tiled=True)  49.6 us
  transfers between devices with their start and end apart: 15, of which 12 were waited for; matrix products, arithmetic and copies ran while one was open for 24% of the time, Pallas kernels for 0%

profile of v1, /device:TPU:0, one launch (start us, length us, event | category | flops | bytes accessed | tf_op | source)
XLA Modules:
  0.0 1122.1 jit_solution(13336660696463552790)
XLA Ops:
  11.8 49.6 %all_to_all.75 = bf16[8,64,1792]{2,1,0:T(8,128)(2,1)S(1)} all-to-all(bf16[8,64,1792]{2,1,0:T(8,128)(2,1)S(1)} %copy.128), channel_id=1, replica_groups=mesh['ctx'=4,'fsdp'=8] {'fsdp'}, dimensions={0} | all-to-all | bytes 3670016 | tf_op jit(solution)/shard_map/all_to_all | solution.py:354
  66.5 12.7 %all-gather.5 = s32[8,2,256]{2,1,0:T(2,128)S(1)} all-gather(s32[1,2,256]{2,1,0:T(2,128)S(1)} %add_bitcast_fusion), channel_id=2, replica_groups=mesh['ctx'=4,'fsdp'=8] {'fsdp'}, dimensions={0}, use_global_device_ids=true | all-gather | bytes 18432 | tf_op jit(solution)/shard_map/all_gather | solution.py:335
  79.3 8.7 all-gather.1
  88.0 14.6 %all-gather.6 = bf16[8,1,2304]{2,1,0:T(2,128)(2,1)S(1)} all-gather(bf16[1,1,2304]{2,1,0:T(2,128)(2,1)S(1)} %reshape.367), channel_id=5, replica_groups=mesh['ctx'=4,'fsdp'=8] {'fsdp'}, dimensions={0}, use_global_device_ids=true | all-gather | bytes 41472 | tf_op jit(solution)/shard_map/all_gather | solution.py:289
  107.4 34.3 %all-gather.13.cloned.1.call-done = bf16[8,256,1792]{2,0,1:T(8,128)(2,1)} async-done(((bf16[8,64,1792]{2,0,1:T(8,128)(2,1)}), bf16[8,256,1792]{2,0,1:T(8,128)(2,1)}) %all-gather.13.cloned.1.call-update) | async-done | bytes 7340048 | tf_op jit(solution)/shard_map/all_gather | solution.py:355
  141.7 7.5 copy.130
  149.2 76.2 %all-gather.19.cloned.1.call-done = bf16[1,2048,2048]{2,1,0:T(8,128)(2,1)} async-done(((bf16[1,256,2048]{2,1,0:T(8,128)(2,1)}), bf16[1,2048,2048]{2,1,0:T(8,128)(2,1)}) %all-gather.19.cloned.1.call-update) | async-done | bytes 8388624 | tf_op jit(solution)/shard_map/all_gather | solution.py:359
  225.4 4.7 convert_reduce_fusion
  237.4 11.7 %broadcast_add_fusion = f32[2048,768]{0,1:T(8,128)S(1)} fusion(f32[768]{0:T(1024)S(1)} %add.129, bf16[2048,2048]{1,0:T(8,128)(2,1)S(1)} %fusion.10, bf16[2048,1792]{1,0:T(8,128)(2,1)} %bitcast.216), kind=kOutput, calls=%fused_computation.78 | convolution fusion | flops 6444023808 | bytes 17828864 | tf_op jit(solution)/shard_map/dot_general | solution.py:370
  252.8 54.8 %all-gather.21.cloned.1.call-done = bf16[1,2048,2048]{2,1,0:T(8,128)(2,1)} async-done(((bf16[1,256,2048]{2,1,0:T(8,128)(2,1)}), bf16[1,2048,2048]{2,1,0:T(8,128)(2,1)}) %all-gather.21.cloned.1.call-update) | async-done | bytes 8388624 | tf_op jit(solution)/shard_map/all_gather | solution.py:360
  307.6 7.0 fusion.59
  325.9 7.4 all-to-all-done.3
  337.2 32.9 %multiply_convert_fusion.1 = (bf16[2048,1024]{1,0:T(8,128)(2,1)}, f32[2048,1024]{1,0:T(8,128)}, f32[2048,1024]{1,0:T(8,128)}) fusion(f32[1024]{0:T(1024)S(1)} %convert_element_type.202, bf16[2048,1792]{1,0:T(8,128)(2,1)} %bitcast.217, bf16[1,2048,2048]{2,1,0:T(8,128)(2,1)} %all-gather.19.cloned.1.call-done, f32[2048]{0:T(1024)S(1)} %bitcast.243, ...), kind=kOutput, calls=%fused_computation.36 | convolution fusion | flops 8753512448 | bytes 33591296 | tf_op jit(solution)/shard_map/dot_general | solution.py:394
  379.3 4.7 fusion.97
  384.0 7.7 fusion.121
  391.7 5.7 fusion.90
  397.4 15.2 %fusion.81 = bf16[2,1024,256]{1,2,0:T(8,128)(2,1)} fusion(f32[2,1024,1024]{1,2,0:T(8,128)} %fusion.97, bf16[2,1024,768]{2,1,0:T(8,128)(2,1)S(1)} %bitcast.204, f32[2,1024,1024]{1,2,0:T(8,128)} %get-tuple-element.110, f32[2,1024]{1,0:T(2,128)S(1)} %get-tuple-element.109), kind=kOutput, calls=%fused_computation.105 | convolution fusion | flops 1088949248 | bytes 35667968 | tf_op jit(solution)/shard_map/sqk,skd->sqd/dot_general | solution.py:418
  412.6 13.7 %fusion.84 = bf16[2,1024,256]{1,2,0:T(8,128)(2,1)} fusion(f32[2,1024,1024]{1,2,0:T(8,128)} %fusion.97, bf16[2,1024,768]{2,1,0:T(8,128)(2,1)S(1)} %bitcast.205, f32[2,1024,1024]{1,2,0:T(8,128)} %get-tuple-element.110, f32[2,1024]{1,0:T(2,128)S(1)} %get-tuple-element.109), kind=kOutput, calls=%fused_computation.106 | convolution fusion | flops 1088949248 | bytes 35667968 | tf_op jit(solution)/shard_map/sqk,sqd->skd/dot_general | solution.py:419
  429.4 8.7 copy.145
  442.8 21.7 %convert_reduce_fusion.2 = (f32[1024]{0:T(1024)S(1)}, bf16[2048,1024]{1,0:T(8,128)(2,1)}) fusion(f32[2048,1024]{1,0:T(8,128)} %get-tuple-element.82, bf16[1024,2048]{1,0:T(8,128)(2,1)} %param.29, bf16[1,2048,2048]{2,1,0:T(8,128)(2,1)} %all-gather.21.cloned.1.call-done, f32[2048,1024]{1,0:T(8,128)} %get-tuple-element.108, f32[1024]{0:T(1024)S(1)} %convert_element_type.202), kind=kOutput, calls=%fused_computation.31 | convolution fusion | flops 8625585152 | bytes 33562624 | tf_op jit(solution)/shard_map/dot_general | solution.py:39
  464.6 13.9 %all-to-all-done.4 = bf16[2,1024,768]{2,0,1:T(2,128)(2,1)} async-done(((bf16[2,1024,768]{2,0,1:T(2,128)(2,1)}), bf16[2,1024,768]{2,0,1:T(2,128)(2,1)}, u32[]{:S(2)}, u32[]{:S(2)}) %all-to-all-start.4) | async-done | bytes 3145760 | tf_op jit(solution)/shard_map/all_to_all | solution.py:422
  478.4 6.7 convert_bitcast_fusion.2
  485.2 12.0 %copy.146 = f32[4,2,256,768]{2,1,0,3:T(2,128)} copy(f32[4,2,256,768]{3,1,2,0:T(2,128)} %convert_bitcast_fusion.2) | data formatting | bytes 12582912 | tf_op jit(solution)/shard_map/convert_element_type | solution.py:423
  497.2 9.0 reshape.346
  514.3 7.2 convolution_convert_fusion.1
  523.4 15.2 %convolution_convert_fusion = bf16[2048,1024]{1,0:T(8,128)(2,1)} fusion(bf16[2048,1024]{1,0:T(8,128)(2,1)} %get-tuple-element.112, bf16[1,2048,2048]{2,1,0:T(8,128)(2,1)} %all-gather.19.cloned.1.call-done, f32[2048]{0:T(1024)S(1)} %bitcast.244, f32[2048]{0:T(1024)S(1)} %bitcast.241, f32[2048]{0:T(1024)S(1)} %add_rsqrt_fusion, ...), kind=kOutput, calls=%fused_computation.65 | convolution fusion | flops 8617197568 | bytes 16809984 | tf_op jit(solution)/shard_map/dot_general | solution.py:45
  538.6 5.4 fusion.87
  549.6 14.5 %fusion.39 = bf16[1024,2048]{1,0:T(8,128)(2,1)} fusion(bf16[2048,1024]{1,0:T(8,128)(2,1)} %get-tuple-element.81, bf16[1,2048,2048]{2,1,0:T(8,128)(2,1)} %all-gather.21.cloned.1.call-done), kind=kOutput, calls=%fused_computation.64 | convolution fusion | flops 8592031744 | bytes 16777216 | tf_op jit(solution)/shard_map/dot_general | solution.py:45
  564.2 6.9 all-to-all-done.2
  571.2 6.8 fusion.62
  578.2 12.6 %fusion.54 = f32[2048,2048]{1,0:T(8,128)} fusion(bf16[2048,768]{0,1:T(8,128)(2,1)} %bitcast.230, bf16[2048,1792]{1,0:T(8,128)(2,1)} %bitcast.218), kind=kOutput, calls=%fused_computation.79 | convolution fusion | flops 6442450944 | bytes 23068672 | tf_op jit(solution)/shard_map/dot_general | solution.py:39
  594.4 23.6 %fusion.116 = (f32[2048]{0:T(1024)S(1)}, f32[2048]{0:T(1024)S(1)}, bf16[2048,2048]{1,0:T(8,128)(2,1)}, f32[2048]{0:T(1024)S(1)}, f32[2048]{0:T(1024)S(1)}) fusion(f32[2048]{0:T(1024)S(1)} %add_rsqrt_fusion, f32[2048]{0:T(1024)S(1)} %broadcast_multiply_fusion.1, bf16[1,2048,2048]{2,1,0:T(8,128)(2,1)} %all-gather.19.cloned.1.call-done, ...), kind=kOutput, calls=%fused_computation.170 | convolution fusion | flops 8644452352 | bytes 42008576 | tf_op jit(solution)/shard_map/dot_general | solution.py:39
  620.9 144.2 %all-reduce.9.cloned.1.call-done = (bf16[256,2048]{1,0:T(8,128)(2,1)}, bf16[8,4,64,1024]{3,2,1,0:T(8,128)(2,1)}, bf16[1024,2048]{1,0:T(8,128)(2,1)}) async-done(((bf16[256,2048]{1,0:T(8,128)(2,1)}, bf16[8,4,64,1024]{3,2,1,0:T(8,128)(2,1)}, bf16[1024,2048]{1,0:T(8,128)(2,1)}), (bf16[256,2048]{1,0:T(8,128)(2,1)}, bf16[8,4,64,1024]{3,2,1,0:T(8,128)(2,1)}, ...) | async-done | bytes 9437200 | tf_op jit(solution)/shard_map/psum | solution.py:491
  767.1 32.2 %all_to_all.76 = bf16[8,64,1024]{2,1,0:T(8,128)(2,1)S(1)} all-to-all(bf16[8,64,1024]{2,1,0:T(8,128)(2,1)S(1)} %dynamic-slice_bitcast_fusion), channel_id=1, replica_groups=mesh['ctx'=4,'fsdp'=8] {'fsdp'}, dimensions={0} | all-to-all | bytes 2097152 | tf_op jit(solution)/shard_map/all_to_all | solution.py:480
  801.7 15.4 %fusion.122 = f32[2048,2048]{1,0:T(8,128)} fusion(bf16[2048,1024]{1,0:T(8,128)(2,1)} %get-tuple-element.81, bf16[1024,2048]{1,0:T(8,128)(2,1)} %param.29), kind=kOutput, calls=%fused_computation.175 | convolution fusion | flops 8589934592 | bytes 25165824 | tf_op jit(solution)/shard_map/dot_general | solution.py:398
  817.1 11.4 %add_convert_fusion.1 = bf16[2048,2048]{1,0:T(8,128)(2,1)} fusion(f32[2048,2048]{1,0:T(8,128)} %fusion.122, bf16[2048,256]{1,0:T(8,128)(2,1)S(1)} %bitcast.201, bf16[256,2048]{1,0:T(8,128)(2,1)S(1)} %copy-done.13), kind=kOutput, calls=%fused_computation.20 | convolution fusion | flops 2155872256 | bytes 27262976 | tf_op jit(solution)/shard_map/dot_general | solution.py:398
  830.4 4.7 convert_reduce_fusion.1
  836.8 15.6 %psum.21 = f32[3072]{0:T(1024)S(1)} all-reduce(f32[3072]{0:T(1024)S(1)} %pad_maximum_fusion.4), channel_id=1, replica_groups=mesh['ctx'=4,'fsdp'=8] {'ctx'}, use_global_device_ids=true, to_apply=%region_19.20 | all-reduce | flops 3072 | bytes 24576 | tf_op jit(solution)/shard_map/psum | solution.py:468
  855.8 6.7 convert_element_type.231
  862.4 9.4 all-gather.15.cloned.1.call-done
  879.8 6.9 copy.153
  886.6 40.5 %all-gather.17.cloned.1.call-done = bf16[8,256,1024]{2,0,1:T(8,128)(2,1)} async-done(((bf16[8,64,1024]{2,0,1:T(8,128)(2,1)}), bf16[8,256,1024]{2,0,1:T(8,128)(2,1)}) %all-gather.17.cloned.1.call-update) | async-done | bytes 4194320 | tf_op jit(solution)/shard_map/all_gather | solution.py:481
  927.1 6.8 copy.152
  933.9 6.8 reshape.352
  940.7 9.1 copy.154
  949.8 69.4 %reduce-scatter.11.cloned.1.call-done = bf16[256,2048]{1,0:T(8,128)(2,1)} async-done(((bf16[2048,2048]{1,0:T(8,128)(2,1)}), bf16[256,2048]{1,0:T(8,128)(2,1)}) %reduce-scatter.11.cloned.1.call-update) | async-done | bytes 1048592 | tf_op jit(solution)/shard_map/reduce_scatter | solution.py:432
  1021.4 88.0 %reduce-scatter.9.cloned.1.call-done = bf16[256,2048]{1,0:T(8,128)(2,1)} async-done(((bf16[2048,2048]{1,0:T(8,128)(2,1)}), bf16[256,2048]{1,0:T(8,128)(2,1)}) %reduce-scatter.9.cloned.1.call-update) | async-done | bytes 1048592 | tf_op jit(solution)/shard_map/reduce_scatter | solution.py:401
  1109.4 5.0 fusion.71
  (198 shorter events, 101.7 us)
Async XLA Ops:
  7.2 1.9 copy-start
  7.2 134.5 %all-gather.13.cloned.1.call-start = ((), (), s32[]{:S(2)}) async-start(), calls=%async_computation.10 | async-start | bytes 9175040 | tf_op jit(solution)/shard_map/all_gather | solution.py:355
  11.3 53.8 %copy-start.20 = (bf16[1024]{0:T(1024)(128)(2,1)S(1)}, bf16[1024]{0:T(1024)(128)(2,1)}, u32[]{:S(2)}) copy-start(bf16[1024]{0:T(1024)(128)(2,1)} %param.28) | copy-start | bytes 6148
  11.3 53.8 %copy-start.24 = (bf16[256]{0:T(256)(128)(2,1)S(1)}, bf16[256]{0:T(256)(128)(2,1)}, u32[]{:S(2)}) copy-start(bf16[256]{0:T(256)(128)(2,1)} %param.19) | copy-start | bytes 1540
  11.4 54.0 %copy-start.25 = (bf16[256]{0:T(256)(128)(2,1)S(1)}, bf16[256]{0:T(256)(128)(2,1)}, u32[]{:S(2)}) copy-start(bf16[256]{0:T(256)(128)(2,1)} %param.20) | copy-start | bytes 1540
  11.4 54.2 %copy-start.26 = (bf16[256]{0:T(256)(128)(2,1)S(1)}, bf16[256]{0:T(256)(128)(2,1)}, u32[]{:S(2)}) copy-start(bf16[256]{0:T(256)(128)(2,1)} %param.21) | copy-start | bytes 1540
  11.4 54.4 %copy-start.27 = (bf16[256]{0:T(256)(128)(2,1)S(1)}, bf16[256]{0:T(256)(128)(2,1)}, u32[]{:S(2)}) copy-start(bf16[256]{0:T(256)(128)(2,1)} %param.22) | copy-start | bytes 1540
  11.4 54.6 %copy-start.21 = (bf16[768]{0:T(1024)(128)(2,1)S(1)}, bf16[768]{0:T(1024)(128)(2,1)}, u32[]{:S(2)}) copy-start(bf16[768]{0:T(1024)(128)(2,1)} %param.24) | copy-start | bytes 4612
  11.4 54.8 %copy-start.28 = (bf16[256]{0:T(256)(128)(2,1)S(1)}, bf16[256]{0:T(256)(128)(2,1)}, u32[]{:S(2)}) copy-start(bf16[256]{0:T(256)(128)(2,1)} %param.26) | copy-start | bytes 1540
  11.4 55.1 %copy-start.29 = (bf16[256]{0:T(256)(128)(2,1)S(1)}, bf16[256]{0:T(256)(128)(2,1)}, u32[]{:S(2)}) copy-start(bf16[256]{0:T(256)(128)(2,1)} %param.30) | copy-start | bytes 1540
  11.4 55.1 %copy-start.22 = (s32[1,256]{1,0:T(1,128)S(1)}, s32[1,256]{1,0:T(1,128)}, u32[]{:S(2)}) copy-start(s32[1,256]{1,0:T(1,128)} %param.18) | copy-start | bytes 3076
  11.4 55.1 %copy-start.23 = (s32[1,256]{1,0:T(1,128)S(1)}, s32[1,256]{1,0:T(1,128)}, u32[]{:S(2)}) copy-start(s32[1,256]{1,0:T(1,128)} %param.17) | copy-start | bytes 3076
  63.6 161.8 %all-gather.19.cloned.1.call-start = ((), (), s32[]{:S(2)}) async-start(), calls=%async_computation.15 | async-start | bytes 9437184 | tf_op jit(solution)/shard_map/all_gather | solution.py:359
  64.4 243.3 %all-gather.21.cloned.1.call-start = ((), (), s32[]{:S(2)}) async-start(), calls=%async_computation.16 | async-start | bytes 9437184 | tf_op jit(solution)/shard_map/all_gather | solution.py:360
  103.2 130.3 %copy-start.15 = (f32[1,2,8,128]{3,1,2,0:T(2,128)}, f32[1,2,8,128]{3,1,2,0:T(2,128)S(1)}, u32[]{:S(2)}) copy-start(f32[1,2,8,128]{3,1,2,0:T(2,128)S(1)} %copy.167) | copy-start | bytes 24580
  225.4 5.8 copy-start.2
  237.4 11.7 %copy-start.6 = (bf16[2048,2048]{1,0:T(8,128)(2,1)}, bf16[2048,2048]{1,0:T(8,128)(2,1)S(1)}, u32[]{:S(2)}) copy-start(bf16[2048,2048]{1,0:T(8,128)(2,1)S(1)} %fusion.10) | copy-start | bytes 25165828
  249.1 3.5 copy-start.5
  252.8 66.1 %copy-start.7 = (f32[2048,64]{0,1:T(8,128)S(1)}, f32[2048,64]{0,1:T(8,128)}, u32[]{:S(2)}) copy-start(f32[2048,64]{0,1:T(8,128)} %get-tuple-element.94) | copy-start | bytes 1572868
  252.8 66.1 %copy-start.10 = (f32[2048,64]{0,1:T(8,128)S(1)}, f32[2048,64]{0,1:T(8,128)}, u32[]{:S(2)}) copy-start(f32[2048,64]{0,1:T(8,128)} %get-tuple-element.93) | copy-start | bytes 1572868
  314.6 18.6 %all-to-all-start.3 = ((bf16[8,256,256]{2,1,0:T(8,128)(2,1)}), bf16[8,256,256]{2,1,0:T(8,128)(2,1)}, u32[]{:S(2)}, u32[]{:S(2)}) async-start(bf16[8,256,256]{2,1,0:T(8,128)(2,1)} %bitcast.19), calls=%async_computation.4 | async-start | bytes 2097152 | tf_op jit(solution)/shard_map/all_to_all | solution.py:408
  333.3 39.9 %all-to-all-start.1 = ((bf16[8,256,768]{1,2,0:T(8,128)(2,1)}), bf16[8,256,768]{1,2,0:T(8,128)(2,1)S(1)}, u32[]{:S(2)}, u32[]{:S(2)}) async-start(bf16[8,256,768]{1,2,0:T(8,128)(2,1)} %copy.131), calls=%async_computation.1 | async-start | bytes 6291456 | tf_op jit(solution)/shard_map/all_to_all | solution.py:376
  373.1 1.7 copy-start.4
  378.0 1.3 copy-start.8
  378.0 6.0 copy-start.12
  438.1 40.3 %all-to-all-start.4 = ((bf16[2,1024,768]{2,0,1:T(2,128)(2,1)}), bf16[2,1024,768]{2,0,1:T(2,128)(2,1)}, u32[]{:S(2)}, u32[]{:S(2)}) async-start(bf16[2,1024,768]{2,0,1:T(2,128)(2,1)} %copy.145), calls=%async_computation.5 | async-start | bytes 6291456 | tf_op jit(solution)/shard_map/all_to_all | solution.py:422
  442.8 148.0 %reduce-scatter.13.cloned.1.call-start = ((), (), s32[]{:S(2)}) async-start(), calls=%async_computation.18 | async-start | bytes 3932160
  506.1 7.8 slice-start
  511.5 2.8 slice-start.1
  513.9 7.6 copy-start.9
  546.0 25.0 %all-to-all-start.2 = ((bf16[2,1024,256]{2,0,1:T(2,128)(2,1)}), bf16[2,1024,256]{2,0,1:T(2,128)(2,1)S(1)}, u32[]{:S(2)}, u32[]{:S(2)}) async-start(bf16[2,1024,256]{2,0,1:T(2,128)(2,1)} %copy.135), calls=%async_computation.2 | async-start | bytes 2097152 | tf_op jit(solution)/shard_map/all_to_all | solution.py:392
  549.6 215.6 %all-reduce.9.cloned.1.call-start = ((), (), s32[]{:S(2)}) async-start(), calls=%async_computation.19 | async-start | bytes 18874368 | tf_op jit(solution)/shard_map/psum | solution.py:491
  578.2 16.3 %copy-start.16 = (f32[1,2,8,128]{3,1,2,0:T(2,128)S(1)}, f32[1,2,8,128]{3,1,2,0:T(2,128)}, u32[]{:S(2)}) copy-start(f32[1,2,8,128]{3,1,2,0:T(2,128)} %copy-done.15) | copy-start | bytes 24580
  590.8 28.2 %all-to-all-start.5 = ((bf16[8,64,768]{2,1,0:T(8,128)(2,1)}), bf16[8,64,768]{2,1,0:T(8,128)(2,1)S(1)}, u32[]{:S(2)}, u32[]{:S(2)}) async-start(bf16[8,64,768]{2,1,0:T(8,128)(2,1)} %bitcast.231), calls=%async_computation.7 | async-start | bytes 1572864 | tf_op jit(solution)/shard_map/all_to_all | solution.py:480
  594.4 26.0 %copy-start.31 = (u32[32]{0:T(128)S(1)}, u32[32]{0:T(128)}, u32[]{:S(2)}) copy-start(u32[32]{0:T(128)} %constant.125) | copy-start | bytes 388
  594.4 240.8 %all-reduce.7.cloned.1.call-start = ((), (), s32[]{:S(2)}) async-start(), calls=%async_computation.17 | async-start | bytes 180224
  618.9 252.9 %all-gather.15.cloned.1.call-start = ((), (), s32[]{:S(2)}) async-start(), calls=%async_computation.13 | async-start | bytes 3932160 | tf_op jit(solution)/shard_map/all_gather | solution.py:481
  620.3 306.8 %all-gather.17.cloned.1.call-start = ((), (), s32[]{:S(2)}) async-start(), calls=%async_computation.14 | async-start | bytes 5242880 | tf_op jit(solution)/shard_map/all_gather | solution.py:481
  800.9 218.3 %reduce-scatter.11.cloned.1.call-start = ((), (), s32[]{:S(2)}) async-start(), calls=%async_computation.12 | async-start | bytes 9437184 | tf_op jit(solution)/shard_map/reduce_scatter | solution.py:432
  801.6 15.4 %copy-start.13 = (bf16[256,2048]{1,0:T(8,128)(2,1)S(1)}, bf16[256,2048]{1,0:T(8,128)(2,1)}, u32[]{:S(2)}) copy-start(bf16[256,2048]{1,0:T(8,128)(2,1)} %param.25) | copy-start | bytes 3145732
  801.6 307.8 %reduce-scatter.9.cloned.1.call-start = ((), (), s32[]{:S(2)}) async-start(), calls=%async_computation.11 | async-start | bytes 9437184 | tf_op jit(solution)/shard_map/reduce_scatter | solution.py:401
  828.4 0.7 copy-start.30
  828.4 1.2 copy-start.18
  828.4 1.2 copy-start.17
  828.4 1.3 copy-start.3
  828.4 25.8 %copy-start.11 = (bf16[256,2048]{1,0:T(8,128)(2,1)S(1)}, bf16[256,2048]{1,0:T(8,128)(2,1)}, u32[]{:S(2)}) copy-start(bf16[256,2048]{1,0:T(8,128)(2,1)} %get-tuple-element.76) | copy-start | bytes 3145732
  854.2 260.3 %copy-start.19 = (f32[256]{0:T(256)}, f32[256]{0:T(256)S(1)}, u32[]{:S(2)}) copy-start(f32[256]{0:T(256)S(1)} %get-tuple-element.142) | copy-start | bytes 3076
  940.7 174.3 %copy-start.1 = (bf16[256,6144]{1,0:T(8,128)(2,1)S(1)}, bf16[256,6144]{1,0:T(8,128)(2,1)}, u32[]{:S(2)}) copy-start(bf16[256,6144]{1,0:T(8,128)(2,1)} %param.23) | copy-start | bytes 9437188
  (1 other events, 0.6 us)
Sparse Core Ops, SparseCore 0:
  63.7 77.9 all-gather.12
  143.3 82.0 all-gather.18
  227.0 80.5 all-gather.20
  523.5 48.7 reduce-scatter.12
  578.2 186.9 all-reduce.8
  767.9 55.1 all-reduce.6
  825.6 46.1 all-gather.14
  874.4 52.6 all-gather.16
  929.5 89.5 reduce-scatter.10
  1021.4 87.9 reduce-scatter.8

commit v2 on v0

--- a/solution.py
+++ b/solution.py
@@ -1,6 +1,8 @@
 import jax
 import jax.numpy as jnp
 from jax import lax
+from jax.experimental import pallas as pl
+from jax.experimental.pallas import tpu as pltpu
 from jax.sharding import PartitionSpec as P
 
 HEADS = 8
@@ -284,6 +286,787 @@
     )
 
 
+LANES = 128
+FAST = pltpu.CompilerParams(vmem_limit_bytes=56 * 1024 * 1024)
+SMALL = pl.CostEstimate(flops=1, bytes_accessed=1, transcendentals=0)
+ANY = pl.BlockSpec(memory_space=pl.ANY)
+SCALARS = pl.BlockSpec(memory_space=pltpu.SMEM)
+WHOLE = pl.BlockSpec(memory_space=pltpu.VMEM)
+low = jnp.bfloat16
+wide = jnp.float32
+
+
+def dot(a, b, left=1, right=0):
+    return lax.dot_general(a, b, (((left,), (right,)), ((), ())), preferred_element_type=wide)
+
+
+def swap(values, axis, mask):
+    return lax.ppermute(values, axis, [(i, i ^ mask) for i in range(lax.axis_size(axis))])
+
+
+def at(values, index, axis=0):
+    return lax.dynamic_index_in_dim(values, index, axis, keepdims=False)
+
+
+def added(*values):
+    total = values[0].astype(wide)
+    for v in values[1:]:
+        total = total + v.astype(wide)
+    return total.astype(low)
+
+
+def then(value, *events):
+    return lax.optimization_barrier((value,) + events)[0]
+
+
+def gather_plane(first, second):
+    first_x, second_y = swap(first, "ctx", 1), swap(second, "ctx", 2)
+    first_y, second_x = swap(first, "ctx", 2), swap(second, "ctx", 1)
+    first_xy = swap(first_y, "ctx", 1)
+    second_xy = swap(second_x, "ctx", 2)
+    return [first, first_x, first_y, first_xy], [second, second_x, second_y, second_xy]
+
+
+def place(pieces, places, count):
+    sizes = [p.shape[0] for p in pieces]
+
+    total = sum(sizes)
+
+    def body(places_ref, *refs):
+        out, buf, sems_in, sems_out = refs[-4:]
+        copies = []
+        for ref, size in zip(refs, sizes):
+            for i in range(size):
+                n = len(copies)
+                copies.append(pltpu.make_async_copy(ref.at[i], buf.at[n], sems_in.at[n]))
+                copies[n].start()
+        leaving = []
+        for n in range(total):
+            copies[n].wait()
+            copy = pltpu.make_async_copy(buf.at[n], out.at[places_ref[n]], sems_out.at[n])
+            copy.start()
+            leaving.append(copy)
+        for copy in leaving:
+            copy.wait()
+
+    return pl.pallas_call(
+        body,
+        out_shape=jax.ShapeDtypeStruct((count,) + pieces[0].shape[1:], pieces[0].dtype),
+        in_specs=[SCALARS] + [ANY] * len(pieces),
+        out_specs=ANY,
+        scratch_shapes=[
+            pltpu.VMEM((total,) + pieces[0].shape[1:], pieces[0].dtype),
+            pltpu.SemaphoreType.DMA((total,)),
+            pltpu.SemaphoreType.DMA((total,)),
+        ],
+        compiler_params=FAST,
+        cost_estimate=SMALL,
+    )(places, *pieces)
+
+
+def cut_weights(qkv_weight, fc_in_weight, extra, places, hd, units, part):
+    span = qkv_weight.shape[1] // 3
+    cols = 3 * hd + units
+
+    def body(places_ref, qkv_ref, in_ref, extra_ref, *refs):
+        outs, buf, sems_in, sems_out = refs[:4], refs[4], refs[5], refs[6]
+        row = pl.ds(pl.multiple_of(places_ref[8] * part, part), part)
+        copies = []
+        for n in range(8):
+            f = places_ref[n]
+            for t in range(3):
+                copies.append(
+                    pltpu.make_async_copy(
+                        qkv_ref.at[row, pl.ds(pl.multiple_of(t * span + f * hd, LANES), hd)],
+                        buf.at[n, :, pl.ds(t * hd, hd)],
+                        sems_in.at[len(copies)],
+                    )
+                )
+                copies[-1].start()
+            copies.append(
+                pltpu.make_async_copy(
+                    in_ref.at[row, pl.ds(pl.multiple_of(f * units, LANES), units)],
+                    buf.at[n, :, pl.ds(3 * hd, units)],
+                    sems_in.at[len(copies)],
+                )
+            )
+            copies[-1].start()
+            copies.append(
+                pltpu.make_async_copy(
+                    extra_ref, buf.at[n, :, pl.ds(cols, LANES)], sems_in.at[len(copies)]
+                )
+            )
+            copies[-1].start()
+        leaving = []
+        for n in range(8):
+            for copy in copies[5 * n : 5 * n + 5]:
+                copy.wait()
+            copy = pltpu.make_async_copy(buf.at[n], outs[n % 4].at[n // 4], sems_out.at[n])
+            copy.start()
+            leaving.append(copy)
+        for copy in leaving:
+            copy.wait()
+
+    return pl.pallas_call(
+        body,
+        out_shape=[jax.ShapeDtypeStruct((2, part, cols + LANES), low)] * 4,
+        in_specs=[SCALARS, ANY, ANY, ANY],
+        out_specs=[ANY] * 4,
+        scratch_shapes=[
+            pltpu.VMEM((8, part, cols + LANES), low),
+            pltpu.SemaphoreType.DMA((40,)),
+            pltpu.SemaphoreType.DMA((8,)),
+        ],
+        compiler_params=FAST,
+        cost_estimate=SMALL,
+    )(places, qkv_weight, fc_in_weight, extra)
+
+
+def finish(pieces, rows_at, cols_at, shape, thirds=1):
+    sizes = [p.shape[0] for p in pieces]
+    total = sum(sizes)
+    rows, cols = pieces[0].shape[1:]
+    span = cols // thirds
+
+    def body(rows_ref, cols_ref, *refs):
+        out, narrow, full, sems_in, sems_out = refs[-5:]
+        copies = []
+        for ref, size in zip(refs, sizes):
+            for i in range(size):
+                n = len(copies)
+                copies.append(pltpu.make_async_copy(ref.at[i], narrow.at[n], sems_in.at[n]))
+                copies[n].start()
+        leaving = []
+        for n in range(total):
+            copies[n].wait()
+            full[n] = narrow[n].astype(wide)
+            row = pl.ds(pl.multiple_of(rows_ref[n] * rows, rows), rows)
+            for t in range(thirds):
+                start = t * (shape[1] // thirds) + cols_ref[n] * span
+                copy = pltpu.make_async_copy(
+                    full.at[n, :, pl.ds(t * span, span)],
+                    out.at[row, pl.ds(pl.multiple_of(start, LANES), span)],
+                    sems_out.at[n * thirds + t],
+                )
+                copy.start()
+                leaving.append(copy)
+        for copy in leaving:
+            copy.wait()
+
+    return pl.pallas_call(
+        body,
+        out_shape=jax.ShapeDtypeStruct(shape, wide),
+        in_specs=[SCALARS, SCALARS] + [ANY] * len(pieces),
+        out_specs=ANY,
+        scratch_shapes=[
+            pltpu.VMEM((total, rows, cols), low),
+            pltpu.VMEM((total, rows, cols), wide),
+            pltpu.SemaphoreType.DMA((total,)),
+            pltpu.SemaphoreType.DMA((total * thirds,)),
+        ],
+        compiler_params=FAST,
+        cost_estimate=SMALL,
+    )(rows_at, cols_at, *pieces)
+
+
+def normalised(values):
+    centred = values - jnp.mean(values, axis=-1, keepdims=True)
+    spread = jnp.mean(centred * centred, axis=-1, keepdims=True)
+    rstd = lax.rsqrt(spread + eps_norm)
+    return centred * rstd, rstd
+
+
+def turn_tables(position, rotary):
+    cosine, sine = rotary_tables(position, rotary)
+    half = rotary // 2
+    zero = jnp.zeros((position.shape[0], LANES - rotary), wide)
+    none = jnp.zeros_like(sine[:, :half])
+    return (
+        jnp.concatenate([cosine, zero + 1.0], axis=1),
+        jnp.concatenate([-sine[:, :half], none, zero], axis=1),
+        jnp.concatenate([none, sine[:, half:], zero], axis=1),
+    )
+
+
+def turn(values, here, above, below, half):
+    return (
+        values * here
+        + pltpu.roll(values, LANES - half, 1) * above
+        + pltpu.roll(values, half, 1) * below
+    )
+
+
+def project(x_all, weight, bias, norms, tables, block, hd):
+    group, width = x_all.shape
+    cols = weight.shape[1]
+    half = hd // 8
+
+    def body(x_ref, w_ref, b_ref, n_ref, t0, t1, t2, first_ref, second_ref, out_ref):
+        normal, _ = normalised(x_ref[...].astype(wide))
+        first = (normal * n_ref[0:1] + n_ref[1:2]).astype(low)
+        second_ref[...] = (normal * n_ref[2:3] + n_ref[3:4]).astype(low)
+        first_ref[...] = first
+        packed = dot(first, w_ref[...]) + b_ref[...]
+        for i in range(3):
+            lead = packed[:, i * hd : i * hd + LANES]
+            if i < 2:
+                lead = turn(lead, t0[...], t1[...], t2[...], half)
+            out_ref[:, i * hd : i * hd + LANES] = lead.astype(low)
+            out_ref[:, i * hd + LANES : (i + 1) * hd] = packed[
+                :, i * hd + LANES : (i + 1) * hd
+            ].astype(low)
+
+    row = lambda n: pl.BlockSpec((block, n), lambda i: (i, 0))
+    return pl.pallas_call(
+        body,
+        grid=(group // block,),
+        in_specs=[row(width), WHOLE, WHOLE, WHOLE, row(LANES), row(LANES), row(LANES)],
+        out_specs=[row(width), row(width), row(cols)],
+        out_shape=[
+            jax.ShapeDtypeStruct((group, width), low),
+            jax.ShapeDtypeStruct((group, width), low),
+            jax.ShapeDtypeStruct((group, cols), low),
+        ],
+        compiler_params=FAST,
+        cost_estimate=SMALL,
+    )(x_all, weight, bias, norms, *tables)
+
+
+def expand(second, weight, bias, block):
+    group, width = second.shape
+    cols = weight.shape[1]
+
+    def body(s_ref, w_ref, b_ref, active_ref, slope_ref):
+        hidden = dot(s_ref[...], w_ref[...]) + b_ref[...]
+        upper = 0.5 * (1.0 + lax.erf(hidden * (0.5**0.5)))
+        active_ref[...] = (hidden * upper).astype(low)
+        bell = jnp.exp(-0.5 * hidden * hidden) * ((2.0 * jnp.pi) ** -0.5)
+        slope_ref[...] = (upper + hidden * bell).astype(low)
+
+    row = lambda n: pl.BlockSpec((block, n), lambda i: (i, 0))
+    return pl.pallas_call(
+        body,
+        grid=(group // block,),
+        in_specs=[row(width), WHOLE, WHOLE],
+        out_specs=[row(cols), row(cols)],
+        out_shape=[jax.ShapeDtypeStruct((group, cols), low)] * 2,
+        compiler_params=FAST,
+        cost_estimate=SMALL,
+    )(second, weight, bias)
+
+
+def contract(o_back, active, dense_weight, fc_out_weight, block):
+    group = active.shape[0]
+    width = fc_out_weight.shape[1]
+
+    def body(o_ref, a_ref, w1_ref, w2_ref, out_ref):
+        out_ref[...] = (dot(o_ref[...], w1_ref[...]) + dot(a_ref[...], w2_ref[...])).astype(low)
+
+    row = lambda n: pl.BlockSpec((block, n), lambda i: (i, 0))
+    return pl.pallas_call(
+        body,
+        grid=(group // block,),
+        in_specs=[row(o_back.shape[1]), row(active.shape[1]), WHOLE, WHOLE],
+        out_specs=row(width),
+        out_shape=jax.ShapeDtypeStruct((group, width), low),
+        compiler_params=FAST,
+        cost_estimate=SMALL,
+    )(o_back, active, dense_weight, fc_out_weight)
+
+
+def hidden_back(g_all, fc_out_weight, slope, block):
+    group, width = g_all.shape
+    units = fc_out_weight.shape[0]
+
+    def body(g_ref, w_ref, s_ref, out_ref, sum_ref):
+        @pl.when(pl.program_id(0) == 0)
+        def _():
+            sum_ref[...] = jnp.zeros_like(sum_ref)
+
+        d_hidden = (dot(g_ref[...], w_ref[...], 1, 1) * s_ref[...].astype(wide)).astype(low)
+        out_ref[...] = d_hidden
+        sum_ref[...] += jnp.sum(d_hidden.astype(wide), axis=0, keepdims=True)
+
+    row = lambda n: pl.BlockSpec((block, n), lambda i: (i, 0))
+    return pl.pallas_call(
+        body,
+        grid=(group // block,),
+        in_specs=[row(width), WHOLE, row(units)],
+        out_specs=[row(units), pl.BlockSpec((1, units), lambda i: (0, 0))],
+        out_shape=[
+            jax.ShapeDtypeStruct((group, units), low),
+            jax.ShapeDtypeStruct((1, units), wide),
+        ],
+        compiler_params=FAST,
+        cost_estimate=SMALL,
+    )(g_all, fc_out_weight, slope)
+
+
+def grad_pair(left, right, keep, send, parts):
+    tokens = left.shape[0]
+    cols = right.shape[1]
+    n = len(keep)
+    size = LANES // parts
+
+    def body(keep_ref, send_ref, a_ref, b_ref, right_ref, keep_out, send_out):
+        both = jnp.concatenate([a_ref[...], b_ref[...]], axis=1)
+        result = dot(both, right_ref[...], 0, 0).astype(low)
+        keep_out[...] = result[:LANES].reshape(1, parts, size, cols)
+        send_out[...] = result[LANES:].reshape(1, parts, size, cols)
+
+    shape = jax.ShapeDtypeStruct((n, parts, size, cols), low)
+    out = pl.BlockSpec((1, parts, size, cols), lambda i, k, s: (i, 0, 0, 0))
+    return pl.pallas_call(
+        body,
+        grid_spec=pltpu.PrefetchScalarGridSpec(
+            num_scalar_prefetch=2,
+            grid=(n,),
+            in_specs=[
+                pl.BlockSpec((tokens, LANES), lambda i, k, s: (0, k[i])),
+                pl.BlockSpec((tokens, LANES), lambda i, k, s: (0, s[i])),
+                pl.BlockSpec((tokens, cols), lambda i, k, s: (0, 0)),
+            ],
+            out_specs=[out, out],
+        ),
+        out_shape=[shape, shape],
+        compiler_params=FAST,
+        cost_estimate=SMALL,
+    )(jnp.stack(keep).astype(jnp.int32), jnp.stack(send).astype(jnp.int32), left, left, right)
+
+
+def add_split(kept, got, bit):
+    n, _, rows, cols = kept.shape
+
+    def body(bit_ref, a_ref, b_ref, keep_out, send_out):
+        for out, half in ((keep_out, bit_ref[0]), (send_out, 1 - bit_ref[0])):
+            out[...] = (a_ref[:, half].astype(wide) + b_ref[:, half].astype(wide)).astype(low)
+
+    shape = jax.ShapeDtypeStruct((n, rows, cols), low)
+    both = pl.BlockSpec((n // 2 if n > 1 else 1, 2, rows, cols), lambda i: (i, 0, 0, 0))
+    out = pl.BlockSpec((n // 2 if n > 1 else 1, rows, cols), lambda i: (i, 0, 0))
+    return pl.pallas_call(
+        body,
+        grid=(2 if n > 1 else 1,),
+        in_specs=[SCALARS, both, both],
+        out_specs=[out, out],
+        out_shape=[shape, shape],
+        compiler_params=FAST,
+        cost_estimate=SMALL,
+    )(bit[None].astype(jnp.int32), kept, got)
+
+
+def fetch(places_ref, sources, target, sems, block, sequences):
+    copies = []
+    for m, source in enumerate(sources):
+        for s in range(sequences):
+            n = len(copies)
+            start = pl.multiple_of(places_ref[m] * block, block)
+            copies.append(
+                pltpu.make_async_copy(source.at[s], target.at[s, pl.ds(start, block)], sems.at[n])
+            )
+            copies[n].start()
+    return copies
+
+
+def send(places_ref, source, targets, sems):
+    copies = [
+        pltpu.make_async_copy(source.at[places_ref[m]], target, sems.at[m])
+        for m, target in enumerate(targets)
+    ]
+    for copy in copies:
+        copy.start()
+    for copy in copies:
+        copy.wait()
+
+
+def block_scores(buf, row_ref, col_ref, s, i, block, hd, scale):
+    count = (i + 1) * block
+    query = buf[s, i * block : count, 0:hd]
+    key = buf[s, 0:count, hd : 2 * hd]
+    scores = dot(query, key, 1, 1) * scale
+    q_index = lax.broadcasted_iota(jnp.int32, (block, count), 0) + i * block
+    k_index = lax.broadcasted_iota(jnp.int32, (block, count), 1)
+    allowed = (col_ref[s, i * block : count, :] == row_ref[s, :, 0:count]) & (k_index <= q_index)
+    scores = jnp.where(allowed, scores, -1e30)
+    probs = jnp.exp(scores - jnp.max(scores, axis=-1, keepdims=True))
+    return query, key, probs / jnp.sum(probs, axis=-1, keepdims=True)
+
+
+def attend(parts, places, seg_row, seg_col, hd):
+    count = len(parts)
+    sequences, block, cols = parts[0].shape
+    scale = hd ** (-0.5)
+
+    def body(places_ref, row_ref, col_ref, *refs):
+        outs, (buf, mixed, sems_in, sems_out) = refs[-4 - count : -4], refs[-4:]
+        for copy in fetch(places_ref, refs[:count], buf, sems_in, block, sequences):
+            copy.wait()
+        for s in range(sequences):
+            for i in range(count):
+                _, _, probs = block_scores(buf, row_ref, col_ref, s, i, block, hd, scale)
+                value = buf[s, 0 : (i + 1) * block, 2 * hd : 3 * hd]
+                mixed[i, s] = dot(probs.astype(low), value).astype(low)
+        send(places_ref, mixed, outs, sems_out)
+
+    return pl.pallas_call(
+        body,
+        out_shape=[jax.ShapeDtypeStruct((sequences, block, hd), low)] * count,
+        in_specs=[SCALARS, WHOLE, WHOLE] + [ANY] * count,
+        out_specs=[ANY] * count,
+        scratch_shapes=[
+            pltpu.VMEM((sequences, count * block, cols), low),
+            pltpu.VMEM((count, sequences, block, hd), low),
+            pltpu.SemaphoreType.DMA((count * sequences,)),
+            pltpu.SemaphoreType.DMA((count,)),
+        ],
+        compiler_params=FAST,
+        cost_estimate=SMALL,
+    )(places, seg_row, seg_col, *parts)
+
+
+def attend_back(parts, d_parts, places, seg_row, seg_col, tables, hd):
+    count = len(parts)
+    sequences, block, cols = parts[0].shape
+    length = count * block
+    scale = hd ** (-0.5)
+    half = hd // 8
+
+    def body(places_ref, row_ref, col_ref, t0, t1, t2, *refs):
+        outs = refs[2 * count : 3 * count]
+        buf, d_buf, key_sum, value_sum, done, sems_in, sems_d, sems_out = refs[3 * count :]
+        waits = fetch(places_ref, refs[:count], buf, sems_in, block, sequences)
+        waits += fetch(places_ref, refs[count : 2 * count], d_buf, sems_d, block, sequences)
+        for copy in waits:
+            copy.wait()
+
+        def put(values, s, i, which):
+            lead = values[:, 0:LANES]
+            if which < 2:
+                rows = slice(i * block, (i + 1) * block)
+                lead = turn(lead, t0[s, rows], -t1[s, rows], -t2[s, rows], half)
+            done[i, s, :, which * hd : which * hd + LANES] = lead.astype(low)
+            done[i, s, :, which * hd + LANES : (which + 1) * hd] = values[:, LANES:].astype(low)
+
+        for s in range(sequences):
+            for i in reversed(range(count)):
+                n = (i + 1) * block
+                query, key, probs = block_scores(buf, row_ref, col_ref, s, i, block, hd, scale)
+                value = buf[s, 0:n, 2 * hd : 3 * hd]
+                d_out = d_buf[s, i * block : n]
+                d_probs = dot(d_out, value, 1, 1)
+                delta = jnp.sum(probs * d_probs, axis=-1, keepdims=True)
+                d_scores = (probs * (d_probs - delta) * scale).astype(low)
+                put(dot(d_scores, key), s, i, 0)
+                key_part = dot(d_scores, query, 0, 0)
+                value_part = dot(probs.astype(low), d_out, 0, 0)
+                if i == count - 1:
+                    key_sum[...] = key_part
+                    value_sum[...] = value_part
+                else:
+                    key_sum[0:n] += key_part
+                    value_sum[0:n] += value_part
+                put(key_sum[i * block : n], s, i, 1)
+                put(value_sum[i * block : n], s, i, 2)
+        send(places_ref, done, outs, sems_out)
+
+    return pl.pallas_call(
+        body,
+        out_shape=[jax.ShapeDtypeStruct((sequences, block, cols), low)] * count,
+        in_specs=[SCALARS] + [WHOLE] * 5 + [ANY] * (2 * count),
+        out_specs=[ANY] * count,
+        scratch_shapes=[
+            pltpu.VMEM((sequences, length, cols), low),
+            pltpu.VMEM((sequences, length, hd), low),
+            pltpu.VMEM((length, hd), wide),
+            pltpu.VMEM((length, hd), wide),
+            pltpu.VMEM((count, sequences, block, cols), low),
+            pltpu.SemaphoreType.DMA((count * sequences,)),
+            pltpu.SemaphoreType.DMA((count * sequences,)),
+            pltpu.SemaphoreType.DMA((count,)),
+        ],
+        compiler_params=FAST,
+        cost_estimate=SMALL,
+    )(places, seg_row, seg_col, *tables, *parts, *d_parts)
+
+
+def norm_back(x_all, d_packed, d_hidden, w_qkv, w_in, gains, block):
+    group, width = x_all.shape
+
+    def body(x_ref, p_ref, h_ref, w1_ref, w2_ref, g_ref, out_ref, sums_ref):
+        @pl.when(pl.program_id(0) == 0)
+        def _():
+            sums_ref[...] = jnp.zeros_like(sums_ref)
+
+        normal, _ = normalised(x_ref[...].astype(wide))
+        one = dot(p_ref[...], w1_ref[...], 1, 1)
+        two = dot(h_ref[...], w2_ref[...], 1, 1)
+        out_ref[...] = (one * g_ref[0:1] + two * g_ref[2:3]).astype(low)
+        sums_ref[0:1] += jnp.sum(one * normal, axis=0, keepdims=True)
+        sums_ref[1:2] += jnp.sum(one, axis=0, keepdims=True)
+        sums_ref[2:3] += jnp.sum(two * normal, axis=0, keepdims=True)
+        sums_ref[3:4] += jnp.sum(two, axis=0, keepdims=True)
+
+    row = lambda n: pl.BlockSpec((block, n), lambda i: (i, 0))
+    return pl.pallas_call(
+        body,
+        grid=(group // block,),
+        in_specs=[row(width), row(d_packed.shape[1]), row(d_hidden.shape[1])] + [WHOLE] * 3,
+        out_specs=[row(width), pl.BlockSpec((4, width), lambda i: (0, 0))],
+        out_shape=[
+            jax.ShapeDtypeStruct((group, width), low),
+            jax.ShapeDtypeStruct((4, width), wide),
+        ],
+        compiler_params=FAST,
+        cost_estimate=SMALL,
+    )(x_all, d_packed, d_hidden, w_qkv, w_in, gains)
+
+
+def local_by_head(
+    tokens,
+    segments,
+    positions,
+    ln1_gain,
+    ln1_bias,
+    ln2_gain,
+    ln2_bias,
+    qkv_weight,
+    qkv_bias,
+    dense_weight,
+    dense_bias,
+    fc_in_weight,
+    fc_in_bias,
+    fc_out_weight,
+    fc_out_bias,
+    cotangent,
+):
+    width = tokens.shape[-1]
+    block = tokens.shape[1]
+    nf = lax.axis_size("fsdp")
+    nc = lax.axis_size("ctx")
+    me_c = lax.axis_index("ctx")
+    me_f = lax.axis_index("fsdp")
+    hd = width // HEADS
+    units = fc_in_weight.shape[1] // nf
+    group = nf * block
+    length = nc * block
+    rows = width // nf
+    part = rows // nc
+    x_own = tokens.reshape(block, width)
+    g_own = cotangent.reshape(block, width)
+    order = jnp.array([2 * j + kk for kk in range(2) for j in range(4)], jnp.int32)
+    owners = jnp.bitwise_xor(order, me_f)
+    plane = jnp.bitwise_xor(jnp.arange(nc, dtype=jnp.int32), me_c)
+
+    ints = jnp.concatenate([segments, positions], axis=0)
+    digits = jnp.concatenate([ints // 32, ints % 32]).astype(low)
+    vectors = [ln1_gain, ln1_bias, ln2_gain, ln2_bias, qkv_bias, dense_bias, fc_out_bias]
+    sizes = [v.shape[0] for v in vectors]
+    extra = jnp.concatenate([digits.reshape(-1)] + vectors)
+    extra = jnp.pad(extra, (0, part * LANES - extra.shape[0])).reshape(part, LANES)
+
+    pieces = cut_weights(
+        qkv_weight,
+        fc_in_weight,
+        extra,
+        jnp.concatenate([owners, me_c[None]]).astype(jnp.int32),
+        hd,
+        units,
+        part,
+    )
+    got = [pieces[0]] + [swap(pieces[j], "fsdp", 2 * j) for j in (1, 2, 3)]
+    x_all = lax.all_gather(then(x_own, *got), "fsdp", axis=0, tiled=True)
+    across = swap(jnp.stack([g[1] for g in got]), "fsdp", 1)
+    g_all = lax.all_gather(then(g_own, across), "fsdp", axis=0, tiled=True)
+    quarter = jnp.concatenate([jnp.stack([g[0] for g in got]), across])
+    cols = 3 * hd + units
+    qkv_parts, in_parts = gather_plane(quarter[..., : 3 * hd], quarter[..., 3 * hd : cols])
+
+    back = (jnp.arange(nf, dtype=jnp.int32)[:, None] == owners[None, :]).astype(low)
+    small = dot(back, quarter[..., cols:].reshape(nf, part * LANES))
+    count = 4 * block
+    digits = small[:, :count].astype(jnp.int32).reshape(nf, 2, 2, block)
+    numbers = digits[:, 0] * 32 + digits[:, 1]
+    position_group = numbers[:, 1].reshape(group)
+    of_chip = numbers.reshape(4, 2, 2, block)
+    seq_ints = [at(of_chip, me_c)] + [swap(at(of_chip, plane[m]), "ctx", m) for m in range(1, nc)]
+    seq_ints = jnp.stack(seq_ints, axis=2)
+    seq_ints = jnp.stack([at(seq_ints, plane[b], 2) for b in range(nc)], axis=2)
+    seq_ints = seq_ints.reshape(2, 2, length)
+    seg_row = seq_ints[:, 0][:, None, :]
+    seg_col = seq_ints[:, 0][:, :, None]
+    tables = turn_tables(position_group, hd // 4)
+    seq_tables = [
+        t.reshape(2, length, LANES) for t in turn_tables(seq_ints[:, 1].reshape(-1), hd // 4)
+    ]
+    whole, start = [], count
+    for size in sizes:
+        whole.append(small[:, start : start + size].reshape(-1))
+        start += size
+    norms = jnp.stack(whole[:4])
+    head_bias = at(whole[4].reshape(3, nf, hd), me_f, 1).reshape(1, -1)
+
+    row_places = (owners[None, :] * nc + plane[:, None]).reshape(-1)
+    w_qkv = place(qkv_parts, row_places, nf * nc).reshape(width, 3 * hd)
+    w_in = place(in_parts, row_places, nf * nc).reshape(width, units)
+
+    first, second, packed = project(
+        then(x_all, w_in), w_qkv, head_bias, norms, tables, block, hd
+    )
+
+    def to_sequences(values):
+        blocks = values.reshape(4, 2, block, values.shape[1])
+        return [
+            at(blocks, plane[m]) if m == 0 else swap(at(blocks, plane[m]), "ctx", m)
+            for m in range(nc)
+        ]
+
+    def to_group(values):
+        got = [values[m] if m == 0 else swap(values[m], "ctx", m) for m in range(nc)]
+        places = (2 * plane[:, None] + jnp.arange(2, dtype=jnp.int32)[None, :]).reshape(-1)
+        return place(got, places, nf).reshape(group, values[0].shape[-1])
+
+    parts = to_sequences(packed)
+    active, slope = expand(
+        then(second, packed), w_in, fc_in_bias.astype(wide).reshape(1, -1), block
+    )
+    o = attend([then(p, active) for p in parts], plane, seg_row, seg_col, hd)
+    o_back = to_group(o)
+    x_bit, y_bit = me_c % 2, me_c // 2
+    d_o = dot(then(g_all, *o), dense_weight, 1, 1).astype(low)
+    d_parts = to_sequences(d_o)
+    partial = contract(then(o_back, d_o), active, dense_weight, fc_out_weight, block)
+    summed = lax.psum_scatter(partial, "fsdp", scatter_dimension=0, tiled=True)
+    d_qkv = attend_back(
+        parts, [then(p, partial) for p in d_parts], plane, seg_row, seg_col, seq_tables, hd
+    )
+    d_packed = to_group(d_qkv)
+
+    rows_of = units // (nc * LANES)
+    blocks = [((2 * y) * rows_of, s) for y in range(2) for s in range(rows_of)]
+    out_kept, out_sent = grad_pair(
+        active,
+        then(g_all, *d_qkv),
+        [b + x_bit * rows_of + s for b, s in blocks],
+        [b + (1 - x_bit) * rows_of + s for b, s in blocks],
+        1,
+    )
+    out_shape = (1, 2, rows_of * LANES, width)
+    out_got = swap(out_sent.reshape(out_shape), "ctx", 1)
+    out_kept = out_kept.reshape(out_shape)
+    d_hidden, hidden_sum = hidden_back(then(g_all, out_sent), fc_out_weight, slope, block)
+    by_bit = lambda bit: ([2 * f + bit for f in range(nf)], [2 * f + 1 - bit for f in range(nf)])
+    in_kept, in_sent = grad_pair(second, d_hidden, *by_bit(y_bit), 2)
+    in_got = swap(in_sent, "ctx", 2)
+    qkv_kept, qkv_sent = grad_pair(first, then(d_packed, in_sent), *by_bit(x_bit), 2)
+    qkv_got = swap(qkv_sent, "ctx", 1)
+    d_partial, sums = norm_back(
+        then(x_all, qkv_sent), d_packed, d_hidden, w_qkv, w_in, norms, block
+    )
+    dense_kept, dense_sent = grad_pair(
+        o_back, then(g_all, d_partial), [y_bit], [1 - y_bit], 2
+    )
+    def spread_out(values, parts):
+        whole = jnp.zeros((parts, nf, values.shape[0] // parts), wide)
+        return lax.dynamic_update_slice_in_dim(
+            whole, values.reshape(parts, 1, -1), me_f, 1
+        ).reshape(nf, -1)
+
+    totals = jnp.concatenate(
+        [sums[i].reshape(nf, -1) for i in range(4)]
+        + [
+            spread_out(jnp.sum(d_packed.astype(wide), axis=0), 3),
+            spread_out(hidden_sum[0], 1),
+            jnp.sum(g_own.astype(wide), axis=0).reshape(nf, -1),
+        ],
+        axis=1,
+    )
+    total_1 = swap(totals, "fsdp", 1)
+    out_kept, out_sent = add_split(out_kept, then(out_got, dense_sent, total_1), y_bit)
+    out_got = swap(out_sent, "ctx", 2)
+    totals = totals + total_1
+    total_2 = swap(totals, "fsdp", 2)
+    in_kept, in_sent = add_split(in_kept, then(in_got, out_sent, total_2), x_bit)
+    in_got = swap(in_sent, "ctx", 1)
+    totals = totals + total_2
+    total_3 = swap(totals, "fsdp", 4)
+    qkv_kept, qkv_sent = add_split(qkv_kept, then(qkv_got, in_sent, total_3), y_bit)
+    qkv_got = swap(qkv_sent, "ctx", 2)
+    d_normal = lax.psum_scatter(
+        then(d_partial, summed, qkv_sent), "fsdp", scatter_dimension=0, tiled=True
+    ).astype(wide)
+    totals = totals + total_3
+    total_4 = swap(totals, "ctx", 1)
+    dense_got = swap(then(dense_sent, qkv_sent), "ctx", 2)
+    out_mine = added(out_kept, then(out_got, qkv_sent, total_4))
+    out_x, out_y = swap(out_mine, "ctx", 1), swap(out_mine, "ctx", 2)
+    totals = totals + total_4
+    total_5 = swap(totals, "ctx", 2)
+    dense_kept, dense_sent = add_split(dense_kept, then(dense_got, qkv_sent, total_5), x_bit)
+    totals = totals + total_5
+    dense_got = swap(dense_sent, "ctx", 1)
+    in_mine = added(in_kept, then(in_got, dense_sent))
+    in_rows = lax.all_to_all(in_mine, "fsdp", 0, 0, tiled=True)
+    qkv_mine = added(qkv_kept, then(qkv_got, in_got))
+    dense_mine = added(dense_kept, then(dense_got, qkv_got))
+    out_xy = swap(then(out_y, dense_got), "ctx", 1)
+    qkv_rows = lax.all_to_all(then(qkv_mine, in_rows), "fsdp", 0, 0, tiled=True)
+    dense_x, dense_y = swap(dense_mine, "ctx", 1), swap(dense_mine, "ctx", 2)
+    in_x, in_y = swap(in_rows, "ctx", 1), swap(in_rows, "ctx", 2)
+    dense_xy = swap(then(dense_x, qkv_rows), "ctx", 2)
+    qkv_x, qkv_y = swap(qkv_rows, "ctx", 1), swap(qkv_rows, "ctx", 2)
+    in_xy = swap(in_x, "ctx", 2)
+    qkv_xy = swap(qkv_y, "ctx", 1)
+    out_all = [out_mine, out_x, out_y, out_xy]
+    in_all = [in_rows, in_x, in_y, in_xy]
+    dense_all = [dense_mine, dense_x, dense_y, dense_xy]
+    qkv_all = [qkv_rows, qkv_x, qkv_y, qkv_xy]
+
+    def whole_rows(pieces, shape):
+        return finish(pieces, plane, jnp.zeros((nc,), jnp.int32), shape)
+
+    def whole_columns(pieces, places, shape, thirds):
+        at_rows = (places[:, None] * jnp.ones((nf,), jnp.int32)).reshape(-1)
+        at_cols = jnp.tile(jnp.arange(nf, dtype=jnp.int32), nc)
+        return finish(pieces, at_rows, at_cols, shape, thirds)
+
+    grad_fc_out = whole_rows(out_all, fc_out_weight.shape)
+    grad_fc_in = whole_columns(in_all, plane, fc_in_weight.shape, 1)
+    grad_dense = whole_rows(dense_all, dense_weight.shape)
+    grad_qkv = whole_columns(qkv_all, 2 * (plane % 2) + plane // 2, qkv_weight.shape, 3)
+
+    x_wide = x_own.astype(wide)
+    output = (x_wide + summed.astype(wide) + whole[5] + whole[6]).astype(low).reshape(tokens.shape)
+    own_normal, own_rstd = normalised(x_wide)
+    d_x = own_rstd * (
+        d_normal
+        - jnp.mean(d_normal, axis=-1, keepdims=True)
+        - own_normal * jnp.mean(d_normal * own_normal, axis=-1, keepdims=True)
+    )
+    input_grad = (g_own.astype(wide) + d_x).reshape(tokens.shape)
+
+    totals = at(totals, me_f)
+    cuts, start = [], 0
+    for size in (rows, rows, rows, rows, 3 * width // nf, units, rows):
+        cuts.append(totals[start : start + size])
+        start += size
+    return (
+        output,
+        input_grad,
+        cuts[0],
+        cuts[1],
+        cuts[2],
+        cuts[3],
+        grad_qkv,
+        cuts[4],
+        grad_dense,
+        cuts[6],
+        grad_fc_in,
+        cuts[5],
+        grad_fc_out,
+        cuts[6],
+    )
+
+
 def solution(mesh):
     placed = (
         P("fsdp", "ctx", None),
@@ -303,8 +1086,9 @@
         P("fsdp"),
         P("fsdp", "ctx", None),
     )
+    by_head = mesh.shape["fsdp"] == HEADS and mesh.shape["ctx"] == 4
     return jax.shard_map(
-        local,
+        local_by_head if by_head else local,
         mesh=mesh,
         in_specs=placed,
         out_specs=(

time: 2400 us -> 660 us (0.28)
  waiting for transfers between devices: 1830 us -> 266 us
  matrix products: 277 us -> 6.2 us
  Pallas kernels: 0 us -> 216 us
  blocking collectives: 171 us -> 0 us
  starting transfers between devices: 0.66 us -> 65.8 us
  other arithmetic: 60.6 us -> 30.2 us
    reduce_scatter x5 -> x2, waiting for transfers between devices: 959 us -> 0.02 us  [the longest x1 0.02 us: local_by_head(): lax.psum_scatter(then(d_partial, summed, qkv_sent), 'fsdp', scatter_dimen...]
    all_gather x6 -> x2, waiting for transfers between devices: 756 us -> 10.3 us  [the longest x1 10.2 us: local_by_head(): g_all = lax.all_gather(then(g_own, across), 'fsdp', axis=0, tiled=True)]
    dot_general x18 -> x2, matrix products: 277 us -> 6.2 us  [dot(): lax.dot_general(a, b, (((left,), (right,)), ((), ())), preferred_element_...]
    ppermute x0 -> x50, waiting for transfers between devices: none -> 219 us  [swap(): lax.ppermute(values, axis, [(i, i ^ mask) for i in range(lax.axis_size(ax...]
    pallas_call x0 -> x24, Pallas kernels: none -> 216 us  [the longest x4 50.1 us: grad_pair(): pl.pallas_call(body, grid_spec=pltpu.PrefetchScalarGridSpec(num_scalar_pr...]
    all_gather x9 -> x0, blocking collectives: 133 us -> none  [the longest x1 28.6 us: local(): lax.all_gather(qkv_bias, 'fsdp', axis=0, tiled=True)]
    psum x1 -> x0, waiting for transfers between devices: 113 us -> none  [reduce_grads(): lax.psum(shared[0].astype(jnp.bfloat16), 'ctx').astype(jnp.float32)]
    ppermute x0 -> x50, starting transfers between devices: none -> 57.2 us  [swap(): lax.ppermute(values, axis, [(i, i ^ mask) for i in range(lax.axis_size(ax...]
  transfers between devices with their start and end apart: 12 -> 56, of which waited for: 12 -> 24; matrix products, arithmetic and copies ran while one was open for 13% -> 8% of each run, Pallas kernels for 0% -> 30%
where the time goes in v2:
time: 660 us; the launch traced here: 655 us
  waiting for transfers between devices  266 us (40%)
  Pallas kernels  216 us (33%)
  starting transfers between devices  65.8 us (10%)
  local copies, waits for them, and re-layouts  47.5 us (7%)
  other arithmetic  30.2 us (5%)
  between operations  22.8 us (3%)
    ppermute x50, waiting for transfers between devices, swap(): lax.ppermute(values, axis, [(i, i ^ mask) for i in range(lax.axis_size(ax...  219 us
    ppermute x50, starting transfers between devices, swap(): lax.ppermute(values, axis, [(i, i ^ mask) for i in range(lax.axis_size(ax...  57.2 us
    pallas_call x4, Pallas kernels, grad_pair(): pl.pallas_call(body, grid_spec=pltpu.PrefetchScalarGridSpec(num_scalar_pr...  50.1 us
    pallas_call x1, Pallas kernels, norm_back(): pl.pallas_call(body, grid=(group // block,), in_specs=[row(width), row(d_...  26.4 us
    all_to_all x1, waiting for transfers between devices, local_by_head(): in_rows = lax.all_to_all(in_mine, 'fsdp', 0, 0, tiled=True)  22 us
    unnamed x114, local copies, waits for them, and re-layouts  21.2 us
    pallas_call x4, Pallas kernels, finish(): pl.pallas_call(body, out_shape=jax.ShapeDtypeStruct(shape, wide), in_spec...  19.3 us
    pallas_call x1, Pallas kernels, project(): pl.pallas_call(body, grid=(group // block,), in_specs=[row(width), WHOLE,...  17.6 us
  transfers between devices with their start and end apart: 56, of which 24 were waited for; matrix products, arithmetic and copies ran while one was open for 8% of the time, Pallas kernels for 30%

profile of v2, /device:TPU:0, one launch (start us, length us, event | category | flops | bytes accessed | tf_op | source)
XLA Modules:
  0.0 655.0 jit_solution(2563201731729725050)
XLA Ops:
  15.5 3.8 shard_map.272
  19.3 3.1 collective-permute-start
  25.0 18.6 %collective-permute-done = bf16[2,64,1920]{2,1,0:T(8,128)(2,1)S(1)} collective-permute-done((bf16[2,64,1920]{2,1,0:T(8,128)(2,1)}, bf16[2,64,1920]{2,1,0:T(8,128)(2,1)S(1)}, u32[]{:S(2)}, u32[]{:S(2)}) %collective-permute-start) | collective-permute-done | bytes 491552 | tf_op jit(solution)/shard_map/ppermute | solution.py:304
  43.6 15.1 %collective-permute-done.1 = bf16[2,64,1920]{2,1,0:T(8,128)(2,1)S(1)} collective-permute-done((bf16[2,64,1920]{2,1,0:T(8,128)(2,1)}, bf16[2,64,1920]{2,1,0:T(8,128)(2,1)S(1)}, u32[]{:S(2)}, u32[]{:S(2)}) %collective-permute-start.1) | collective-permute-done | bytes 491552 | tf_op jit(solution)/shard_map/ppermute | solution.py:304
  88.1 10.5 %collective-permute-done.4 = s32[2,2,256]{2,1,0:T(2,128)S(1)} collective-permute-done((s32[2,2,256]{2,1,0:T(2,128)S(1)}, s32[2,2,256]{2,1,0:T(2,128)S(1)}, u32[]{:S(2)}, u32[]{:S(2)}) %collective-permute-start.4) | collective-permute-done | bytes 4128 | tf_op jit(solution)/shard_map/ppermute | solution.py:304
  101.8 4.0 fusion.16
  105.9 4.0 fusion.18
  111.1 13.7 %collective-permute-done.7.refs_1_ = bf16[8,64,1024]{2,1,0:T(8,128)(2,1)} collective-permute-done((bf16[8,64,1024]{2,1,0:T(8,128)(2,1)S(1)}, bf16[8,64,1024]{2,1,0:T(8,128)(2,1)}, u32[]{:S(2)}, u32[]{:S(2)}) %collective-permute-start.7) | collective-permute-done | bytes 1048608 | tf_op jit(solution)/shard_map/ppermute | solution.py:304
  129.7 9.7 %collective-permute-done.12.refs_3_ = bf16[8,64,768]{2,1,0:T(8,128)(2,1)S(1)} collective-permute-done((bf16[8,64,768]{2,1,0:T(8,128)(2,1)}, bf16[8,64,768]{2,1,0:T(8,128)(2,1)S(1)}, u32[]{:S(2)}, u32[]{:S(2)}) %collective-permute-start.12) | collective-permute-done | bytes 786464 | tf_op jit(solution)/shard_map/ppermute | solution.py:304
  140.3 4.2 shard_map.274
  147.2 5.3 shard_map.273
  152.5 17.6 %shard_map.275 = (bf16[2048,2048]{1,0:T(8,128)(2,1)}, bf16[2048,2048]{1,0:T(8,128)(2,1)}, bf16[2048,768]{1,0:T(8,128)(2,1)}) custom-call(bf16[2048,2048]{1,0:T(8,128)(2,1)} %all-gather.3.cloned.1.call-done.x_ref, bf16[2048,768]{1,0:T(8,128)(2,1)} %bitcast.155, f32[1,768]{1,0:T(1,128)} %bitcast.180, f32[4,2048]{1,0:T(4,128)} %pad_maximum_fusion.7.n_ref.g_ref, ...), custom_call_target="tpu_custom_call" | custom-call | flops 1 | bytes 1 | tf_op jit(solution)/shard_map/pallas_call | solution.py:520
  170.1 3.6 dynamic-slice_bitcast_fusion
  179.8 17.1 %shard_map.276 = (bf16[2048,1024]{1,0:T(8,128)(2,1)}, bf16[2048,1024]{1,0:T(8,128)(2,1)}) custom-call(bf16[2048,2048]{1,0:T(8,128)(2,1)} %get-tuple-element.91.s_ref.a_ref.b_ref, bf16[2048,1024]{1,0:T(8,128)(2,1)} %bitcast.153, f32[1,1024]{1,0:T(1,128)} %bitcast.178), custom_call_target="tpu_custom_call" | custom-call | flops 1 | bytes 1 | tf_op jit(solution)/shard_map/pallas_call | solution.py:547
  196.9 11.2 %collective-permute-done.14.refs_2_ = bf16[2,256,768]{2,1,0:T(8,128)(2,1)S(1)} collective-permute-done((bf16[2,256,768]{2,1,0:T(8,128)(2,1)}, bf16[2,256,768]{2,1,0:T(8,128)(2,1)S(1)}, u32[]{:S(2)}, u32[]{:S(2)}) %collective-permute-start.14) | collective-permute-done | bytes 786464 | tf_op jit(solution)/shard_map/ppermute | solution.py:304
  209.3 8.4 %shard_map.277 = (bf16[2,256,256]{2,1,0:T(8,128)(2,1)}, bf16[2,256,256]{2,1,0:T(8,128)(2,1)}, bf16[2,256,256]{2,1,0:T(8,128)(2,1)}, bf16[2,256,256]{2,1,0:T(8,128)(2,1)}) custom-call(s32[4]{0:T(128)} %copy-done.34, s32[2,1,1024]{2,1,0:T(1,128)} %get-tuple-element.196.row_ref, s32[2,1024,1]{2,1,0:T(8,128)} %broadcast_in_dim_squeeze.4.col_ref, ...), custom_call_target="tpu_custom_call" | custom-call | flops 1 | bytes 1 | tf_op jit(solution)/shard_map/pallas_call | solution.py:711
  221.3 10.2 %all-gather.5.cloned.1.call-done.right_ref.g_ref = bf16[2048,2048]{1,0:T(8,128)(2,1)} async-done(((bf16[256,2048]{1,0:T(8,128)(2,1)}), bf16[2048,2048]{1,0:T(8,128)(2,1)}) %all-gather.5.cloned.1.call-update) | async-done | bytes 8388624 | tf_op jit(solution)/shard_map/all_gather | solution.py:879
  231.5 6.0 convolution_convert_fusion
  241.8 16.1 %shard_map.279 = bf16[2048,2048]{1,0:T(8,128)(2,1)} custom-call(bf16[2048,256]{1,0:T(8,128)(2,1)} %bitcast.158, bf16[2048,1024]{1,0:T(8,128)(2,1)} %get-tuple-element.92.a_ref.b_ref, bf16[256,2048]{1,0:T(8,128)(2,1)} %w1_ref.1, bf16[1024,2048]{1,0:T(8,128)(2,1)} %w_ref.1), custom_call_target="tpu_custom_call" | custom-call | flops 1 | bytes 1 | tf_op jit(solution)/shard_map/pallas_call | solution.py:566
  263.7 5.6 collective-permute-done.21.refs_7_
  269.3 4.9 collective-permute-done.20.refs_6_
  275.0 14.0 %shard_map.280 = (bf16[2,256,768]{2,1,0:T(8,128)(2,1)}, bf16[2,256,768]{2,1,0:T(8,128)(2,1)}, bf16[2,256,768]{2,1,0:T(8,128)(2,1)}, bf16[2,256,768]{2,1,0:T(8,128)(2,1)}) custom-call(s32[4]{0:T(128)} %copy-done.34, s32[2,1,1024]{2,1,0:T(1,128)} %get-tuple-element.196.row_ref, s32[2,1024,1]{2,1,0:T(8,128)} %broadcast_in_dim_squeeze.4.col_ref, ...), custom_call_target="tpu_custom_call" | custom-call | flops 1 | bytes 1 | tf_op jit(solution)/shard_map/pallas_call | solution.py:772
  294.5 15.2 %shard_map.282 = (bf16[4,1,128,2048]{3,2,1,0:T(8,128)(2,1)}, bf16[4,1,128,2048]{3,2,1,0:T(8,128)(2,1)}) custom-call(s32[4]{0:T(128)} %get-tuple-element.222.keep_ref, s32[4]{0:T(128)} %get-tuple-element.223.send_ref, bf16[2048,1024]{1,0:T(8,128)(2,1)} %get-tuple-element.92.a_ref.b_ref, bf16[2048,1024]{1,0:T(8,128)(2,1)} %get-tuple-element.92.a_ref.b_ref, ...), custom_call_target="tpu_custom_call" | custom-call | flops 1 | bytes 1 | tf_op jit(solution)/shard_map/pallas_call | solution.py:619
  311.2 15.4 %shard_map.283 = (bf16[2048,1024]{1,0:T(8,128)(2,1)}, f32[1,1024]{1,0:T(1,128)}) custom-call(bf16[2048,2048]{1,0:T(8,128)(2,1)} %all-gather.5.cloned.1.call-done.right_ref.g_ref, bf16[1024,2048]{1,0:T(8,128)(2,1)} %w_ref.1, bf16[2048,1024]{1,0:T(8,128)(2,1)} %get-tuple-element.116.s_ref), custom_call_target="tpu_custom_call" | custom-call | flops 1 | bytes 1 | tf_op jit(solution)/shard_map/pallas_call | solution.py:591
  326.6 14.6 %shard_map.284 = (bf16[8,2,64,1024]{3,2,1,0:T(8,128)(2,1)}, bf16[8,2,64,1024]{3,2,1,0:T(8,128)(2,1)}) custom-call(s32[8]{0:T(128)} %stack.202.keep_ref, s32[8]{0:T(128)} %stack.211.send_ref, bf16[2048,2048]{1,0:T(8,128)(2,1)} %get-tuple-element.91.s_ref.a_ref.b_ref, bf16[2048,2048]{1,0:T(8,128)(2,1)} %get-tuple-element.91.s_ref.a_ref.b_ref, ...), custom_call_target="tpu_custom_call" | custom-call | flops 1 | bytes 1 | tf_op jit(solution)/shard_map/pallas_call | solution.py:619
  345.3 3.5 shard_map.281
  348.8 13.1 %shard_map.285 = (bf16[8,2,64,768]{3,2,1,0:T(8,128)(2,1)}, bf16[8,2,64,768]{3,2,1,0:T(8,128)(2,1)}) custom-call(s32[8]{0:T(128)} %stack.184.keep_ref, s32[8]{0:T(128)} %stack.193.send_ref, bf16[2048,2048]{1,0:T(8,128)(2,1)} %get-tuple-element.104.a_ref.b_ref, bf16[2048,2048]{1,0:T(8,128)(2,1)} %get-tuple-element.104.a_ref.b_ref, bf16[2048,768]{1,0:T(8,128)(2,1)} %bitcast.151), custom_call_target="tpu_custom_call" | custom-call | flops 1 | bytes 1 | tf_op jit(solution)/shard_map/pallas_call | solution.py:619
  363.6 26.4 %shard_map.286 = (bf16[2048,2048]{1,0:T(8,128)(2,1)}, f32[4,2048]{1,0:T(4,128)}) custom-call(bf16[2048,2048]{1,0:T(8,128)(2,1)} %all-gather.3.cloned.1.call-done.x_ref, bf16[2048,768]{1,0:T(8,128)(2,1)} %bitcast.152, bf16[2048,1024]{1,0:T(8,128)(2,1)} %get-tuple-element.117.right_ref.h_ref, bf16[2048,768]{1,0:T(8,128)(2,1)} %bitcast.156, ...), custom_call_target="tpu_custom_call" | custom-call | flops 1 | bytes 1 | tf_op jit(solution)/shard_map/pallas_call | solution.py:810
  395.2 3.1 collective-permute-done.29
  401.3 7.0 %shard_map.287 = (bf16[1,2,64,2048]{3,2,1,0:T(8,128)(2,1)}, bf16[1,2,64,2048]{3,2,1,0:T(8,128)(2,1)}) custom-call(s32[1]{0:T(128)} %bitcast.50.keep_ref.bit_ref, s32[1]{0:T(128)} %bitcast.58.send_ref, bf16[2048,256]{1,0:T(8,128)(2,1)} %bitcast.159, bf16[2048,256]{1,0:T(8,128)(2,1)} %bitcast.160, bf16[2048,2048]{1,0:T(8,128)(2,1)} %all-gather.5.cloned.1.call-done.right_ref.g_ref), custom_call_target="tpu_custom_call" | custom-call | flops 1 | bytes 1 | tf_op jit(solution)/shard_map/pallas_call | solution.py:619
  408.3 3.9 shard_map.288
  412.3 3.5 shard_map.289
  422.6 23.6 %collective-permute-done.31 = f32[8,3072]{1,0:T(8,128)S(1)} collective-permute-done((f32[8,3072]{1,0:T(8,128)S(1)}, f32[8,3072]{1,0:T(8,128)S(1)}, u32[]{:S(2)}, u32[]{:S(2)}) %collective-permute-start.31) | collective-permute-done | bytes 98336 | tf_op jit(solution)/shard_map/ppermute | solution.py:304
  446.9 4.0 collective-permute-done.32
  455.2 3.6 all-to-all-start
  460.9 18.5 %collective-permute-done.33 = bf16[8,64,768]{2,1,0:T(8,128)(2,1)S(1)} collective-permute-done((bf16[8,64,768]{2,1,0:T(8,128)(2,1)}, bf16[8,64,768]{2,1,0:T(8,128)(2,1)S(1)}, u32[]{:S(2)}, u32[]{:S(2)}) %collective-permute-start.33) | collective-permute-done | bytes 786464 | tf_op jit(solution)/shard_map/ppermute | solution.py:304
  480.5 22.0 %all-to-all-done.refs_0_ = bf16[8,64,1024]{2,1,0:T(8,128)(2,1)S(1)} async-done(((bf16[8,64,1024]{2,1,0:T(8,128)(2,1)}), bf16[8,64,1024]{2,1,0:T(8,128)(2,1)S(1)}, u32[]{:S(2)}, u32[]{:S(2)}) %all-to-all-start) | async-done | bytes 1048608 | tf_op jit(solution)/shard_map/all_to_all | solution.py:1008
  502.5 4.2 all-to-all-start.1
  512.4 7.1 %collective-permute-done.39 = bf16[1,64,2048]{2,1,0:T(8,128)(2,1)S(1)} collective-permute-done((bf16[1,64,2048]{2,1,0:T(8,128)(2,1)S(1)}, bf16[1,64,2048]{2,1,0:T(8,128)(2,1)S(1)}, u32[]{:S(2)}, u32[]{:S(2)}) %collective-permute-start.39) | collective-permute-done | bytes 262176 | tf_op jit(solution)/shard_map/ppermute | solution.py:304
  522.6 15.0 %all-to-all-done.1.refs_0_ = bf16[8,64,768]{2,1,0:T(8,128)(2,1)} async-done(((bf16[8,64,768]{2,1,0:T(8,128)(2,1)}), bf16[8,64,768]{2,1,0:T(8,128)(2,1)}, u32[]{:S(2)}, u32[]{:S(2)}) %all-to-all-start.1) | async-done | bytes 786464 | tf_op jit(solution)/shard_map/all_to_all | solution.py:1012
  539.7 29.7 %collective-permute-done.40.refs_1_ = bf16[1,64,2048]{2,1,0:T(8,128)(2,1)} collective-permute-done((bf16[1,64,2048]{2,1,0:T(8,128)(2,1)S(1)}, bf16[1,64,2048]{2,1,0:T(8,128)(2,1)}, u32[]{:S(2)}, u32[]{:S(2)}) %collective-permute-start.40) | collective-permute-done | bytes 262176 | tf_op jit(solution)/shard_map/ppermute | solution.py:304
  578.1 17.6 %collective-permute-done.49.refs_3_ = bf16[1,256,2048]{2,1,0:T(8,128)(2,1)} collective-permute-done((bf16[1,256,2048]{2,1,0:T(8,128)(2,1)}, bf16[1,256,2048]{2,1,0:T(8,128)(2,1)}, u32[]{:S(2)}, u32[]{:S(2)}) %collective-permute-start.49) | collective-permute-done | bytes 1048608 | tf_op jit(solution)/shard_map/ppermute | solution.py:304
  598.9 5.4 shard_map.295
  604.3 19.9 %collective-permute-done.42.refs_3_ = bf16[1,64,2048]{2,1,0:T(8,128)(2,1)S(1)} collective-permute-done((bf16[1,64,2048]{2,1,0:T(8,128)(2,1)}, bf16[1,64,2048]{2,1,0:T(8,128)(2,1)S(1)}, u32[]{:S(2)}, u32[]{:S(2)}) %collective-permute-start.42) | collective-permute-done | bytes 262176 | tf_op jit(solution)/shard_map/ppermute | solution.py:304
  625.0 3.0 shard_map.293
  630.0 5.4 shard_map.294
  637.1 5.4 shard_map.292
  644.7 2.9 fusion.6
  (311 shorter events, 131.9 us)
Async XLA Ops:
  7.2 145.3 %all-gather.3.cloned.1.call-start = ((), (), s32[]{:S(2)}) async-start(), calls=%async_computation.4 | async-start | bytes 9437184 | tf_op jit(solution)/shard_map/all_gather | solution.py:877
  19.3 24.3 %collective-permute-start = (bf16[2,64,1920]{2,1,0:T(8,128)(2,1)}, bf16[2,64,1920]{2,1,0:T(8,128)(2,1)S(1)}, u32[]{:S(2)}, u32[]{:S(2)}) collective-permute-start(bf16[2,64,1920]{2,1,0:T(8,128)(2,1)} %get-tuple-element.84), channel_id=1, source_target_pairs={{0,2},{1,3},{2,0},{3,1},{4,6},{5,7},{6,4},{7,5},{8,10},{9,11},{10,... | collective-permute-start | bytes 1474568 | tf_op jit(solution)/shard_map/ppermute | solution.py:304
  22.4 36.3 %collective-permute-start.1 = (bf16[2,64,1920]{2,1,0:T(8,128)(2,1)}, bf16[2,64,1920]{2,1,0:T(8,128)(2,1)S(1)}, u32[]{:S(2)}, u32[]{:S(2)}) collective-permute-start(bf16[2,64,1920]{2,1,0:T(8,128)(2,1)} %get-tuple-element.85), channel_id=1, source_target_pairs={{0,4},{1,5},{2,6},{3,7},{4,0},{5,1},{6,2},{7,3},{8,12},{9,13},{10,... | collective-permute-start | bytes 1474568 | tf_op jit(solution)/shard_map/ppermute | solution.py:304
  25.0 33.7 %collective-permute-start.2 = (bf16[2,64,1920]{2,1,0:T(8,128)(2,1)}, bf16[2,64,1920]{2,1,0:T(8,128)(2,1)S(1)}, u32[]{:S(2)}, u32[]{:S(2)}) collective-permute-start(bf16[2,64,1920]{2,1,0:T(8,128)(2,1)} %get-tuple-element.86), channel_id=1, source_target_pairs={{0,6},{1,7},{2,4},{3,5},{4,2},{5,3},{6,0},{7,1},{8,14},{9,15},{10,... | collective-permute-start | bytes 1474568 | tf_op jit(solution)/shard_map/ppermute | solution.py:304
  58.8 172.7 %all-gather.5.cloned.1.call-start = ((), (), s32[]{:S(2)}) async-start(), calls=%async_computation.5 | async-start | bytes 9437184 | tf_op jit(solution)/shard_map/all_gather | solution.py:879
  65.6 353.0 %reduce-scatter.3.cloned.1.call-start = ((), (), s32[]{:S(2)}) async-start(), calls=%async_computation.6 | async-start | bytes 9437184 | tf_op jit(solution)/shard_map/reduce_scatter | solution.py:938
  77.6 32.7 %collective-permute-start.11 = (bf16[8,64,768]{2,1,0:T(8,128)(2,1)S(1)}, bf16[8,64,768]{2,1,0:T(8,128)(2,1)}, u32[]{:S(2)}, u32[]{:S(2)}) collective-permute-start(bf16[8,64,768]{2,1,0:T(8,128)(2,1)S(1)} %slice.224.refs_0_), channel_id=1, source_target_pairs={{0,16},{8,24},{16,0},{24,8},{1,17},{9,25},{17,1},{25,9},{2,18},{10... | collective-permute-start | bytes 2359304 | tf_op jit(solution)/shard_map/ppermute | solution.py:304
  79.1 50.6 %collective-permute-start.10 = (bf16[8,64,768]{2,1,0:T(8,128)(2,1)S(1)}, bf16[8,64,768]{2,1,0:T(8,128)(2,1)}, u32[]{:S(2)}, u32[]{:S(2)}) collective-permute-start(bf16[8,64,768]{2,1,0:T(8,128)(2,1)S(1)} %slice.224.refs_0_), channel_id=1, source_target_pairs={{0,8},{8,0},{16,24},{24,16},{1,9},{9,1},{17,25},{25,17},{2,10},{10... | collective-permute-start | bytes 2359304 | tf_op jit(solution)/shard_map/ppermute | solution.py:304
  81.8 16.8 %collective-permute-start.4 = (s32[2,2,256]{2,1,0:T(2,128)S(1)}, s32[2,2,256]{2,1,0:T(2,128)S(1)}, u32[]{:S(2)}, u32[]{:S(2)}) collective-permute-start(s32[2,2,256]{2,1,0:T(2,128)S(1)} %bitcast.187), channel_id=1, source_target_pairs={{0,8},{8,0},{16,24},{24,16},{1,9},{9,1},{17,25},{25,17},{2,10},{10... | collective-permute-start | bytes 12296 | tf_op jit(solution)/shard_map/ppermute | solution.py:304
  82.4 17.6 %collective-permute-start.5 = (s32[2,2,256]{2,1,0:T(2,128)S(1)}, s32[2,2,256]{2,1,0:T(2,128)S(1)}, u32[]{:S(2)}, u32[]{:S(2)}) collective-permute-start(s32[2,2,256]{2,1,0:T(2,128)S(1)} %bitcast.186), channel_id=1, source_target_pairs={{0,16},{8,24},{16,0},{24,8},{1,17},{9,25},{17,1},{25,9},{2,18},{10... | collective-permute-start | bytes 12296 | tf_op jit(solution)/shard_map/ppermute | solution.py:304
  83.0 17.5 %collective-permute-start.6 = (s32[2,2,256]{2,1,0:T(2,128)S(1)}, s32[2,2,256]{2,1,0:T(2,128)S(1)}, u32[]{:S(2)}, u32[]{:S(2)}) collective-permute-start(s32[2,2,256]{2,1,0:T(2,128)S(1)} %bitcast.185), channel_id=1, source_target_pairs={{0,24},{8,16},{16,8},{24,0},{1,25},{9,17},{17,9},{25,1},{2,26},{10... | collective-permute-start | bytes 12296 | tf_op jit(solution)/shard_map/ppermute | solution.py:304
  98.6 26.2 %collective-permute-start.7 = (bf16[8,64,1024]{2,1,0:T(8,128)(2,1)S(1)}, bf16[8,64,1024]{2,1,0:T(8,128)(2,1)}, u32[]{:S(2)}, u32[]{:S(2)}) collective-permute-start(bf16[8,64,1024]{2,1,0:T(8,128)(2,1)S(1)} %slice.223.refs_0_), channel_id=1, source_target_pairs={{0,8},{8,0},{16,24},{24,16},{1,9},{9,1},{17,25},{25,17},{2,10},{10... | collective-permute-start | bytes 3145736 | tf_op jit(solution)/shard_map/ppermute | solution.py:304
  100.0 44.4 %collective-permute-start.8 = (bf16[8,64,1024]{2,1,0:T(8,128)(2,1)S(1)}, bf16[8,64,1024]{2,1,0:T(8,128)(2,1)}, u32[]{:S(2)}, u32[]{:S(2)}) collective-permute-start(bf16[8,64,1024]{2,1,0:T(8,128)(2,1)S(1)} %slice.223.refs_0_), channel_id=1, source_target_pairs={{0,16},{8,24},{16,0},{24,8},{1,17},{9,25},{17,1},{25,9},{2,18},{10... | collective-permute-start | bytes 3145736 | tf_op jit(solution)/shard_map/ppermute | solution.py:304
  110.3 29.1 %collective-permute-start.12 = (bf16[8,64,768]{2,1,0:T(8,128)(2,1)}, bf16[8,64,768]{2,1,0:T(8,128)(2,1)S(1)}, u32[]{:S(2)}, u32[]{:S(2)}) collective-permute-start(bf16[8,64,768]{2,1,0:T(8,128)(2,1)} %collective-permute-done.11.refs_2_), channel_id=1, source_target_pairs={{0,8},{8,0},{16,24},{24,16},{1,9},{9,1},{17,25},{25,17},{2,10},{10... | collective-permute-start | bytes 2359304 | tf_op jit(solution)/shard_map/ppermute | solution.py:304
  124.8 21.4 %collective-permute-start.9 = (bf16[8,64,1024]{2,1,0:T(8,128)(2,1)}, bf16[8,64,1024]{2,1,0:T(8,128)(2,1)S(1)}, u32[]{:S(2)}, u32[]{:S(2)}) collective-permute-start(bf16[8,64,1024]{2,1,0:T(8,128)(2,1)} %collective-permute-done.7.refs_1_), channel_id=1, source_target_pairs={{0,16},{8,24},{16,0},{24,8},{1,17},{9,25},{17,1},{25,9},{2,18},{10... | collective-permute-start | bytes 3145736 | tf_op jit(solution)/shard_map/ppermute | solution.py:304
  173.7 23.2 %collective-permute-start.15 = (bf16[2,256,768]{2,1,0:T(8,128)(2,1)}, bf16[2,256,768]{2,1,0:T(8,128)(2,1)S(1)}, u32[]{:S(2)}, u32[]{:S(2)}) collective-permute-start(bf16[2,256,768]{2,1,0:T(8,128)(2,1)} %get-tuple-element.158), channel_id=1, source_target_pairs={{0,24},{8,16},{16,8},{24,0},{1,25},{9,17},{17,9},{25,1},{2,26},{10... | collective-permute-start | bytes 2359304 | tf_op jit(solution)/shard_map/ppermute | solution.py:304
  174.7 33.5 %collective-permute-start.14 = (bf16[2,256,768]{2,1,0:T(8,128)(2,1)}, bf16[2,256,768]{2,1,0:T(8,128)(2,1)S(1)}, u32[]{:S(2)}, u32[]{:S(2)}) collective-permute-start(bf16[2,256,768]{2,1,0:T(8,128)(2,1)} %get-tuple-element.159), channel_id=1, source_target_pairs={{0,16},{8,24},{16,0},{24,8},{1,17},{9,25},{17,1},{25,9},{2,18},{10... | collective-permute-start | bytes 2359304 | tf_op jit(solution)/shard_map/ppermute | solution.py:304
  176.6 31.7 %collective-permute-start.13 = (bf16[2,256,768]{2,1,0:T(8,128)(2,1)}, bf16[2,256,768]{2,1,0:T(8,128)(2,1)S(1)}, u32[]{:S(2)}, u32[]{:S(2)}) collective-permute-start(bf16[2,256,768]{2,1,0:T(8,128)(2,1)} %get-tuple-element.160), channel_id=1, source_target_pairs={{0,8},{8,0},{16,24},{24,16},{1,9},{9,1},{17,25},{25,17},{2,10},{10... | collective-permute-start | bytes 2359304 | tf_op jit(solution)/shard_map/ppermute | solution.py:304
  217.7 19.8 %collective-permute-start.16 = (bf16[2,256,256]{2,1,0:T(8,128)(2,1)}, bf16[2,256,256]{2,1,0:T(8,128)(2,1)S(1)}, u32[]{:S(2)}, u32[]{:S(2)}) collective-permute-start(bf16[2,256,256]{2,1,0:T(8,128)(2,1)} %get-tuple-element.98), channel_id=1, source_target_pairs={{0,8},{8,0},{16,24},{24,16},{1,9},{9,1},{17,25},{25,17},{2,10},{10... | collective-permute-start | bytes 786440 | tf_op jit(solution)/shard_map/ppermute | solution.py:304
  219.3 18.3 %collective-permute-start.17 = (bf16[2,256,256]{2,1,0:T(8,128)(2,1)}, bf16[2,256,256]{2,1,0:T(8,128)(2,1)S(1)}, u32[]{:S(2)}, u32[]{:S(2)}) collective-permute-start(bf16[2,256,256]{2,1,0:T(8,128)(2,1)} %get-tuple-element.99), channel_id=1, source_target_pairs={{0,16},{8,24},{16,0},{24,8},{1,17},{9,25},{17,1},{25,9},{2,18},{10... | collective-permute-start | bytes 786440 | tf_op jit(solution)/shard_map/ppermute | solution.py:304
  220.1 17.5 %collective-permute-start.18 = (bf16[2,256,256]{2,1,0:T(8,128)(2,1)}, bf16[2,256,256]{2,1,0:T(8,128)(2,1)S(1)}, u32[]{:S(2)}, u32[]{:S(2)}) collective-permute-start(bf16[2,256,256]{2,1,0:T(8,128)(2,1)} %get-tuple-element.100), channel_id=1, source_target_pairs={{0,24},{8,16},{16,8},{24,0},{1,25},{9,17},{17,9},{25,1},{2,26},{10... | collective-permute-start | bytes 786440 | tf_op jit(solution)/shard_map/ppermute | solution.py:304
  257.9 384.7 %reduce-scatter.5.cloned.1.call-start = ((), (), s32[]{:S(2)}) async-start(), calls=%async_computation.7 | async-start | bytes 9437184 | tf_op jit(solution)/shard_map/reduce_scatter | solution.py:994
  289.0 54.2 %collective-permute-start.22 = (bf16[2,256,768]{2,1,0:T(8,128)(2,1)}, bf16[2,256,768]{2,1,0:T(8,128)(2,1)S(1)}, u32[]{:S(2)}, u32[]{:S(2)}) collective-permute-start(bf16[2,256,768]{2,1,0:T(8,128)(2,1)} %get-tuple-element.110), channel_id=1, source_target_pairs={{0,8},{8,0},{16,24},{24,16},{1,9},{9,1},{17,25},{25,17},{2,10},{10... | collective-permute-start | bytes 2359304 | tf_op jit(solution)/shard_map/ppermute | solution.py:304
  290.6 52.6 %collective-permute-start.23 = (bf16[2,256,768]{2,1,0:T(8,128)(2,1)}, bf16[2,256,768]{2,1,0:T(8,128)(2,1)S(1)}, u32[]{:S(2)}, u32[]{:S(2)}) collective-permute-start(bf16[2,256,768]{2,1,0:T(8,128)(2,1)} %get-tuple-element.111), channel_id=1, source_target_pairs={{0,16},{8,24},{16,0},{24,8},{1,17},{9,25},{17,1},{25,9},{2,18},{10... | collective-permute-start | bytes 2359304 | tf_op jit(solution)/shard_map/ppermute | solution.py:304
  291.3 52.0 %collective-permute-start.24 = (bf16[2,256,768]{2,1,0:T(8,128)(2,1)}, bf16[2,256,768]{2,1,0:T(8,128)(2,1)S(1)}, u32[]{:S(2)}, u32[]{:S(2)}) collective-permute-start(bf16[2,256,768]{2,1,0:T(8,128)(2,1)} %get-tuple-element.112), channel_id=1, source_target_pairs={{0,24},{8,16},{16,8},{24,0},{1,25},{9,17},{17,9},{25,1},{2,26},{10... | collective-permute-start | bytes 2359304 | tf_op jit(solution)/shard_map/ppermute | solution.py:304
  309.7 98.6 %collective-permute-start.27 = (bf16[1,2,256,2048]{3,2,1,0:T(8,128)(2,1)}, bf16[1,2,256,2048]{3,2,1,0:T(8,128)(2,1)}, u32[]{:S(2)}, u32[]{:S(2)}) collective-permute-start(bf16[1,2,256,2048]{3,2,1,0:T(8,128)(2,1)} %bitcast.192), channel_id=1, source_target_pairs={{0,8},{8,0},{16,24},{24,16},{1,9},{9,1},{17,25},{25,17},{2,10},{10... | collective-permute-start | bytes 6291464 | tf_op jit(solution)/shard_map/ppermute | solution.py:304
  341.2 71.0 %collective-permute-start.26 = (bf16[8,2,64,1024]{3,2,1,0:T(8,128)(2,1)}, bf16[8,2,64,1024]{3,2,1,0:T(8,128)(2,1)}, u32[]{:S(2)}, u32[]{:S(2)}) collective-permute-start(bf16[8,2,64,1024]{3,2,1,0:T(8,128)(2,1)} %get-tuple-element.118), channel_id=1, source_target_pairs={{0,16},{8,24},{16,0},{24,8},{1,17},{9,25},{17,1},{25,9},{2,18},{10... | collective-permute-start | bytes 6291464 | tf_op jit(solution)/shard_map/ppermute | solution.py:304
  361.9 53.9 %collective-permute-start.25 = (bf16[8,2,64,768]{3,2,1,0:T(8,128)(2,1)}, bf16[8,2,64,768]{3,2,1,0:T(8,128)(2,1)}, u32[]{:S(2)}, u32[]{:S(2)}) collective-permute-start(bf16[8,2,64,768]{3,2,1,0:T(8,128)(2,1)} %get-tuple-element.120), channel_id=1, source_target_pairs={{0,8},{8,0},{16,24},{24,16},{1,9},{9,1},{17,25},{25,17},{2,10},{10... | collective-permute-start | bytes 4718600 | tf_op jit(solution)/shard_map/ppermute | solution.py:304
  398.4 17.4 %collective-permute-start.30 = (f32[8,3072]{1,0:T(8,128)S(1)}, f32[8,3072]{1,0:T(8,128)S(1)}, u32[]{:S(2)}, u32[]{:S(2)}) collective-permute-start(f32[8,3072]{1,0:T(8,128)S(1)} %add.314), channel_id=1, source_target_pairs={{0,4},{1,5},{2,6},{3,7},{4,0},{5,1},{6,2},{7,3},{8,12},{9,13},{10,... | collective-permute-start | bytes 294920 | tf_op jit(solution)/shard_map/ppermute | solution.py:304
  419.9 33.9 %collective-permute-start.34 = (bf16[8,64,1024]{2,1,0:T(8,128)(2,1)S(1)}, bf16[8,64,1024]{2,1,0:T(8,128)(2,1)S(1)}, u32[]{:S(2)}, u32[]{:S(2)}) collective-permute-start(bf16[8,64,1024]{2,1,0:T(8,128)(2,1)S(1)} %copy-done.40), channel_id=1, source_target_pairs={{0,8},{8,0},{16,24},{24,16},{1,9},{9,1},{17,25},{25,17},{2,10},{10... | collective-permute-start | bytes 3145736 | tf_op jit(solution)/shard_map/ppermute | solution.py:304
  420.3 30.6 %collective-permute-start.35 = (bf16[1,2,64,2048]{3,2,1,0:T(8,128)(2,1)S(1)}, bf16[1,2,64,2048]{3,2,1,0:T(8,128)(2,1)S(1)}, u32[]{:S(2)}, u32[]{:S(2)}) collective-permute-start(bf16[1,2,64,2048]{3,2,1,0:T(8,128)(2,1)S(1)} %copy-done.41), channel_id=1, source_target_pairs={{0,16},{8,24},{16,0},{24,8},{1,17},{9,25},{17,1},{25,9},{2,18},{10... | collective-permute-start | bytes 1572872 | tf_op jit(solution)/shard_map/ppermute | solution.py:304
  421.6 24.6 %collective-permute-start.31 = (f32[8,3072]{1,0:T(8,128)S(1)}, f32[8,3072]{1,0:T(8,128)S(1)}, u32[]{:S(2)}, u32[]{:S(2)}) collective-permute-start(f32[8,3072]{1,0:T(8,128)S(1)} %add.316), channel_id=1, source_target_pairs={{0,8},{8,0},{16,24},{24,16},{1,9},{9,1},{17,25},{25,17},{2,10},{10... | collective-permute-start | bytes 294920 | tf_op jit(solution)/shard_map/ppermute | solution.py:304
  455.2 47.3 %all-to-all-start = ((bf16[8,64,1024]{2,1,0:T(8,128)(2,1)}), bf16[8,64,1024]{2,1,0:T(8,128)(2,1)S(1)}, u32[]{:S(2)}, u32[]{:S(2)}) async-start(bf16[8,64,1024]{2,1,0:T(8,128)(2,1)} %add_convert_fusion.1), calls=%async_computation.2 | async-start | bytes 2097152 | tf_op jit(solution)/shard_map/all_to_all | solution.py:1008
  458.8 20.6 %collective-permute-start.33 = (bf16[8,64,768]{2,1,0:T(8,128)(2,1)}, bf16[8,64,768]{2,1,0:T(8,128)(2,1)S(1)}, u32[]{:S(2)}, u32[]{:S(2)}) collective-permute-start(bf16[8,64,768]{2,1,0:T(8,128)(2,1)} %get-tuple-element.135), channel_id=1, source_target_pairs={{0,16},{8,24},{16,0},{24,8},{1,17},{9,25},{17,1},{25,9},{2,18},{10... | collective-permute-start | bytes 2359304 | tf_op jit(solution)/shard_map/ppermute | solution.py:304
  459.4 47.3 %collective-permute-start.46 = (bf16[1,256,2048]{2,1,0:T(8,128)(2,1)}, bf16[1,256,2048]{2,1,0:T(8,128)(2,1)S(1)}, u32[]{:S(2)}, u32[]{:S(2)}) collective-permute-start(bf16[1,256,2048]{2,1,0:T(8,128)(2,1)} %get-tuple-element.131), channel_id=1, source_target_pairs={{0,16},{8,24},{16,0},{24,8},{1,17},{9,25},{17,1},{25,9},{2,18},{10... | collective-permute-start | bytes 3145736 | tf_op jit(solution)/shard_map/ppermute | solution.py:304
  502.5 35.1 %all-to-all-start.1 = ((bf16[8,64,768]{2,1,0:T(8,128)(2,1)}), bf16[8,64,768]{2,1,0:T(8,128)(2,1)}, u32[]{:S(2)}, u32[]{:S(2)}) async-start(bf16[8,64,768]{2,1,0:T(8,128)(2,1)} %add_convert_fusion.2), calls=%async_computation.3 | async-start | bytes 1572864 | tf_op jit(solution)/shard_map/all_to_all | solution.py:1012
  509.7 28.9 %collective-permute-start.48 = (bf16[1,256,2048]{2,1,0:T(8,128)(2,1)S(1)}, bf16[1,256,2048]{2,1,0:T(8,128)(2,1)}, u32[]{:S(2)}, u32[]{:S(2)}) collective-permute-start(bf16[1,256,2048]{2,1,0:T(8,128)(2,1)S(1)} %add_convert_fusion.refs_0_), channel_id=1, source_target_pairs={{0,16},{8,24},{16,0},{24,8},{1,17},{9,25},{17,1},{25,9},{2,18},{10... | collective-permute-start | bytes 3145736 | tf_op jit(solution)/shard_map/ppermute | solution.py:304
  511.5 63.0 %collective-permute-start.47 = (bf16[1,256,2048]{2,1,0:T(8,128)(2,1)S(1)}, bf16[1,256,2048]{2,1,0:T(8,128)(2,1)}, u32[]{:S(2)}, u32[]{:S(2)}) collective-permute-start(bf16[1,256,2048]{2,1,0:T(8,128)(2,1)S(1)} %add_convert_fusion.refs_0_), channel_id=1, source_target_pairs={{0,8},{8,0},{16,24},{24,16},{1,9},{9,1},{17,25},{25,17},{2,10},{10... | collective-permute-start | bytes 3145736 | tf_op jit(solution)/shard_map/ppermute | solution.py:304
  519.5 53.3 %collective-permute-start.43 = (bf16[8,64,1024]{2,1,0:T(8,128)(2,1)S(1)}, bf16[8,64,1024]{2,1,0:T(8,128)(2,1)}, u32[]{:S(2)}, u32[]{:S(2)}) collective-permute-start(bf16[8,64,1024]{2,1,0:T(8,128)(2,1)S(1)} %all-to-all-done.refs_0_), channel_id=1, source_target_pairs={{0,8},{8,0},{16,24},{24,16},{1,9},{9,1},{17,25},{25,17},{2,10},{10... | collective-permute-start | bytes 3145736 | tf_op jit(solution)/shard_map/ppermute | solution.py:304
  521.7 47.7 %collective-permute-start.40 = (bf16[1,64,2048]{2,1,0:T(8,128)(2,1)S(1)}, bf16[1,64,2048]{2,1,0:T(8,128)(2,1)}, u32[]{:S(2)}, u32[]{:S(2)}) collective-permute-start(bf16[1,64,2048]{2,1,0:T(8,128)(2,1)S(1)} %add_convert_fusion.3.refs_0_), channel_id=1, source_target_pairs={{0,8},{8,0},{16,24},{24,16},{1,9},{9,1},{17,25},{25,17},{2,10},{10... | collective-permute-start | bytes 786440 | tf_op jit(solution)/shard_map/ppermute | solution.py:304
  537.6 37.8 %collective-permute-start.37 = (bf16[8,64,768]{2,1,0:T(8,128)(2,1)}, bf16[8,64,768]{2,1,0:T(8,128)(2,1)}, u32[]{:S(2)}, u32[]{:S(2)}) collective-permute-start(bf16[8,64,768]{2,1,0:T(8,128)(2,1)} %all-to-all-done.1.refs_0_), channel_id=1, source_target_pairs={{0,16},{8,24},{16,0},{24,8},{1,17},{9,25},{17,1},{25,9},{2,18},{10... | collective-permute-start | bytes 2359304 | tf_op jit(solution)/shard_map/ppermute | solution.py:304
  538.7 33.3 %collective-permute-start.41 = (bf16[1,64,2048]{2,1,0:T(8,128)(2,1)S(1)}, bf16[1,64,2048]{2,1,0:T(8,128)(2,1)}, u32[]{:S(2)}, u32[]{:S(2)}) collective-permute-start(bf16[1,64,2048]{2,1,0:T(8,128)(2,1)S(1)} %add_convert_fusion.3.refs_0_), channel_id=1, source_target_pairs={{0,16},{8,24},{16,0},{24,8},{1,17},{9,25},{17,1},{25,9},{2,18},{10... | collective-permute-start | bytes 786440 | tf_op jit(solution)/shard_map/ppermute | solution.py:304
  569.4 26.4 %collective-permute-start.49 = (bf16[1,256,2048]{2,1,0:T(8,128)(2,1)}, bf16[1,256,2048]{2,1,0:T(8,128)(2,1)}, u32[]{:S(2)}, u32[]{:S(2)}) collective-permute-start(bf16[1,256,2048]{2,1,0:T(8,128)(2,1)} %collective-permute-done.48.refs_2_), channel_id=1, source_target_pairs={{0,8},{8,0},{16,24},{24,16},{1,9},{9,1},{17,25},{25,17},{2,10},{10... | collective-permute-start | bytes 3145736 | tf_op jit(solution)/shard_map/ppermute | solution.py:304
  572.0 56.0 %collective-permute-start.44 = (bf16[8,64,1024]{2,1,0:T(8,128)(2,1)S(1)}, bf16[8,64,1024]{2,1,0:T(8,128)(2,1)S(1)}, u32[]{:S(2)}, u32[]{:S(2)}) collective-permute-start(bf16[8,64,1024]{2,1,0:T(8,128)(2,1)S(1)} %all-to-all-done.refs_0_), channel_id=1, source_target_pairs={{0,16},{8,24},{16,0},{24,8},{1,17},{9,25},{17,1},{25,9},{2,18},{10... | collective-permute-start | bytes 3145736 | tf_op jit(solution)/shard_map/ppermute | solution.py:304
  572.8 55.3 %collective-permute-start.45 = (bf16[8,64,1024]{2,1,0:T(8,128)(2,1)}, bf16[8,64,1024]{2,1,0:T(8,128)(2,1)S(1)}, u32[]{:S(2)}, u32[]{:S(2)}) collective-permute-start(bf16[8,64,1024]{2,1,0:T(8,128)(2,1)} %collective-permute-done.43.refs_1_), channel_id=1, source_target_pairs={{0,16},{8,24},{16,0},{24,8},{1,17},{9,25},{17,1},{25,9},{2,18},{10... | collective-permute-start | bytes 3145736 | tf_op jit(solution)/shard_map/ppermute | solution.py:304
  574.5 60.9 %collective-permute-start.36 = (bf16[8,64,768]{2,1,0:T(8,128)(2,1)}, bf16[8,64,768]{2,1,0:T(8,128)(2,1)S(1)}, u32[]{:S(2)}, u32[]{:S(2)}) collective-permute-start(bf16[8,64,768]{2,1,0:T(8,128)(2,1)} %all-to-all-done.1.refs_0_), channel_id=1, source_target_pairs={{0,8},{8,0},{16,24},{24,16},{1,9},{9,1},{17,25},{25,17},{2,10},{10... | collective-permute-start | bytes 2359304 | tf_op jit(solution)/shard_map/ppermute | solution.py:304
  575.5 59.9 %collective-permute-start.38 = (bf16[8,64,768]{2,1,0:T(8,128)(2,1)}, bf16[8,64,768]{2,1,0:T(8,128)(2,1)S(1)}, u32[]{:S(2)}, u32[]{:S(2)}) collective-permute-start(bf16[8,64,768]{2,1,0:T(8,128)(2,1)} %collective-permute-done.37.refs_2_), channel_id=1, source_target_pairs={{0,8},{8,0},{16,24},{24,16},{1,9},{9,1},{17,25},{25,17},{2,10},{10... | collective-permute-start | bytes 2359304 | tf_op jit(solution)/shard_map/ppermute | solution.py:304
  595.8 28.5 %collective-permute-start.42 = (bf16[1,64,2048]{2,1,0:T(8,128)(2,1)}, bf16[1,64,2048]{2,1,0:T(8,128)(2,1)S(1)}, u32[]{:S(2)}, u32[]{:S(2)}) collective-permute-start(bf16[1,64,2048]{2,1,0:T(8,128)(2,1)} %collective-permute-done.40.refs_1_), channel_id=1, source_target_pairs={{0,16},{8,24},{16,0},{24,8},{1,17},{9,25},{17,1},{25,9},{2,18},{10... | collective-permute-start | bytes 786440 | tf_op jit(solution)/shard_map/ppermute | solution.py:304
  (51 other events, 684.1 us)
Sparse Core Ops, SparseCore 0:
  58.9 90.3 all-gather.2
  150.9 80.5 all-gather.4
  258.0 91.3 reduce-scatter.2
  418.8 114.1 reduce-scatter.4

commit v3 on v2

--- a/solution.py
+++ b/solution.py
@@ -351,6 +351,7 @@
 
     return pl.pallas_call(
         body,
+        name="place",
         out_shape=jax.ShapeDtypeStruct((count,) + pieces[0].shape[1:], pieces[0].dtype),
         in_specs=[SCALARS] + [ANY] * len(pieces),
         out_specs=ANY,
@@ -409,6 +410,7 @@
 
     return pl.pallas_call(
         body,
+        name="cut_weights",
         out_shape=[jax.ShapeDtypeStruct((2, part, cols + LANES), low)] * 4,
         in_specs=[SCALARS, ANY, ANY, ANY],
         out_specs=[ANY] * 4,
@@ -422,17 +424,17 @@
     )(places, qkv_weight, fc_in_weight, extra)
 
 
-def finish(pieces, rows_at, cols_at, shape, thirds=1):
-    sizes = [p.shape[0] for p in pieces]
-    total = sum(sizes)
+def finish(pieces, rows_at, cols_at, shape, thirds=1, chosen=None):
+    begin, size = chosen or (0, pieces[0].shape[0])
+    total = size * len(pieces)
     rows, cols = pieces[0].shape[1:]
     span = cols // thirds
 
     def body(rows_ref, cols_ref, *refs):
         out, narrow, full, sems_in, sems_out = refs[-5:]
         copies = []
-        for ref, size in zip(refs, sizes):
-            for i in range(size):
+        for ref in refs[: len(pieces)]:
+            for i in range(begin, begin + size):
                 n = len(copies)
                 copies.append(pltpu.make_async_copy(ref.at[i], narrow.at[n], sems_in.at[n]))
                 copies[n].start()
@@ -455,6 +457,7 @@
 
     return pl.pallas_call(
         body,
+        name="finish",
         out_shape=jax.ShapeDtypeStruct(shape, wide),
         in_specs=[SCALARS, SCALARS] + [ANY] * len(pieces),
         out_specs=ANY,
@@ -519,6 +522,7 @@
     row = lambda n: pl.BlockSpec((block, n), lambda i: (i, 0))
     return pl.pallas_call(
         body,
+        name="project",
         grid=(group // block,),
         in_specs=[row(width), WHOLE, WHOLE, WHOLE, row(LANES), row(LANES), row(LANES)],
         out_specs=[row(width), row(width), row(cols)],
@@ -546,6 +550,7 @@
     row = lambda n: pl.BlockSpec((block, n), lambda i: (i, 0))
     return pl.pallas_call(
         body,
+        name="expand",
         grid=(group // block,),
         in_specs=[row(width), WHOLE, WHOLE],
         out_specs=[row(cols), row(cols)],
@@ -555,23 +560,27 @@
     )(second, weight, bias)
 
 
-def contract(o_back, active, dense_weight, fc_out_weight, block):
-    group = active.shape[0]
-    width = fc_out_weight.shape[1]
-
-    def body(o_ref, a_ref, w1_ref, w2_ref, out_ref):
-        out_ref[...] = (dot(o_ref[...], w1_ref[...]) + dot(a_ref[...], w2_ref[...])).astype(low)
+def contract(left, weight, block, more=None):
+    group = left.shape[0]
+    width = weight.shape[1]
+
+    def body(left_ref, weight_ref, *refs):
+        total = dot(left_ref[...], weight_ref[...])
+        if more is not None:
+            total = total + refs[0][...].astype(wide)
+        refs[-1][...] = total.astype(low)
 
     row = lambda n: pl.BlockSpec((block, n), lambda i: (i, 0))
     return pl.pallas_call(
         body,
+        name="contract",
         grid=(group // block,),
-        in_specs=[row(o_back.shape[1]), row(active.shape[1]), WHOLE, WHOLE],
+        in_specs=[row(left.shape[1]), WHOLE] + ([] if more is None else [row(width)]),
         out_specs=row(width),
         out_shape=jax.ShapeDtypeStruct((group, width), low),
         compiler_params=FAST,
         cost_estimate=SMALL,
-    )(o_back, active, dense_weight, fc_out_weight)
+    )(left, weight, *(() if more is None else (more,)))
 
 
 def hidden_back(g_all, fc_out_weight, slope, block):
@@ -590,6 +599,7 @@
     row = lambda n: pl.BlockSpec((block, n), lambda i: (i, 0))
     return pl.pallas_call(
         body,
+        name="hidden_back",
         grid=(group // block,),
         in_specs=[row(width), WHOLE, row(units)],
         out_specs=[row(units), pl.BlockSpec((1, units), lambda i: (0, 0))],
@@ -618,6 +628,7 @@
     out = pl.BlockSpec((1, parts, size, cols), lambda i, k, s: (i, 0, 0, 0))
     return pl.pallas_call(
         body,
+        name="grad_pair",
         grid_spec=pltpu.PrefetchScalarGridSpec(
             num_scalar_prefetch=2,
             grid=(n,),
@@ -646,6 +657,7 @@
     out = pl.BlockSpec((n // 2 if n > 1 else 1, rows, cols), lambda i: (i, 0, 0))
     return pl.pallas_call(
         body,
+        name="add_split",
         grid=(2 if n > 1 else 1,),
         in_specs=[SCALARS, both, both],
         out_specs=[out, out],
@@ -653,6 +665,29 @@
         compiler_params=FAST,
         cost_estimate=SMALL,
     )(bit[None].astype(jnp.int32), kept, got)
+
+
+def add_split_two(kept, got, other_kept, other_got, bit):
+    n, _, rows, cols = kept.shape
+    more = other_kept.shape[3] // cols
+
+    def body(bit_ref, a_ref, b_ref, c_ref, d_ref, keep_out, send_out):
+        for out, half in ((keep_out, bit_ref[0]), (send_out, 1 - bit_ref[0])):
+            out[:n] = (a_ref[:, half].astype(wide) + b_ref[:, half].astype(wide)).astype(low)
+            other = (c_ref[0, half].astype(wide) + d_ref[0, half].astype(wide)).astype(low)
+            for i in range(more):
+                out[n + i] = other[:, i * cols : (i + 1) * cols]
+
+    shape = jax.ShapeDtypeStruct((n + more, rows, cols), low)
+    return pl.pallas_call(
+        body,
+        name="add_split_two",
+        in_specs=[SCALARS] + [WHOLE] * 4,
+        out_specs=[WHOLE] * 2,
+        out_shape=[shape, shape],
+        compiler_params=FAST,
+        cost_estimate=SMALL,
+    )(bit[None].astype(jnp.int32), kept, got, other_kept, other_got)
 
 
 def fetch(places_ref, sources, target, sems, block, sequences):
@@ -710,6 +745,7 @@
 
     return pl.pallas_call(
         body,
+        name="attend",
         out_shape=[jax.ShapeDtypeStruct((sequences, block, hd), low)] * count,
         in_specs=[SCALARS, WHOLE, WHOLE] + [ANY] * count,
         out_specs=[ANY] * count,
@@ -771,6 +807,7 @@
 
     return pl.pallas_call(
         body,
+        name="attend_back",
         out_shape=[jax.ShapeDtypeStruct((sequences, block, cols), low)] * count,
         in_specs=[SCALARS] + [WHOLE] * 5 + [ANY] * (2 * count),
         out_specs=[ANY] * count,
@@ -809,6 +846,7 @@
     row = lambda n: pl.BlockSpec((block, n), lambda i: (i, 0))
     return pl.pallas_call(
         body,
+        name="norm_back",
         grid=(group // block,),
         in_specs=[row(width), row(d_packed.shape[1]), row(d_hidden.shape[1])] + [WHOLE] * 3,
         out_specs=[row(width), pl.BlockSpec((4, width), lambda i: (0, 0))],
@@ -929,23 +967,27 @@
     active, slope = expand(
         then(second, packed), w_in, fc_in_bias.astype(wide).reshape(1, -1), block
     )
-    o = attend([then(p, active) for p in parts], plane, seg_row, seg_col, hd)
+    mlp = contract(active, fc_out_weight, block)
+    o = attend([then(p, mlp) for p in parts], plane, seg_row, seg_col, hd)
     o_back = to_group(o)
     x_bit, y_bit = me_c % 2, me_c // 2
     d_o = dot(then(g_all, *o), dense_weight, 1, 1).astype(low)
     d_parts = to_sequences(d_o)
-    partial = contract(then(o_back, d_o), active, dense_weight, fc_out_weight, block)
-    summed = lax.psum_scatter(partial, "fsdp", scatter_dimension=0, tiled=True)
+    partial = contract(then(o_back, d_o), dense_weight, block, mlp)
+    dense_kept, dense_sent = grad_pair(o_back, then(g_all, partial), [y_bit], [1 - y_bit], 2)
+    dense_got = swap(dense_sent, "ctx", 2)
     d_qkv = attend_back(
-        parts, [then(p, partial) for p in d_parts], plane, seg_row, seg_col, seq_tables, hd
+        parts, [then(p, dense_sent) for p in d_parts], plane, seg_row, seg_col, seq_tables, hd
     )
     d_packed = to_group(d_qkv)
+    summed = lax.psum_scatter(then(partial, *d_qkv), "fsdp", scatter_dimension=0, tiled=True)
 
     rows_of = units // (nc * LANES)
     blocks = [((2 * y) * rows_of, s) for y in range(2) for s in range(rows_of)]
+    d_hidden, hidden_sum = hidden_back(then(g_all, *d_qkv), fc_out_weight, slope, block)
     out_kept, out_sent = grad_pair(
         active,
-        then(g_all, *d_qkv),
+        then(g_all, d_hidden),
         [b + x_bit * rows_of + s for b, s in blocks],
         [b + (1 - x_bit) * rows_of + s for b, s in blocks],
         1,
@@ -953,17 +995,14 @@
     out_shape = (1, 2, rows_of * LANES, width)
     out_got = swap(out_sent.reshape(out_shape), "ctx", 1)
     out_kept = out_kept.reshape(out_shape)
-    d_hidden, hidden_sum = hidden_back(then(g_all, out_sent), fc_out_weight, slope, block)
-    by_bit = lambda bit: ([2 * f + bit for f in range(nf)], [2 * f + 1 - bit for f in range(nf)])
-    in_kept, in_sent = grad_pair(second, d_hidden, *by_bit(y_bit), 2)
+    by_y = [2 * f + y_bit for f in range(nf)], [2 * f + 1 - y_bit for f in range(nf)]
+    in_kept, in_sent = grad_pair(second, then(d_hidden, out_sent), *by_y, 2)
     in_got = swap(in_sent, "ctx", 2)
-    qkv_kept, qkv_sent = grad_pair(first, then(d_packed, in_sent), *by_bit(x_bit), 2)
+    to_x = [2 * f + x_bit for f in range(nf)], [2 * f + 1 - x_bit for f in range(nf)]
+    qkv_kept, qkv_sent = grad_pair(first, then(d_packed, in_sent), *to_x, 2)
     qkv_got = swap(qkv_sent, "ctx", 1)
     d_partial, sums = norm_back(
         then(x_all, qkv_sent), d_packed, d_hidden, w_qkv, w_in, norms, block
-    )
-    dense_kept, dense_sent = grad_pair(
-        o_back, then(g_all, d_partial), [y_bit], [1 - y_bit], 2
     )
     def spread_out(values, parts):
         whole = jnp.zeros((parts, nf, values.shape[0] // parts), wide)
@@ -980,61 +1019,55 @@
         ],
         axis=1,
     )
-    total_1 = swap(totals, "fsdp", 1)
-    out_kept, out_sent = add_split(out_kept, then(out_got, dense_sent, total_1), y_bit)
-    out_got = swap(out_sent, "ctx", 2)
-    totals = totals + total_1
-    total_2 = swap(totals, "fsdp", 2)
-    in_kept, in_sent = add_split(in_kept, then(in_got, out_sent, total_2), x_bit)
-    in_got = swap(in_sent, "ctx", 1)
-    totals = totals + total_2
-    total_3 = swap(totals, "fsdp", 4)
-    qkv_kept, qkv_sent = add_split(qkv_kept, then(qkv_got, in_sent, total_3), y_bit)
-    qkv_got = swap(qkv_sent, "ctx", 2)
+    rows_kept, rows_sent = add_split(out_kept, then(out_got, d_partial), y_bit)
+    rows_got = swap(rows_sent, "ctx", 2)
+    both_kept, both_sent = add_split_two(
+        in_kept, then(in_got, rows_sent), dense_kept, dense_got, x_bit
+    )
+    both_got = swap(both_sent, "ctx", 1)
+    qkv_kept2, qkv_sent2 = add_split(qkv_kept, then(qkv_got, both_sent), y_bit)
+    qkv_got2 = swap(qkv_sent2, "ctx", 2)
     d_normal = lax.psum_scatter(
-        then(d_partial, summed, qkv_sent), "fsdp", scatter_dimension=0, tiled=True
-    ).astype(wide)
-    totals = totals + total_3
-    total_4 = swap(totals, "ctx", 1)
-    dense_got = swap(then(dense_sent, qkv_sent), "ctx", 2)
-    out_mine = added(out_kept, then(out_got, qkv_sent, total_4))
-    out_x, out_y = swap(out_mine, "ctx", 1), swap(out_mine, "ctx", 2)
-    totals = totals + total_4
-    total_5 = swap(totals, "ctx", 2)
-    dense_kept, dense_sent = add_split(dense_kept, then(dense_got, qkv_sent, total_5), x_bit)
-    totals = totals + total_5
-    dense_got = swap(dense_sent, "ctx", 1)
-    in_mine = added(in_kept, then(in_got, dense_sent))
-    in_rows = lax.all_to_all(in_mine, "fsdp", 0, 0, tiled=True)
-    qkv_mine = added(qkv_kept, then(qkv_got, in_got))
-    dense_mine = added(dense_kept, then(dense_got, qkv_got))
-    out_xy = swap(then(out_y, dense_got), "ctx", 1)
-    qkv_rows = lax.all_to_all(then(qkv_mine, in_rows), "fsdp", 0, 0, tiled=True)
-    dense_x, dense_y = swap(dense_mine, "ctx", 1), swap(dense_mine, "ctx", 2)
+        then(d_partial, summed, qkv_sent2), "fsdp", scatter_dimension=0, tiled=True
+    )
+
+    def with_totals(values):
+        rest = jnp.pad(totals.astype(low).reshape(nf, -1, values.shape[2]), ((0, 0), (0, 4), (0, 0)))
+        return jnp.concatenate([values, rest], axis=1)
+
+    both_got = then(both_got, rows_got, qkv_got2)
+    in_mine = added(both_kept, both_got)
+    rows_mine = added(rows_kept, then(rows_got, both_got))
+    rows_x, rows_y = swap(rows_mine, "ctx", 1), swap(rows_mine, "ctx", 2)
+    in_rows = lax.all_to_all(in_mine[:nf], "fsdp", 0, 0, tiled=True)
+    qkv_mine = added(qkv_kept2, then(qkv_got2, both_got, rows_x, rows_y))
+    qkv_rows = lax.all_to_all(with_totals(qkv_mine), "fsdp", 0, 0, tiled=True)
+    rows_xy = swap(rows_y, "ctx", 1)
+    in_rows = jnp.concatenate([then(in_rows, rows_x, rows_y), in_mine[nf:]])
     in_x, in_y = swap(in_rows, "ctx", 1), swap(in_rows, "ctx", 2)
-    dense_xy = swap(then(dense_x, qkv_rows), "ctx", 2)
+    totals = jnp.sum(qkv_rows[:, part:].astype(wide), axis=0).astype(low)
+    totals = jnp.pad(totals, ((0, part - totals.shape[0]), (0, 0)))[None]
+    qkv_rows = then(jnp.concatenate([qkv_rows[:, :part], totals]), rows_xy, in_y)
     qkv_x, qkv_y = swap(qkv_rows, "ctx", 1), swap(qkv_rows, "ctx", 2)
-    in_xy = swap(in_x, "ctx", 2)
+    in_xy = swap(then(in_x, qkv_rows), "ctx", 2)
     qkv_xy = swap(qkv_y, "ctx", 1)
-    out_all = [out_mine, out_x, out_y, out_xy]
+    rows_all = [rows_mine, rows_x, rows_y, rows_xy]
     in_all = [in_rows, in_x, in_y, in_xy]
-    dense_all = [dense_mine, dense_x, dense_y, dense_xy]
     qkv_all = [qkv_rows, qkv_x, qkv_y, qkv_xy]
-
-    def whole_rows(pieces, shape):
-        return finish(pieces, plane, jnp.zeros((nc,), jnp.int32), shape)
-
-    def whole_columns(pieces, places, shape, thirds):
-        at_rows = (places[:, None] * jnp.ones((nf,), jnp.int32)).reshape(-1)
-        at_cols = jnp.tile(jnp.arange(nf, dtype=jnp.int32), nc)
-        return finish(pieces, at_rows, at_cols, shape, thirds)
-
-    grad_fc_out = whole_rows(out_all, fc_out_weight.shape)
+    by_x = 2 * (plane % 2) + plane // 2
+
+    def whole_columns(pieces, places, shape, thirds, begin=0, count=nf):
+        at_rows = (places[:, None] * jnp.ones((count,), jnp.int32)).reshape(-1)
+        at_cols = jnp.tile(jnp.arange(count, dtype=jnp.int32), nc)
+        return finish(pieces, at_rows, at_cols, shape, thirds, (begin, count))
+
+    grad_fc_out = whole_columns(rows_all, plane, fc_out_weight.shape, 1, 0, 1)
     grad_fc_in = whole_columns(in_all, plane, fc_in_weight.shape, 1)
-    grad_dense = whole_rows(dense_all, dense_weight.shape)
-    grad_qkv = whole_columns(qkv_all, 2 * (plane % 2) + plane // 2, qkv_weight.shape, 3)
+    grad_dense = whole_columns(in_all, plane, dense_weight.shape, 1, nf, width // units)
+    grad_qkv = whole_columns(qkv_all, by_x, qkv_weight.shape, 3)
 
     x_wide = x_own.astype(wide)
+    d_normal = then(d_normal, qkv_x).astype(wide)
     output = (x_wide + summed.astype(wide) + whole[5] + whole[6]).astype(low).reshape(tokens.shape)
     own_normal, own_rstd = normalised(x_wide)
     d_x = own_rstd * (
@@ -1044,7 +1077,7 @@
     )
     input_grad = (g_own.astype(wide) + d_x).reshape(tokens.shape)
 
-    totals = at(totals, me_f)
+    totals = sum(r[-1, :4].astype(wide) for r in qkv_all).reshape(-1)
     cuts, start = [], 0
     for size in (rows, rows, rows, rows, 3 * width // nf, units, rows):
         cuts.append(totals[start : start + size])

time: 660 us -> 619 us (0.938)
  waiting for transfers between devices: 266 us -> 224 us
  Pallas kernels: 216 us -> 226 us
  starting transfers between devices: 65.8 us -> 56 us
    ppermute x50 -> x41, waiting for transfers between devices: 219 us -> 180 us  [swap(): lax.ppermute(values, axis, [(i, i ^ mask) for i in range(lax.axis_size(ax...]
    ppermute x50 -> x41, starting transfers between devices: 57.2 us -> 47 us  [swap(): lax.ppermute(values, axis, [(i, i ^ mask) for i in range(lax.axis_size(ax...]
    pallas_call x24, Pallas kernels: 216 us -> 226 us  [the longest x4 50.2 us: grad_pair(): pl.pallas_call(body, name='grad_pair', grid_spec=pltpu.PrefetchScalarGrid...]
    unnamed x114 -> x98, local copies, waits for them, and re-layouts: 21.2 us -> 16.2 us
  transfers between devices with their start and end apart: 56 -> 47, of which waited for: 24 -> 20; matrix products, arithmetic and copies ran while one was open for 8% -> 10% of each run, Pallas kernels for 30% -> 34%
where the time goes in v3:
time: 619 us; the launch traced here: 614 us
  Pallas kernels  226 us (37%)
  waiting for transfers between devices  224 us (36%)
  starting transfers between devices  56 us (9%)
  local copies, waits for them, and re-layouts  43.8 us (7%)
  other arithmetic  35.2 us (6%)
  between operations  22.8 us (4%)
    ppermute x41, waiting for transfers between devices, swap(): lax.ppermute(values, axis, [(i, i ^ mask) for i in range(lax.axis_size(ax...  180 us
    pallas_call x4, Pallas kernels, grad_pair(): pl.pallas_call(body, name='grad_pair', grid_spec=pltpu.PrefetchScalarGrid...  50.2 us
    ppermute x41, starting transfers between devices, swap(): lax.ppermute(values, axis, [(i, i ^ mask) for i in range(lax.axis_size(ax...  47 us
    pallas_call x1, Pallas kernels, norm_back(): pl.pallas_call(body, name='norm_back', grid=(group // block,), in_specs=[...  26.4 us
    pallas_call x2, Pallas kernels, contract(): pl.pallas_call(body, name='contract', grid=(group // block,), in_specs=[r...  25.9 us
    all_to_all x1, waiting for transfers between devices, local_by_head(): qkv_rows = lax.all_to_all(with_totals(qkv_mine), 'fsdp', 0, 0, tiled=True)  24.3 us
    pallas_call x4, Pallas kernels, finish(): pl.pallas_call(body, name='finish', out_shape=jax.ShapeDtypeStruct(shape,...  19.2 us
    pallas_call x1, Pallas kernels, project(): pl.pallas_call(body, name='project', grid=(group // block,), in_specs=[ro...  17.9 us
  transfers between devices with their start and end apart: 47, of which 20 were waited for; matrix products, arithmetic and copies ran while one was open for 10% of the time, Pallas kernels for 34%

profile of v3, /device:TPU:0, one launch (start us, length us, event | category | flops | bytes accessed | tf_op | source)
XLA Modules:
  0.0 613.9 jit_solution(17106500285325791638)
XLA Ops:
  15.5 3.8 cut_weights.1
  19.3 3.1 collective-permute-start
  22.4 2.6 collective-permute-start.1
  25.0 18.6 %collective-permute-done = bf16[2,64,1920]{2,1,0:T(8,128)(2,1)S(1)} collective-permute-done((bf16[2,64,1920]{2,1,0:T(8,128)(2,1)}, bf16[2,64,1920]{2,1,0:T(8,128)(2,1)S(1)}, u32[]{:S(2)}, u32[]{:S(2)}) %collective-permute-start) | collective-permute-done | bytes 491552 | tf_op jit(solution)/shard_map/ppermute | solution.py:304
  43.6 15.1 %collective-permute-done.1 = bf16[2,64,1920]{2,1,0:T(8,128)(2,1)S(1)} collective-permute-done((bf16[2,64,1920]{2,1,0:T(8,128)(2,1)}, bf16[2,64,1920]{2,1,0:T(8,128)(2,1)S(1)}, u32[]{:S(2)}, u32[]{:S(2)}) %collective-permute-start.1) | collective-permute-done | bytes 491552 | tf_op jit(solution)/shard_map/ppermute | solution.py:304
  88.2 16.0 %collective-permute-done.6 = s32[2,2,256]{2,1,0:T(2,128)S(1)} collective-permute-done((s32[2,2,256]{2,1,0:T(2,128)S(1)}, s32[2,2,256]{2,1,0:T(2,128)S(1)}, u32[]{:S(2)}, u32[]{:S(2)}) %collective-permute-start.6) | collective-permute-done | bytes 4128 | tf_op jit(solution)/shard_map/ppermute | solution.py:304
  107.4 4.0 fusion.21
  111.5 4.0 fusion.19
  115.9 8.2 %collective-permute-done.11.refs_2_ = bf16[8,64,768]{2,1,0:T(8,128)(2,1)} collective-permute-done((bf16[8,64,768]{2,1,0:T(8,128)(2,1)S(1)}, bf16[8,64,768]{2,1,0:T(8,128)(2,1)}, u32[]{:S(2)}, u32[]{:S(2)}) %collective-permute-start.11) | collective-permute-done | bytes 786464 | tf_op jit(solution)/shard_map/ppermute | solution.py:304
  126.9 2.9 fusion.14
  129.8 12.1 %collective-permute-done.12.refs_3_ = bf16[8,64,768]{2,1,0:T(8,128)(2,1)S(1)} collective-permute-done((bf16[8,64,768]{2,1,0:T(8,128)(2,1)}, bf16[8,64,768]{2,1,0:T(8,128)(2,1)S(1)}, u32[]{:S(2)}, u32[]{:S(2)}) %collective-permute-start.12) | collective-permute-done | bytes 786464 | tf_op jit(solution)/shard_map/ppermute | solution.py:304
  142.7 4.2 place.5
  148.6 5.2 place.4
  153.8 17.9 %project.1 = (bf16[2048,2048]{1,0:T(8,128)(2,1)}, bf16[2048,2048]{1,0:T(8,128)(2,1)}, bf16[2048,768]{1,0:T(8,128)(2,1)}) custom-call(bf16[2048,2048]{1,0:T(8,128)(2,1)} %all-gather.3.cloned.1.call-done.x_ref, bf16[2048,768]{1,0:T(8,128)(2,1)} %bitcast.150, f32[1,768]{1,0:T(1,128)} %bitcast.175, f32[4,2048]{1,0:T(4,128)} %pad_maximum_fusion.9.n_ref.g_ref, ...), custom_call_target="tpu_custom_call" | custom-call | flops 1 | bytes 1 | tf_op jit(solution)/shard_map/project/pallas_call | solution.py:523
  171.7 3.0 dynamic-slice_bitcast_fusion
  180.1 16.9 %expand.1 = (bf16[2048,1024]{1,0:T(8,128)(2,1)}, bf16[2048,1024]{1,0:T(8,128)(2,1)}) custom-call(bf16[2048,2048]{1,0:T(8,128)(2,1)} %get-tuple-element.89.s_ref.a_ref.b_ref, bf16[2048,1024]{1,0:T(8,128)(2,1)} %bitcast.148, f32[1,1024]{1,0:T(1,128)} %bitcast.173), custom_call_target="tpu_custom_call" | custom-call | flops 1 | bytes 1 | tf_op jit(solution)/shard_map/expand/pallas_call | solution.py:551
  197.0 14.4 %contract.2.refs_0_ = bf16[2048,2048]{1,0:T(8,128)(2,1)} custom-call(bf16[2048,1024]{1,0:T(8,128)(2,1)} %get-tuple-element.90.left_ref.a_ref.b_ref, bf16[1024,2048]{1,0:T(8,128)(2,1)} %w_ref.1), custom_call_target="tpu_custom_call" | custom-call | flops 1 | bytes 1 | tf_op jit(solution)/shard_map/contract/pallas_call | solution.py:574
  212.7 8.5 %attend.1 = (bf16[2,256,256]{2,1,0:T(8,128)(2,1)}, bf16[2,256,256]{2,1,0:T(8,128)(2,1)}, bf16[2,256,256]{2,1,0:T(8,128)(2,1)}, bf16[2,256,256]{2,1,0:T(8,128)(2,1)}) custom-call(s32[4]{0:T(128)} %copy-done.26, s32[2,1,1024]{2,1,0:T(1,128)} %get-tuple-element.192.row_ref, s32[2,1024,1]{2,1,0:T(8,128)} %broadcast_in_dim_squeeze.4.col_ref, ...), custom_call_target="tpu_custom_call" | custom-call | flops 1 | bytes 1 | tf_op jit(solution)/shard_map/attend/pallas_call | solution.py:746
  224.8 6.7 %all-gather.5.cloned.1.call-done.right_ref.g_ref = bf16[2048,2048]{1,0:T(8,128)(2,1)} async-done(((bf16[256,2048]{1,0:T(8,128)(2,1)}), bf16[2048,2048]{1,0:T(8,128)(2,1)}) %all-gather.5.cloned.1.call-update) | async-done | bytes 8388624 | tf_op jit(solution)/shard_map/all_gather | solution.py:917
  231.5 5.8 convolution_convert_fusion
  244.8 2.8 place.6
  247.6 11.5 %contract.3 = bf16[2048,2048]{1,0:T(8,128)(2,1)} custom-call(bf16[2048,256]{1,0:T(8,128)(2,1)} %bitcast.153, bf16[256,2048]{1,0:T(8,128)(2,1)} %weight_ref.3, bf16[2048,2048]{1,0:T(8,128)(2,1)} %contract.2.refs_0_), custom_call_target="tpu_custom_call" | custom-call | flops 1 | bytes 1 | tf_op jit(solution)/shard_map/contract/pallas_call | solution.py:574
  259.1 7.1 %grad_pair.4 = (bf16[1,2,64,2048]{3,2,1,0:T(8,128)(2,1)}, bf16[1,2,64,2048]{3,2,1,0:T(8,128)(2,1)}) custom-call(s32[1]{0:T(128)} %bitcast.29.keep_ref.bit_ref, s32[1]{0:T(128)} %bitcast.30.send_ref, bf16[2048,256]{1,0:T(8,128)(2,1)} %bitcast.154, bf16[2048,256]{1,0:T(8,128)(2,1)} %bitcast.155, bf16[2048,2048]{1,0:T(8,128)(2,1)} %all-gather.5.cloned.1.call-done.right_ref.g_ref), custom_call_target="tpu_custom_call" | custom-call | flops 1 | bytes 1 | tf_op jit(solution)/shard_map/grad_pair/pallas_call | solution.py:629
  267.1 13.9 %attend_back.1 = (bf16[2,256,768]{2,1,0:T(8,128)(2,1)}, bf16[2,256,768]{2,1,0:T(8,128)(2,1)}, bf16[2,256,768]{2,1,0:T(8,128)(2,1)}, bf16[2,256,768]{2,1,0:T(8,128)(2,1)}) custom-call(s32[4]{0:T(128)} %copy-done.26, s32[2,1,1024]{2,1,0:T(1,128)} %get-tuple-element.192.row_ref, s32[2,1024,1]{2,1,0:T(8,128)} %broadcast_in_dim_squeeze.4.col_ref, ...), custom_call_target="tpu_custom_call" | custom-call | flops 1 | bytes 1 | tf_op jit(solution)/shard_map/attend_back/pallas_call | solution.py:808
  285.9 16.2 %hidden_back.1 = (bf16[2048,1024]{1,0:T(8,128)(2,1)}, f32[1,1024]{1,0:T(1,128)}) custom-call(bf16[2048,2048]{1,0:T(8,128)(2,1)} %all-gather.5.cloned.1.call-done.right_ref.g_ref, bf16[1024,2048]{1,0:T(8,128)(2,1)} %w_ref.1, bf16[2048,1024]{1,0:T(8,128)(2,1)} %get-tuple-element.115.s_ref), custom_call_target="tpu_custom_call" | custom-call | flops 1 | bytes 1 | tf_op jit(solution)/shard_map/hidden_back/pallas_call | solution.py:600
  302.1 15.1 %grad_pair.5 = (bf16[4,1,128,2048]{3,2,1,0:T(8,128)(2,1)}, bf16[4,1,128,2048]{3,2,1,0:T(8,128)(2,1)}) custom-call(s32[4]{0:T(128)} %get-tuple-element.218.keep_ref, s32[4]{0:T(128)} %get-tuple-element.219.send_ref, bf16[2048,1024]{1,0:T(8,128)(2,1)} %get-tuple-element.90.left_ref.a_ref.b_ref, bf16[2048,1024]{1,0:T(8,128)(2,1)} %get-tuple-element.90.left_ref.a_ref.b_ref, ...), custom_call_target="tpu_custom_call" | custom-call | flops 1 | bytes 1 | tf_op jit(solution)/shard_map/grad_pair/pallas_call | solution.py:629
  319.3 14.8 %grad_pair.6 = (bf16[8,2,64,1024]{3,2,1,0:T(8,128)(2,1)}, bf16[8,2,64,1024]{3,2,1,0:T(8,128)(2,1)}) custom-call(s32[8]{0:T(128)} %stack.203.keep_ref, s32[8]{0:T(128)} %stack.211.send_ref, bf16[2048,2048]{1,0:T(8,128)(2,1)} %get-tuple-element.89.s_ref.a_ref.b_ref, bf16[2048,2048]{1,0:T(8,128)(2,1)} %get-tuple-element.89.s_ref.a_ref.b_ref, ...), custom_call_target="tpu_custom_call" | custom-call | flops 1 | bytes 1 | tf_op jit(solution)/shard_map/grad_pair/pallas_call | solution.py:629
  337.7 3.4 place.7
  341.2 13.3 %grad_pair.7 = (bf16[8,2,64,768]{3,2,1,0:T(8,128)(2,1)}, bf16[8,2,64,768]{3,2,1,0:T(8,128)(2,1)}) custom-call(s32[8]{0:T(128)} %stack.186.keep_ref, s32[8]{0:T(128)} %stack.195.send_ref, bf16[2048,2048]{1,0:T(8,128)(2,1)} %get-tuple-element.113.a_ref.b_ref, bf16[2048,2048]{1,0:T(8,128)(2,1)} %get-tuple-element.113.a_ref.b_ref, bf16[2048,768]{1,0:T(8,128)(2,1)} %bitcast.146), custom_call_target="tpu_custom_call" | custom-call | flops 1 | bytes 1 | tf_op jit(solution)/shard_map/grad_pair/pallas_call | solution.py:629
  355.4 26.4 %norm_back.1 = (bf16[2048,2048]{1,0:T(8,128)(2,1)}, f32[4,2048]{1,0:T(4,128)}) custom-call(bf16[2048,2048]{1,0:T(8,128)(2,1)} %all-gather.3.cloned.1.call-done.x_ref, bf16[2048,768]{1,0:T(8,128)(2,1)} %bitcast.147, bf16[2048,1024]{1,0:T(8,128)(2,1)} %get-tuple-element.119.right_ref.h_ref, bf16[2048,768]{1,0:T(8,128)(2,1)} %bitcast.151, ...), custom_call_target="tpu_custom_call" | custom-call | flops 1 | bytes 1 | tf_op jit(solution)/shard_map/norm_back/pallas_call | solution.py:847
  383.2 3.9 add_split.2
  387.1 3.5 collective-permute-done.28.d_ref
  391.4 4.5 add_split_two.1
  396.7 2.8 add_split.3
  403.5 23.8 %collective-permute-done.31 = bf16[1,256,2048]{2,1,0:T(8,128)(2,1)S(1)} collective-permute-done((bf16[1,256,2048]{2,1,0:T(8,128)(2,1)}, bf16[1,256,2048]{2,1,0:T(8,128)(2,1)S(1)}, u32[]{:S(2)}, u32[]{:S(2)}) %collective-permute-start.31) | collective-permute-done | bytes 1048608 | tf_op jit(solution)/shard_map/ppermute | solution.py:304
  427.3 12.5 %collective-permute-done.29 = bf16[8,64,768]{2,1,0:T(8,128)(2,1)} collective-permute-done((bf16[8,64,768]{2,1,0:T(8,128)(2,1)}, bf16[8,64,768]{2,1,0:T(8,128)(2,1)}, u32[]{:S(2)}, u32[]{:S(2)}) %collective-permute-start.29) | collective-permute-done | bytes 786464 | tf_op jit(solution)/shard_map/ppermute | solution.py:304
  444.3 4.2 all-to-all-start.1
  453.6 22.7 %collective-permute-done.32.refs_1_ = bf16[1,256,2048]{2,1,0:T(8,128)(2,1)} collective-permute-done((bf16[1,256,2048]{2,1,0:T(8,128)(2,1)S(1)}, bf16[1,256,2048]{2,1,0:T(8,128)(2,1)}, u32[]{:S(2)}, u32[]{:S(2)}) %collective-permute-start.32) | collective-permute-done | bytes 1048608 | tf_op jit(solution)/shard_map/ppermute | solution.py:304
  479.3 13.1 %all-to-all-done.1 = bf16[8,64,1024]{2,1,0:T(8,128)(2,1)} async-done(((bf16[8,64,1024]{2,1,0:T(8,128)(2,1)}), bf16[8,64,1024]{2,1,0:T(8,128)(2,1)}, u32[]{:S(2)}, u32[]{:S(2)}) %all-to-all-start.1) | async-done | bytes 1048608 | tf_op jit(solution)/shard_map/all_to_all | solution.py:1042
  492.3 4.4 all-to-all-start
  501.8 24.3 %all-to-all-done = bf16[8,72,768]{2,1,0:T(8,128)(2,1)} async-done(((bf16[8,72,768]{2,1,0:T(8,128)(2,1)}), bf16[8,72,768]{2,1,0:T(8,128)(2,1)}, u32[]{:S(2)}, u32[]{:S(2)}) %all-to-all-start) | async-done | bytes 884768 | tf_op jit(solution)/shard_map/all_to_all | solution.py:1044
  530.9 22.4 %collective-permute-done.39.refs_1_ = bf16[10,64,1024]{2,1,0:T(8,128)(2,1)} collective-permute-done((bf16[10,64,1024]{2,1,0:T(8,128)(2,1)S(1)}, bf16[10,64,1024]{2,1,0:T(8,128)(2,1)}, u32[]{:S(2)}, u32[]{:S(2)}) %collective-permute-start.39) | collective-permute-done | bytes 1310752 | tf_op jit(solution)/shard_map/ppermute | solution.py:304
  559.0 5.4 finish.7
  564.5 19.1 %collective-permute-done.40.refs_3_ = bf16[10,64,1024]{2,1,0:T(8,128)(2,1)} collective-permute-done((bf16[10,64,1024]{2,1,0:T(8,128)(2,1)}, bf16[10,64,1024]{2,1,0:T(8,128)(2,1)}, u32[]{:S(2)}, u32[]{:S(2)}) %collective-permute-start.40) | collective-permute-done | bytes 1310752 | tf_op jit(solution)/shard_map/ppermute | solution.py:304
  583.5 3.0 finish.5
  586.6 5.4 finish.6
  593.6 5.3 finish.4
  603.6 2.9 fusion.6
  (288 shorter events, 110.4 us)
Async XLA Ops:
  7.2 146.7 %all-gather.3.cloned.1.call-start = ((), (), s32[]{:S(2)}) async-start(), calls=%async_computation.4 | async-start | bytes 9437184 | tf_op jit(solution)/shard_map/all_gather | solution.py:915
  19.3 24.3 %collective-permute-start = (bf16[2,64,1920]{2,1,0:T(8,128)(2,1)}, bf16[2,64,1920]{2,1,0:T(8,128)(2,1)S(1)}, u32[]{:S(2)}, u32[]{:S(2)}) collective-permute-start(bf16[2,64,1920]{2,1,0:T(8,128)(2,1)} %get-tuple-element.82), channel_id=1, source_target_pairs={{0,2},{1,3},{2,0},{3,1},{4,6},{5,7},{6,4},{7,5},{8,10},{9,11},{10,... | collective-permute-start | bytes 1474568 | tf_op jit(solution)/shard_map/ppermute | solution.py:304
  22.4 36.3 %collective-permute-start.1 = (bf16[2,64,1920]{2,1,0:T(8,128)(2,1)}, bf16[2,64,1920]{2,1,0:T(8,128)(2,1)S(1)}, u32[]{:S(2)}, u32[]{:S(2)}) collective-permute-start(bf16[2,64,1920]{2,1,0:T(8,128)(2,1)} %get-tuple-element.83), channel_id=1, source_target_pairs={{0,4},{1,5},{2,6},{3,7},{4,0},{5,1},{6,2},{7,3},{8,12},{9,13},{10,... | collective-permute-start | bytes 1474568 | tf_op jit(solution)/shard_map/ppermute | solution.py:304
  25.0 33.7 %collective-permute-start.2 = (bf16[2,64,1920]{2,1,0:T(8,128)(2,1)}, bf16[2,64,1920]{2,1,0:T(8,128)(2,1)S(1)}, u32[]{:S(2)}, u32[]{:S(2)}) collective-permute-start(bf16[2,64,1920]{2,1,0:T(8,128)(2,1)} %get-tuple-element.84), channel_id=1, source_target_pairs={{0,6},{1,7},{2,4},{3,5},{4,2},{5,3},{6,0},{7,1},{8,14},{9,15},{10,... | collective-permute-start | bytes 1474568 | tf_op jit(solution)/shard_map/ppermute | solution.py:304
  58.8 172.7 %all-gather.5.cloned.1.call-start = ((), (), s32[]{:S(2)}) async-start(), calls=%async_computation.5 | async-start | bytes 9437184 | tf_op jit(solution)/shard_map/all_gather | solution.py:917
  62.9 2.6 collective-permute-start.3
  65.6 333.9 %reduce-scatter.3.cloned.1.call-start = ((), (), s32[]{:S(2)}) async-start(), calls=%async_computation.6 | async-start | bytes 9437184 | tf_op jit(solution)/shard_map/reduce_scatter | solution.py:983
  77.8 46.9 %collective-permute-start.7 = (bf16[8,64,1024]{2,1,0:T(8,128)(2,1)S(1)}, bf16[8,64,1024]{2,1,0:T(8,128)(2,1)}, u32[]{:S(2)}, u32[]{:S(2)}) collective-permute-start(bf16[8,64,1024]{2,1,0:T(8,128)(2,1)S(1)} %slice.231.refs_0_), channel_id=1, source_target_pairs={{0,8},{8,0},{16,24},{24,16},{1,9},{9,1},{17,25},{25,17},{2,10},{10... | collective-permute-start | bytes 3145736 | tf_op jit(solution)/shard_map/ppermute | solution.py:304
  79.2 67.8 %collective-permute-start.8 = (bf16[8,64,1024]{2,1,0:T(8,128)(2,1)S(1)}, bf16[8,64,1024]{2,1,0:T(8,128)(2,1)}, u32[]{:S(2)}, u32[]{:S(2)}) collective-permute-start(bf16[8,64,1024]{2,1,0:T(8,128)(2,1)S(1)} %slice.231.refs_0_), channel_id=1, source_target_pairs={{0,16},{8,24},{16,0},{24,8},{1,17},{9,25},{17,1},{25,9},{2,18},{10... | collective-permute-start | bytes 3145736 | tf_op jit(solution)/shard_map/ppermute | solution.py:304
  82.1 22.0 %collective-permute-start.6 = (s32[2,2,256]{2,1,0:T(2,128)S(1)}, s32[2,2,256]{2,1,0:T(2,128)S(1)}, u32[]{:S(2)}, u32[]{:S(2)}) collective-permute-start(s32[2,2,256]{2,1,0:T(2,128)S(1)} %bitcast.179), channel_id=1, source_target_pairs={{0,24},{8,16},{16,8},{24,0},{1,25},{9,17},{17,9},{25,1},{2,26},{10... | collective-permute-start | bytes 12296 | tf_op jit(solution)/shard_map/ppermute | solution.py:304
  82.8 22.8 %collective-permute-start.5 = (s32[2,2,256]{2,1,0:T(2,128)S(1)}, s32[2,2,256]{2,1,0:T(2,128)S(1)}, u32[]{:S(2)}, u32[]{:S(2)}) collective-permute-start(s32[2,2,256]{2,1,0:T(2,128)S(1)} %bitcast.178), channel_id=1, source_target_pairs={{0,16},{8,24},{16,0},{24,8},{1,17},{9,25},{17,1},{25,9},{2,18},{10... | collective-permute-start | bytes 12296 | tf_op jit(solution)/shard_map/ppermute | solution.py:304
  84.2 21.9 %collective-permute-start.4 = (s32[2,2,256]{2,1,0:T(2,128)S(1)}, s32[2,2,256]{2,1,0:T(2,128)S(1)}, u32[]{:S(2)}, u32[]{:S(2)}) collective-permute-start(s32[2,2,256]{2,1,0:T(2,128)S(1)} %bitcast.177), channel_id=1, source_target_pairs={{0,8},{8,0},{16,24},{24,16},{1,9},{9,1},{17,25},{25,17},{2,10},{10... | collective-permute-start | bytes 12296 | tf_op jit(solution)/shard_map/ppermute | solution.py:304
  104.2 25.6 %collective-permute-start.10 = (bf16[8,64,768]{2,1,0:T(8,128)(2,1)S(1)}, bf16[8,64,768]{2,1,0:T(8,128)(2,1)}, u32[]{:S(2)}, u32[]{:S(2)}) collective-permute-start(bf16[8,64,768]{2,1,0:T(8,128)(2,1)S(1)} %slice.232.refs_0_), channel_id=1, source_target_pairs={{0,8},{8,0},{16,24},{24,16},{1,9},{9,1},{17,25},{25,17},{2,10},{10... | collective-permute-start | bytes 2359304 | tf_op jit(solution)/shard_map/ppermute | solution.py:304
  105.5 18.6 %collective-permute-start.11 = (bf16[8,64,768]{2,1,0:T(8,128)(2,1)S(1)}, bf16[8,64,768]{2,1,0:T(8,128)(2,1)}, u32[]{:S(2)}, u32[]{:S(2)}) collective-permute-start(bf16[8,64,768]{2,1,0:T(8,128)(2,1)S(1)} %slice.232.refs_0_), channel_id=1, source_target_pairs={{0,16},{8,24},{16,0},{24,8},{1,17},{9,25},{17,1},{25,9},{2,18},{10... | collective-permute-start | bytes 2359304 | tf_op jit(solution)/shard_map/ppermute | solution.py:304
  124.1 17.8 %collective-permute-start.12 = (bf16[8,64,768]{2,1,0:T(8,128)(2,1)}, bf16[8,64,768]{2,1,0:T(8,128)(2,1)S(1)}, u32[]{:S(2)}, u32[]{:S(2)}) collective-permute-start(bf16[8,64,768]{2,1,0:T(8,128)(2,1)} %collective-permute-done.11.refs_2_), channel_id=1, source_target_pairs={{0,8},{8,0},{16,24},{24,16},{1,9},{9,1},{17,25},{25,17},{2,10},{10... | collective-permute-start | bytes 2359304 | tf_op jit(solution)/shard_map/ppermute | solution.py:304
  124.7 23.0 %collective-permute-start.9 = (bf16[8,64,1024]{2,1,0:T(8,128)(2,1)}, bf16[8,64,1024]{2,1,0:T(8,128)(2,1)S(1)}, u32[]{:S(2)}, u32[]{:S(2)}) collective-permute-start(bf16[8,64,1024]{2,1,0:T(8,128)(2,1)} %collective-permute-done.7.refs_1_), channel_id=1, source_target_pairs={{0,16},{8,24},{16,0},{24,8},{1,17},{9,25},{17,1},{25,9},{2,18},{10... | collective-permute-start | bytes 3145736 | tf_op jit(solution)/shard_map/ppermute | solution.py:304
  174.7 36.6 %collective-permute-start.13 = (bf16[2,256,768]{2,1,0:T(8,128)(2,1)S(1)}, bf16[2,256,768]{2,1,0:T(8,128)(2,1)S(1)}, u32[]{:S(2)}, u32[]{:S(2)}) collective-permute-start(bf16[2,256,768]{2,1,0:T(8,128)(2,1)S(1)} %get-tuple-element.156), channel_id=1, source_target_pairs={{0,8},{8,0},{16,24},{24,16},{1,9},{9,1},{17,25},{25,17},{2,10},{10... | collective-permute-start | bytes 2359304 | tf_op jit(solution)/shard_map/ppermute | solution.py:304
  176.2 35.1 %collective-permute-start.14 = (bf16[2,256,768]{2,1,0:T(8,128)(2,1)S(1)}, bf16[2,256,768]{2,1,0:T(8,128)(2,1)S(1)}, u32[]{:S(2)}, u32[]{:S(2)}) collective-permute-start(bf16[2,256,768]{2,1,0:T(8,128)(2,1)S(1)} %get-tuple-element.155), channel_id=1, source_target_pairs={{0,16},{8,24},{16,0},{24,8},{1,17},{9,25},{17,1},{25,9},{2,18},{10... | collective-permute-start | bytes 2359304 | tf_op jit(solution)/shard_map/ppermute | solution.py:304
  176.4 34.9 %collective-permute-start.15 = (bf16[2,256,768]{2,1,0:T(8,128)(2,1)S(1)}, bf16[2,256,768]{2,1,0:T(8,128)(2,1)S(1)}, u32[]{:S(2)}, u32[]{:S(2)}) collective-permute-start(bf16[2,256,768]{2,1,0:T(8,128)(2,1)S(1)} %get-tuple-element.154), channel_id=1, source_target_pairs={{0,24},{8,16},{16,8},{24,0},{1,25},{9,17},{17,9},{25,1},{2,26},{10... | collective-permute-start | bytes 2359304 | tf_op jit(solution)/shard_map/ppermute | solution.py:304
  221.2 19.9 %collective-permute-start.16 = (bf16[2,256,256]{2,1,0:T(8,128)(2,1)}, bf16[2,256,256]{2,1,0:T(8,128)(2,1)S(1)}, u32[]{:S(2)}, u32[]{:S(2)}) collective-permute-start(bf16[2,256,256]{2,1,0:T(8,128)(2,1)} %get-tuple-element.96), channel_id=1, source_target_pairs={{0,8},{8,0},{16,24},{24,16},{1,9},{9,1},{17,25},{25,17},{2,10},{10... | collective-permute-start | bytes 786440 | tf_op jit(solution)/shard_map/ppermute | solution.py:304
  222.8 20.6 %collective-permute-start.17 = (bf16[2,256,256]{2,1,0:T(8,128)(2,1)}, bf16[2,256,256]{2,1,0:T(8,128)(2,1)S(1)}, u32[]{:S(2)}, u32[]{:S(2)}) collective-permute-start(bf16[2,256,256]{2,1,0:T(8,128)(2,1)} %get-tuple-element.97), channel_id=1, source_target_pairs={{0,16},{8,24},{16,0},{24,8},{1,17},{9,25},{17,1},{25,9},{2,18},{10... | collective-permute-start | bytes 786440 | tf_op jit(solution)/shard_map/ppermute | solution.py:304
  222.9 20.5 %collective-permute-start.18 = (bf16[2,256,256]{2,1,0:T(8,128)(2,1)}, bf16[2,256,256]{2,1,0:T(8,128)(2,1)S(1)}, u32[]{:S(2)}, u32[]{:S(2)}) collective-permute-start(bf16[2,256,256]{2,1,0:T(8,128)(2,1)} %get-tuple-element.98), channel_id=1, source_target_pairs={{0,24},{8,16},{16,8},{24,0},{1,25},{9,17},{17,9},{25,1},{2,26},{10... | collective-permute-start | bytes 786440 | tf_op jit(solution)/shard_map/ppermute | solution.py:304
  238.1 28.1 %collective-permute-start.19 = (bf16[2,256,256]{2,1,0:T(8,128)(2,1)S(1)}, bf16[2,256,256]{2,1,0:T(8,128)(2,1)S(1)}, u32[]{:S(2)}, u32[]{:S(2)}) collective-permute-start(bf16[2,256,256]{2,1,0:T(8,128)(2,1)S(1)} %get-tuple-element.166), channel_id=1, source_target_pairs={{0,8},{8,0},{16,24},{24,16},{1,9},{9,1},{17,25},{25,17},{2,10},{10... | collective-permute-start | bytes 786440 | tf_op jit(solution)/shard_map/ppermute | solution.py:304
  239.6 26.6 %collective-permute-start.20 = (bf16[2,256,256]{2,1,0:T(8,128)(2,1)S(1)}, bf16[2,256,256]{2,1,0:T(8,128)(2,1)S(1)}, u32[]{:S(2)}, u32[]{:S(2)}) collective-permute-start(bf16[2,256,256]{2,1,0:T(8,128)(2,1)S(1)} %get-tuple-element.165), channel_id=1, source_target_pairs={{0,16},{8,24},{16,0},{24,8},{1,17},{9,25},{17,1},{25,9},{2,18},{10... | collective-permute-start | bytes 786440 | tf_op jit(solution)/shard_map/ppermute | solution.py:304
  241.1 25.2 %collective-permute-start.21 = (bf16[2,256,256]{2,1,0:T(8,128)(2,1)S(1)}, bf16[2,256,256]{2,1,0:T(8,128)(2,1)S(1)}, u32[]{:S(2)}, u32[]{:S(2)}) collective-permute-start(bf16[2,256,256]{2,1,0:T(8,128)(2,1)S(1)} %get-tuple-element.164), channel_id=1, source_target_pairs={{0,24},{8,16},{16,8},{24,0},{1,25},{9,17},{17,9},{25,1},{2,26},{10... | collective-permute-start | bytes 786440 | tf_op jit(solution)/shard_map/ppermute | solution.py:304
  281.0 320.6 %reduce-scatter.5.cloned.1.call-start = ((), (), s32[]{:S(2)}) async-start(), calls=%async_computation.7 | async-start | bytes 9437184 | tf_op jit(solution)/shard_map/reduce_scatter | solution.py:1030
  281.1 55.8 %collective-permute-start.22 = (bf16[2,256,768]{2,1,0:T(8,128)(2,1)}, bf16[2,256,768]{2,1,0:T(8,128)(2,1)S(1)}, u32[]{:S(2)}, u32[]{:S(2)}) collective-permute-start(bf16[2,256,768]{2,1,0:T(8,128)(2,1)} %get-tuple-element.109), channel_id=1, source_target_pairs={{0,8},{8,0},{16,24},{24,16},{1,9},{9,1},{17,25},{25,17},{2,10},{10... | collective-permute-start | bytes 2359304 | tf_op jit(solution)/shard_map/ppermute | solution.py:304
  282.6 54.3 %collective-permute-start.23 = (bf16[2,256,768]{2,1,0:T(8,128)(2,1)}, bf16[2,256,768]{2,1,0:T(8,128)(2,1)}, u32[]{:S(2)}, u32[]{:S(2)}) collective-permute-start(bf16[2,256,768]{2,1,0:T(8,128)(2,1)} %get-tuple-element.110), channel_id=1, source_target_pairs={{0,16},{8,24},{16,0},{24,8},{1,17},{9,25},{17,1},{25,9},{2,18},{10... | collective-permute-start | bytes 2359304 | tf_op jit(solution)/shard_map/ppermute | solution.py:304
  284.1 52.8 %collective-permute-start.24 = (bf16[2,256,768]{2,1,0:T(8,128)(2,1)}, bf16[2,256,768]{2,1,0:T(8,128)(2,1)}, u32[]{:S(2)}, u32[]{:S(2)}) collective-permute-start(bf16[2,256,768]{2,1,0:T(8,128)(2,1)} %get-tuple-element.111), channel_id=1, source_target_pairs={{0,24},{8,16},{16,8},{24,0},{1,25},{9,17},{17,9},{25,1},{2,26},{10... | collective-permute-start | bytes 2359304 | tf_op jit(solution)/shard_map/ppermute | solution.py:304
  317.2 64.6 %collective-permute-start.27 = (bf16[1,2,256,2048]{3,2,1,0:T(8,128)(2,1)}, bf16[1,2,256,2048]{3,2,1,0:T(8,128)(2,1)S(1)}, u32[]{:S(2)}, u32[]{:S(2)}) collective-permute-start(bf16[1,2,256,2048]{3,2,1,0:T(8,128)(2,1)} %bitcast.180), channel_id=1, source_target_pairs={{0,8},{8,0},{16,24},{24,16},{1,9},{9,1},{17,25},{25,17},{2,10},{10... | collective-permute-start | bytes 6291464 | tf_op jit(solution)/shard_map/ppermute | solution.py:304
  334.1 53.0 %collective-permute-start.26 = (bf16[8,2,64,1024]{3,2,1,0:T(8,128)(2,1)}, bf16[8,2,64,1024]{3,2,1,0:T(8,128)(2,1)}, u32[]{:S(2)}, u32[]{:S(2)}) collective-permute-start(bf16[8,2,64,1024]{3,2,1,0:T(8,128)(2,1)} %get-tuple-element.120), channel_id=1, source_target_pairs={{0,16},{8,24},{16,0},{24,8},{1,17},{9,25},{17,1},{25,9},{2,18},{10... | collective-permute-start | bytes 6291464 | tf_op jit(solution)/shard_map/ppermute | solution.py:304
  354.5 42.2 %collective-permute-start.25 = (bf16[8,2,64,768]{3,2,1,0:T(8,128)(2,1)}, bf16[8,2,64,768]{3,2,1,0:T(8,128)(2,1)}, u32[]{:S(2)}, u32[]{:S(2)}) collective-permute-start(bf16[8,2,64,768]{3,2,1,0:T(8,128)(2,1)} %get-tuple-element.122), channel_id=1, source_target_pairs={{0,8},{8,0},{16,24},{24,16},{1,9},{9,1},{17,25},{25,17},{2,10},{10... | collective-permute-start | bytes 4718600 | tf_op jit(solution)/shard_map/ppermute | solution.py:304
  355.0 35.6 %collective-permute-start.28 = (bf16[1,2,64,2048]{3,2,1,0:T(8,128)(2,1)S(1)}, bf16[1,2,64,2048]{3,2,1,0:T(8,128)(2,1)S(1)}, u32[]{:S(2)}, u32[]{:S(2)}) collective-permute-start(bf16[1,2,64,2048]{3,2,1,0:T(8,128)(2,1)S(1)} %copy-done.34), channel_id=1, source_target_pairs={{0,16},{8,24},{16,0},{24,8},{1,17},{9,25},{17,1},{25,9},{2,18},{10... | collective-permute-start | bytes 1572872 | tf_op jit(solution)/shard_map/ppermute | solution.py:304
  399.5 40.3 %collective-permute-start.30 = (bf16[10,64,1024]{2,1,0:T(8,128)(2,1)}, bf16[10,64,1024]{2,1,0:T(8,128)(2,1)S(1)}, u32[]{:S(2)}, u32[]{:S(2)}) collective-permute-start(bf16[10,64,1024]{2,1,0:T(8,128)(2,1)} %get-tuple-element.132), channel_id=1, source_target_pairs={{0,8},{8,0},{16,24},{24,16},{1,9},{9,1},{17,25},{25,17},{2,10},{10... | collective-permute-start | bytes 3932168 | tf_op jit(solution)/shard_map/ppermute | solution.py:304
  401.0 26.3 %collective-permute-start.31 = (bf16[1,256,2048]{2,1,0:T(8,128)(2,1)}, bf16[1,256,2048]{2,1,0:T(8,128)(2,1)S(1)}, u32[]{:S(2)}, u32[]{:S(2)}) collective-permute-start(bf16[1,256,2048]{2,1,0:T(8,128)(2,1)} %get-tuple-element.129), channel_id=1, source_target_pairs={{0,16},{8,24},{16,0},{24,8},{1,17},{9,25},{17,1},{25,9},{2,18},{10... | collective-permute-start | bytes 3145736 | tf_op jit(solution)/shard_map/ppermute | solution.py:304
  402.5 37.3 %collective-permute-start.29 = (bf16[8,64,768]{2,1,0:T(8,128)(2,1)}, bf16[8,64,768]{2,1,0:T(8,128)(2,1)}, u32[]{:S(2)}, u32[]{:S(2)}) collective-permute-start(bf16[8,64,768]{2,1,0:T(8,128)(2,1)} %get-tuple-element.134), channel_id=1, source_target_pairs={{0,16},{8,24},{16,0},{24,8},{1,17},{9,25},{17,1},{25,9},{2,18},{10... | collective-permute-start | bytes 2359304 | tf_op jit(solution)/shard_map/ppermute | solution.py:304
  444.3 48.0 %all-to-all-start.1 = ((bf16[8,64,1024]{2,1,0:T(8,128)(2,1)}), bf16[8,64,1024]{2,1,0:T(8,128)(2,1)}, u32[]{:S(2)}, u32[]{:S(2)}) async-start(bf16[8,64,1024]{2,1,0:T(8,128)(2,1)} %slice.252), calls=%async_computation.3 | async-start | bytes 2097152 | tf_op jit(solution)/shard_map/all_to_all | solution.py:1042
  450.7 25.7 %collective-permute-start.32 = (bf16[1,256,2048]{2,1,0:T(8,128)(2,1)S(1)}, bf16[1,256,2048]{2,1,0:T(8,128)(2,1)}, u32[]{:S(2)}, u32[]{:S(2)}) collective-permute-start(bf16[1,256,2048]{2,1,0:T(8,128)(2,1)S(1)} %add_convert_fusion.1.refs_0_), channel_id=1, source_target_pairs={{0,8},{8,0},{16,24},{24,16},{1,9},{9,1},{17,25},{25,17},{2,10},{10... | collective-permute-start | bytes 3145736 | tf_op jit(solution)/shard_map/ppermute | solution.py:304
  451.5 25.2 %collective-permute-start.33 = (bf16[1,256,2048]{2,1,0:T(8,128)(2,1)S(1)}, bf16[1,256,2048]{2,1,0:T(8,128)(2,1)}, u32[]{:S(2)}, u32[]{:S(2)}) collective-permute-start(bf16[1,256,2048]{2,1,0:T(8,128)(2,1)S(1)} %add_convert_fusion.1.refs_0_), channel_id=1, source_target_pairs={{0,16},{8,24},{16,0},{24,8},{1,17},{9,25},{17,1},{25,9},{2,18},{10... | collective-permute-start | bytes 3145736 | tf_op jit(solution)/shard_map/ppermute | solution.py:304
  492.3 33.7 %all-to-all-start = ((bf16[8,72,768]{2,1,0:T(8,128)(2,1)}), bf16[8,72,768]{2,1,0:T(8,128)(2,1)}, u32[]{:S(2)}, u32[]{:S(2)}) async-start(bf16[8,72,768]{2,1,0:T(8,128)(2,1)} %fusion.18), calls=%async_computation.2 | async-start | bytes 1769472 | tf_op jit(solution)/shard_map/all_to_all | solution.py:1044
  498.2 59.9 %copy-start.2 = (bf16[10,64,1024]{2,1,0:T(8,128)(2,1)}, bf16[10,64,1024]{2,1,0:T(8,128)(2,1)S(1)}, u32[]{:S(2)}) copy-start(bf16[10,64,1024]{2,1,0:T(8,128)(2,1)S(1)} %pad_maximum_fusion.4.refs_0_) | copy-start | bytes 3932164
  498.2 31.2 %collective-permute-start.35 = (bf16[10,64,1024]{2,1,0:T(8,128)(2,1)S(1)}, bf16[10,64,1024]{2,1,0:T(8,128)(2,1)}, u32[]{:S(2)}, u32[]{:S(2)}) collective-permute-start(bf16[10,64,1024]{2,1,0:T(8,128)(2,1)S(1)} %pad_maximum_fusion.4.refs_0_), channel_id=1, source_target_pairs={{0,16},{8,24},{16,0},{24,8},{1,17},{9,25},{17,1},{25,9},{2,18},{10... | collective-permute-start | bytes 3932168 | tf_op jit(solution)/shard_map/ppermute | solution.py:304
  499.7 29.5 %collective-permute-start.34 = (bf16[1,256,2048]{2,1,0:T(8,128)(2,1)}, bf16[1,256,2048]{2,1,0:T(8,128)(2,1)}, u32[]{:S(2)}, u32[]{:S(2)}) collective-permute-start(bf16[1,256,2048]{2,1,0:T(8,128)(2,1)} %collective-permute-done.33.refs_2_), channel_id=1, source_target_pairs={{0,8},{8,0},{16,24},{24,16},{1,9},{9,1},{17,25},{25,17},{2,10},{10... | collective-permute-start | bytes 3145736 | tf_op jit(solution)/shard_map/ppermute | solution.py:304
  500.4 52.9 %collective-permute-start.39 = (bf16[10,64,1024]{2,1,0:T(8,128)(2,1)S(1)}, bf16[10,64,1024]{2,1,0:T(8,128)(2,1)}, u32[]{:S(2)}, u32[]{:S(2)}) collective-permute-start(bf16[10,64,1024]{2,1,0:T(8,128)(2,1)S(1)} %pad_maximum_fusion.4.refs_0_), channel_id=1, source_target_pairs={{0,8},{8,0},{16,24},{24,16},{1,9},{9,1},{17,25},{25,17},{2,10},{10... | collective-permute-start | bytes 3932168 | tf_op jit(solution)/shard_map/ppermute | solution.py:304
  529.4 25.2 %collective-permute-start.37 = (bf16[9,64,768]{2,1,0:T(8,128)(2,1)}, bf16[9,64,768]{2,1,0:T(8,128)(2,1)}, u32[]{:S(2)}, u32[]{:S(2)}) collective-permute-start(bf16[9,64,768]{2,1,0:T(8,128)(2,1)} %pad_maximum_fusion.8.refs_0_), channel_id=1, source_target_pairs={{0,16},{8,24},{16,0},{24,8},{1,17},{9,25},{17,1},{25,9},{2,18},{10... | collective-permute-start | bytes 2654216 | tf_op jit(solution)/shard_map/ppermute | solution.py:304
  553.3 30.2 %collective-permute-start.40 = (bf16[10,64,1024]{2,1,0:T(8,128)(2,1)}, bf16[10,64,1024]{2,1,0:T(8,128)(2,1)}, u32[]{:S(2)}, u32[]{:S(2)}) collective-permute-start(bf16[10,64,1024]{2,1,0:T(8,128)(2,1)} %collective-permute-done.39.refs_1_), channel_id=1, source_target_pairs={{0,16},{8,24},{16,0},{24,8},{1,17},{9,25},{17,1},{25,9},{2,18},{10... | collective-permute-start | bytes 3932168 | tf_op jit(solution)/shard_map/ppermute | solution.py:304
  553.8 38.1 %collective-permute-start.36 = (bf16[9,64,768]{2,1,0:T(8,128)(2,1)}, bf16[9,64,768]{2,1,0:T(8,128)(2,1)}, u32[]{:S(2)}, u32[]{:S(2)}) collective-permute-start(bf16[9,64,768]{2,1,0:T(8,128)(2,1)} %pad_maximum_fusion.8.refs_0_), channel_id=1, source_target_pairs={{0,8},{8,0},{16,24},{24,16},{1,9},{9,1},{17,25},{25,17},{2,10},{10... | collective-permute-start | bytes 2654216 | tf_op jit(solution)/shard_map/ppermute | solution.py:304
  554.6 39.0 %collective-permute-start.38 = (bf16[9,64,768]{2,1,0:T(8,128)(2,1)}, bf16[9,64,768]{2,1,0:T(8,128)(2,1)}, u32[]{:S(2)}, u32[]{:S(2)}) collective-permute-start(bf16[9,64,768]{2,1,0:T(8,128)(2,1)} %collective-permute-done.37.refs_2_), channel_id=1, source_target_pairs={{0,8},{8,0},{16,24},{24,16},{1,9},{9,1},{17,25},{25,17},{2,10},{10... | collective-permute-start | bytes 2654216 | tf_op jit(solution)/shard_map/ppermute | solution.py:304
  (34 other events, 333.6 us)
Sparse Core Ops, SparseCore 0:
  58.9 90.3 all-gather.2
  150.9 80.5 all-gather.4
  281.1 89.6 reduce-scatter.2
  399.7 106.4 reduce-scatter.4

commit v4 on v3

--- a/solution.py
+++ b/solution.py
@@ -690,28 +690,19 @@
     )(bit[None].astype(jnp.int32), kept, got, other_kept, other_got)
 
 
-def fetch(places_ref, sources, target, sems, block, sequences):
+def fetch(source, target, sems):
+    count, sequences, block, _ = source.shape
     copies = []
-    for m, source in enumerate(sources):
+    for m in range(count):
         for s in range(sequences):
             n = len(copies)
-            start = pl.multiple_of(places_ref[m] * block, block)
             copies.append(
-                pltpu.make_async_copy(source.at[s], target.at[s, pl.ds(start, block)], sems.at[n])
+                pltpu.make_async_copy(
+                    source.at[m, s], target.at[s, pl.ds(m * block, block)], sems.at[n]
+                )
             )
             copies[n].start()
     return copies
-
-
-def send(places_ref, source, targets, sems):
-    copies = [
-        pltpu.make_async_copy(source.at[places_ref[m]], target, sems.at[m])
-        for m, target in enumerate(targets)
-    ]
-    for copy in copies:
-        copy.start()
-    for copy in copies:
-        copy.wait()
 
 
 def block_scores(buf, row_ref, col_ref, s, i, block, hd, scale):
@@ -727,52 +718,48 @@
     return query, key, probs / jnp.sum(probs, axis=-1, keepdims=True)
 
 
-def attend(parts, places, seg_row, seg_col, hd):
-    count = len(parts)
-    sequences, block, cols = parts[0].shape
+def attend(parts, seg_row, seg_col, hd):
+    count, sequences, block, cols = parts.shape
     scale = hd ** (-0.5)
 
-    def body(places_ref, row_ref, col_ref, *refs):
-        outs, (buf, mixed, sems_in, sems_out) = refs[-4 - count : -4], refs[-4:]
-        for copy in fetch(places_ref, refs[:count], buf, sems_in, block, sequences):
+    def body(row_ref, col_ref, parts_ref, out, buf, mixed, sems_in, sem_out):
+        for copy in fetch(parts_ref, buf, sems_in):
             copy.wait()
         for s in range(sequences):
             for i in range(count):
                 _, _, probs = block_scores(buf, row_ref, col_ref, s, i, block, hd, scale)
                 value = buf[s, 0 : (i + 1) * block, 2 * hd : 3 * hd]
                 mixed[i, s] = dot(probs.astype(low), value).astype(low)
-        send(places_ref, mixed, outs, sems_out)
+        copy = pltpu.make_async_copy(mixed, out, sem_out)
+        copy.start()
+        copy.wait()
 
     return pl.pallas_call(
         body,
         name="attend",
-        out_shape=[jax.ShapeDtypeStruct((sequences, block, hd), low)] * count,
-        in_specs=[SCALARS, WHOLE, WHOLE] + [ANY] * count,
-        out_specs=[ANY] * count,
+        out_shape=jax.ShapeDtypeStruct((count, sequences, block, hd), low),
+        in_specs=[WHOLE, WHOLE, ANY],
+        out_specs=ANY,
         scratch_shapes=[
             pltpu.VMEM((sequences, count * block, cols), low),
             pltpu.VMEM((count, sequences, block, hd), low),
             pltpu.SemaphoreType.DMA((count * sequences,)),
-            pltpu.SemaphoreType.DMA((count,)),
+            pltpu.SemaphoreType.DMA,
         ],
         compiler_params=FAST,
         cost_estimate=SMALL,
-    )(places, seg_row, seg_col, *parts)
-
-
-def attend_back(parts, d_parts, places, seg_row, seg_col, tables, hd):
-    count = len(parts)
-    sequences, block, cols = parts[0].shape
+    )(seg_row, seg_col, parts)
+
+
+def attend_back(parts, d_parts, seg_row, seg_col, tables, hd):
+    count, sequences, block, cols = parts.shape
     length = count * block
     scale = hd ** (-0.5)
     half = hd // 8
 
-    def body(places_ref, row_ref, col_ref, t0, t1, t2, *refs):
-        outs = refs[2 * count : 3 * count]
-        buf, d_buf, key_sum, value_sum, done, sems_in, sems_d, sems_out = refs[3 * count :]
-        waits = fetch(places_ref, refs[:count], buf, sems_in, block, sequences)
-        waits += fetch(places_ref, refs[count : 2 * count], d_buf, sems_d, block, sequences)
-        for copy in waits:
+    def body(row_ref, col_ref, t0, t1, t2, parts_ref, d_ref, out, *scratch):
+        buf, d_buf, key_sum, value_sum, done, sems_in, sems_d, sem_out = scratch
+        for copy in fetch(parts_ref, buf, sems_in) + fetch(d_ref, d_buf, sems_d):
             copy.wait()
 
         def put(values, s, i, which):
@@ -803,14 +790,16 @@
                     value_sum[0:n] += value_part
                 put(key_sum[i * block : n], s, i, 1)
                 put(value_sum[i * block : n], s, i, 2)
-        send(places_ref, done, outs, sems_out)
+        copy = pltpu.make_async_copy(done, out, sem_out)
+        copy.start()
+        copy.wait()
 
     return pl.pallas_call(
         body,
         name="attend_back",
-        out_shape=[jax.ShapeDtypeStruct((sequences, block, cols), low)] * count,
-        in_specs=[SCALARS] + [WHOLE] * 5 + [ANY] * (2 * count),
-        out_specs=[ANY] * count,
+        out_shape=jax.ShapeDtypeStruct((count, sequences, block, cols), low),
+        in_specs=[WHOLE] * 5 + [ANY] * 2,
+        out_specs=ANY,
         scratch_shapes=[
             pltpu.VMEM((sequences, length, cols), low),
             pltpu.VMEM((sequences, length, hd), low),
@@ -819,11 +808,11 @@
             pltpu.VMEM((count, sequences, block, cols), low),
             pltpu.SemaphoreType.DMA((count * sequences,)),
             pltpu.SemaphoreType.DMA((count * sequences,)),
-            pltpu.SemaphoreType.DMA((count,)),
+            pltpu.SemaphoreType.DMA,
         ],
         compiler_params=FAST,
         cost_estimate=SMALL,
-    )(places, seg_row, seg_col, *tables, *parts, *d_parts)
+    )(seg_row, seg_col, *tables, parts, d_parts)
 
 
 def norm_back(x_all, d_packed, d_hidden, w_qkv, w_in, gains, block):
@@ -952,39 +941,36 @@
     )
 
     def to_sequences(values):
-        blocks = values.reshape(4, 2, block, values.shape[1])
-        return [
-            at(blocks, plane[m]) if m == 0 else swap(at(blocks, plane[m]), "ctx", m)
-            for m in range(nc)
-        ]
+        return lax.all_to_all(
+            values.reshape(4, 2, block, values.shape[1]), "ctx", 0, 0, tiled=True
+        )
 
     def to_group(values):
-        got = [values[m] if m == 0 else swap(values[m], "ctx", m) for m in range(nc)]
-        places = (2 * plane[:, None] + jnp.arange(2, dtype=jnp.int32)[None, :]).reshape(-1)
-        return place(got, places, nf).reshape(group, values[0].shape[-1])
+        moved = lax.all_to_all(values, "ctx", 0, 0, tiled=True)
+        return moved.reshape(group, values.shape[-1])
 
     parts = to_sequences(packed)
     active, slope = expand(
         then(second, packed), w_in, fc_in_bias.astype(wide).reshape(1, -1), block
     )
     mlp = contract(active, fc_out_weight, block)
-    o = attend([then(p, mlp) for p in parts], plane, seg_row, seg_col, hd)
+    o = attend(then(parts, mlp), seg_row, seg_col, hd)
     o_back = to_group(o)
     x_bit, y_bit = me_c % 2, me_c // 2
-    d_o = dot(then(g_all, *o), dense_weight, 1, 1).astype(low)
+    d_o = dot(then(g_all, o), dense_weight, 1, 1).astype(low)
     d_parts = to_sequences(d_o)
     partial = contract(then(o_back, d_o), dense_weight, block, mlp)
     dense_kept, dense_sent = grad_pair(o_back, then(g_all, partial), [y_bit], [1 - y_bit], 2)
     dense_got = swap(dense_sent, "ctx", 2)
     d_qkv = attend_back(
-        parts, [then(p, dense_sent) for p in d_parts], plane, seg_row, seg_col, seq_tables, hd
+        parts, then(d_parts, dense_sent), seg_row, seg_col, seq_tables, hd
     )
     d_packed = to_group(d_qkv)
-    summed = lax.psum_scatter(then(partial, *d_qkv), "fsdp", scatter_dimension=0, tiled=True)
+    summed = lax.psum_scatter(then(partial, d_qkv), "fsdp", scatter_dimension=0, tiled=True)
 
     rows_of = units // (nc * LANES)
     blocks = [((2 * y) * rows_of, s) for y in range(2) for s in range(rows_of)]
-    d_hidden, hidden_sum = hidden_back(then(g_all, *d_qkv), fc_out_weight, slope, block)
+    d_hidden, hidden_sum = hidden_back(then(g_all, d_qkv), fc_out_weight, slope, block)
     out_kept, out_sent = grad_pair(
         active,
         then(g_all, d_hidden),
@@ -999,10 +985,12 @@
     in_kept, in_sent = grad_pair(second, then(d_hidden, out_sent), *by_y, 2)
     in_got = swap(in_sent, "ctx", 2)
     to_x = [2 * f + x_bit for f in range(nf)], [2 * f + 1 - x_bit for f in range(nf)]
-    qkv_kept, qkv_sent = grad_pair(first, then(d_packed, in_sent), *to_x, 2)
+    qkv_kept, qkv_sent = grad_pair(first, then(d_packed, in_sent, dense_got), *to_x, 2)
     qkv_got = swap(qkv_sent, "ctx", 1)
+    rows_kept, rows_sent = add_split(out_kept, then(out_got, qkv_sent), y_bit)
+    rows_got = swap(rows_sent, "ctx", 2)
     d_partial, sums = norm_back(
-        then(x_all, qkv_sent), d_packed, d_hidden, w_qkv, w_in, norms, block
+        then(x_all, rows_sent), d_packed, d_hidden, w_qkv, w_in, norms, block
     )
     def spread_out(values, parts):
         whole = jnp.zeros((parts, nf, values.shape[0] // parts), wide)
@@ -1019,13 +1007,11 @@
         ],
         axis=1,
     )
-    rows_kept, rows_sent = add_split(out_kept, then(out_got, d_partial), y_bit)
-    rows_got = swap(rows_sent, "ctx", 2)
     both_kept, both_sent = add_split_two(
-        in_kept, then(in_got, rows_sent), dense_kept, dense_got, x_bit
+        in_kept, then(in_got, d_partial), dense_kept, dense_got, x_bit
     )
     both_got = swap(both_sent, "ctx", 1)
-    qkv_kept2, qkv_sent2 = add_split(qkv_kept, then(qkv_got, both_sent), y_bit)
+    qkv_kept2, qkv_sent2 = add_split(qkv_kept, then(qkv_got, both_sent, rows_got), y_bit)
     qkv_got2 = swap(qkv_sent2, "ctx", 2)
     d_normal = lax.psum_scatter(
         then(d_partial, summed, qkv_sent2), "fsdp", scatter_dimension=0, tiled=True
@@ -1043,11 +1029,11 @@
     qkv_mine = added(qkv_kept2, then(qkv_got2, both_got, rows_x, rows_y))
     qkv_rows = lax.all_to_all(with_totals(qkv_mine), "fsdp", 0, 0, tiled=True)
     rows_xy = swap(rows_y, "ctx", 1)
-    in_rows = jnp.concatenate([then(in_rows, rows_x, rows_y), in_mine[nf:]])
+    in_rows = jnp.concatenate([then(in_rows, rows_x, rows_y, rows_xy), in_mine[nf:]])
     in_x, in_y = swap(in_rows, "ctx", 1), swap(in_rows, "ctx", 2)
     totals = jnp.sum(qkv_rows[:, part:].astype(wide), axis=0).astype(low)
     totals = jnp.pad(totals, ((0, part - totals.shape[0]), (0, 0)))[None]
-    qkv_rows = then(jnp.concatenate([qkv_rows[:, :part], totals]), rows_xy, in_y)
+    qkv_rows = then(jnp.concatenate([qkv_rows[:, :part], totals]), in_y)
     qkv_x, qkv_y = swap(qkv_rows, "ctx", 1), swap(qkv_rows, "ctx", 2)
     in_xy = swap(then(in_x, qkv_rows), "ctx", 2)
     qkv_xy = swap(qkv_y, "ctx", 1)
@@ -1060,11 +1046,6 @@
         at_rows = (places[:, None] * jnp.ones((count,), jnp.int32)).reshape(-1)
         at_cols = jnp.tile(jnp.arange(count, dtype=jnp.int32), nc)
         return finish(pieces, at_rows, at_cols, shape, thirds, (begin, count))
-
-    grad_fc_out = whole_columns(rows_all, plane, fc_out_weight.shape, 1, 0, 1)
-    grad_fc_in = whole_columns(in_all, plane, fc_in_weight.shape, 1)
-    grad_dense = whole_columns(in_all, plane, dense_weight.shape, 1, nf, width // units)
-    grad_qkv = whole_columns(qkv_all, by_x, qkv_weight.shape, 3)
 
     x_wide = x_own.astype(wide)
     d_normal = then(d_normal, qkv_x).astype(wide)
@@ -1078,6 +1059,13 @@
     input_grad = (g_own.astype(wide) + d_x).reshape(tokens.shape)
 
     totals = sum(r[-1, :4].astype(wide) for r in qkv_all).reshape(-1)
+    grad_fc_out = whole_columns(rows_all, plane, fc_out_weight.shape, 1, 0, 1)
+    grad_dense = whole_columns(in_all, plane, dense_weight.shape, 1, nf, width // units)
+    in_all[3] = then(in_all[3], grad_fc_out, grad_dense, input_grad, output)
+    grad_fc_in = whole_columns(in_all, plane, fc_in_weight.shape, 1)
+    qkv_all[3] = then(qkv_all[3], grad_fc_in)
+    grad_qkv = whole_columns(qkv_all, by_x, qkv_weight.shape, 3)
+
     cuts, start = [], 0
     for size in (rows, rows, rows, rows, 3 * width // nf, units, rows):
         cuts.append(totals[start : start + size])

time: 619 us -> 616 us (level)
  Pallas kernels: 226 us -> 217 us
  waiting for transfers between devices: 224 us -> 231 us
    ppermute x41 -> x29, starting transfers between devices: 47 us -> 27.9 us  [swap(): lax.ppermute(values, axis, [(i, i ^ mask) for i in range(lax.axis_size(ax...]
    all_to_all x0 -> x4, starting transfers between devices: none -> 16 us  [the longest x2 8.13 us: to_sequences(): lax.all_to_all(values.reshape(4, 2, block, values.shape[1]), 'ctx', 0, 0,...]
    pallas_call x4 -> x2, Pallas kernels: 15.6 us -> 9.47 us  [place(): pl.pallas_call(body, name='place', out_shape=jax.ShapeDtypeStruct((count,...]
    ppermute x41 -> x29, waiting for transfers between devices: 180 us -> 182 us  [swap(): lax.ppermute(values, axis, [(i, i ^ mask) for i in range(lax.axis_size(ax...]
    unnamed x98 -> x84, local copies, waits for them, and re-layouts: 16.2 us -> 16.1 us
  transfers between devices with their start and end apart: 47 -> 39, of which waited for: 20 -> 20; matrix products, arithmetic and copies ran while one was open for 10% -> 9% of each run, Pallas kernels for 34% -> 31%
where the time goes in v4:
time: 616 us; the launch traced here: 606 us
  waiting for transfers between devices  231 us (38%)
  Pallas kernels  217 us (35%)
  starting transfers between devices  52.9 us (9%)
  local copies, waits for them, and re-layouts  39.2 us (6%)
  other arithmetic  35.3 us (6%)
  between operations  22.9 us (4%)
  matrix products  6.96 us (1%)
    ppermute x29, waiting for transfers between devices, swap(): lax.ppermute(values, axis, [(i, i ^ mask) for i in range(lax.axis_size(ax...  182 us
    pallas_call x4, Pallas kernels, grad_pair(): pl.pallas_call(body, name='grad_pair', grid_spec=pltpu.PrefetchScalarGrid...  49.9 us
    ppermute x29, starting transfers between devices, swap(): lax.ppermute(values, axis, [(i, i ^ mask) for i in range(lax.axis_size(ax...  27.9 us
    all_to_all x1, waiting for transfers between devices, local_by_head(): qkv_rows = lax.all_to_all(with_totals(qkv_mine), 'fsdp', 0, 0, tiled=True)  27.3 us
    pallas_call x1, Pallas kernels, norm_back(): pl.pallas_call(body, name='norm_back', grid=(group // block,), in_specs=[...  26.3 us
    pallas_call x2, Pallas kernels, contract(): pl.pallas_call(body, name='contract', grid=(group // block,), in_specs=[r...  25.1 us
    pallas_call x4, Pallas kernels, finish(): pl.pallas_call(body, name='finish', out_shape=jax.ShapeDtypeStruct(shape,...  19.2 us
    pallas_call x1, Pallas kernels, project(): pl.pallas_call(body, name='project', grid=(group // block,), in_specs=[ro...  17.7 us
  transfers between devices with their start and end apart: 39, of which 20 were waited for; matrix products, arithmetic and copies ran while one was open for 9% of the time, Pallas kernels for 31%

profile of v4, /device:TPU:0, one launch (start us, length us, event | category | flops | bytes accessed | tf_op | source)
XLA Modules:
  0.0 605.6 jit_solution(8320251845689178129)
XLA Ops:
  15.6 3.8 cut_weights.1
  19.3 3.1 collective-permute-start
  25.0 18.6 %collective-permute-done = bf16[2,64,1920]{2,1,0:T(8,128)(2,1)S(1)} collective-permute-done((bf16[2,64,1920]{2,1,0:T(8,128)(2,1)}, bf16[2,64,1920]{2,1,0:T(8,128)(2,1)S(1)}, u32[]{:S(2)}, u32[]{:S(2)}) %collective-permute-start) | collective-permute-done | bytes 491552 | tf_op jit(solution)/shard_map/ppermute | solution.py:304
  43.6 15.1 %collective-permute-done.1 = bf16[2,64,1920]{2,1,0:T(8,128)(2,1)S(1)} collective-permute-done((bf16[2,64,1920]{2,1,0:T(8,128)(2,1)}, bf16[2,64,1920]{2,1,0:T(8,128)(2,1)S(1)}, u32[]{:S(2)}, u32[]{:S(2)}) %collective-permute-start.1) | collective-permute-done | bytes 491552 | tf_op jit(solution)/shard_map/ppermute | solution.py:304
  87.7 10.5 %collective-permute-done.4 = s32[2,2,256]{2,1,0:T(2,128)S(1)} collective-permute-done((s32[2,2,256]{2,1,0:T(2,128)S(1)}, s32[2,2,256]{2,1,0:T(2,128)S(1)}, u32[]{:S(2)}, u32[]{:S(2)}) %collective-permute-start.4) | collective-permute-done | bytes 4128 | tf_op jit(solution)/shard_map/ppermute | solution.py:304
  101.6 4.7 fusion.19
  106.4 4.0 fusion.21
  111.3 13.1 %collective-permute-done.7.refs_1_ = bf16[8,64,1024]{2,1,0:T(8,128)(2,1)S(1)} collective-permute-done((bf16[8,64,1024]{2,1,0:T(8,128)(2,1)S(1)}, bf16[8,64,1024]{2,1,0:T(8,128)(2,1)S(1)}, u32[]{:S(2)}, u32[]{:S(2)}) %collective-permute-start.7) | collective-permute-done | bytes 1048608 | tf_op jit(solution)/shard_map/ppermute | solution.py:304
  126.5 2.9 fusion.14
  129.4 9.8 %collective-permute-done.12.refs_3_ = bf16[8,64,768]{2,1,0:T(8,128)(2,1)S(1)} collective-permute-done((bf16[8,64,768]{2,1,0:T(8,128)(2,1)}, bf16[8,64,768]{2,1,0:T(8,128)(2,1)S(1)}, u32[]{:S(2)}, u32[]{:S(2)}) %collective-permute-start.12) | collective-permute-done | bytes 786464 | tf_op jit(solution)/shard_map/ppermute | solution.py:304
  140.1 4.2 place.3
  147.0 5.3 place.2
  152.3 17.7 %project.1 = (bf16[2048,2048]{1,0:T(8,128)(2,1)}, bf16[2048,2048]{1,0:T(8,128)(2,1)}, bf16[2048,768]{1,0:T(8,128)(2,1)}) custom-call(bf16[2048,2048]{1,0:T(8,128)(2,1)} %all-gather.3.cloned.1.call-done.x_ref, bf16[2048,768]{1,0:T(8,128)(2,1)} %bitcast.134, f32[1,768]{1,0:T(1,128)} %bitcast.159, f32[4,2048]{1,0:T(4,128)} %pad_maximum_fusion.9.n_ref.g_ref, ...), custom_call_target="tpu_custom_call" | custom-call | flops 1 | bytes 1 | tf_op jit(solution)/shard_map/project/pallas_call | solution.py:523
  170.0 4.3 all-to-all-start
  176.2 16.8 %expand.1 = (bf16[2048,1024]{1,0:T(8,128)(2,1)}, bf16[2048,1024]{1,0:T(8,128)(2,1)}) custom-call(bf16[2048,2048]{1,0:T(8,128)(2,1)} %get-tuple-element.77.s_ref.a_ref.b_ref, bf16[2048,1024]{1,0:T(8,128)(2,1)} %bitcast.132, f32[1,1024]{1,0:T(1,128)} %bitcast.157), custom_call_target="tpu_custom_call" | custom-call | flops 1 | bytes 1 | tf_op jit(solution)/shard_map/expand/pallas_call | solution.py:551
  193.0 14.1 %contract.2.refs_0_ = bf16[2048,2048]{1,0:T(8,128)(2,1)} custom-call(bf16[2048,1024]{1,0:T(8,128)(2,1)} %get-tuple-element.78.left_ref.a_ref.b_ref, bf16[1024,2048]{1,0:T(8,128)(2,1)} %w_ref.1), custom_call_target="tpu_custom_call" | custom-call | flops 1 | bytes 1 | tf_op jit(solution)/shard_map/contract/pallas_call | solution.py:574
  209.6 8.3 %attend.1 = bf16[4,2,256,256]{3,2,1,0:T(8,128)(2,1)} custom-call(s32[2,1,1024]{2,1,0:T(1,128)} %get-tuple-element.160.row_ref, s32[2,1024,1]{2,1,0:T(8,128)} %broadcast_in_dim_squeeze.4.col_ref, bf16[4,2,256,768]{3,2,1,0:T(8,128)(2,1)} %copy-done.2), custom_call_target="tpu_custom_call" | custom-call | flops 1 | bytes 1 | tf_op jit(solution)/shard_map/attend/pallas_call | solution.py:737
  217.9 3.7 all-to-all-start.1
  221.5 10.0 %all-gather.5.cloned.1.call-done.right_ref.g_ref = bf16[2048,2048]{1,0:T(8,128)(2,1)} async-done(((bf16[256,2048]{1,0:T(8,128)(2,1)}), bf16[2048,2048]{1,0:T(8,128)(2,1)}) %all-gather.5.cloned.1.call-update) | async-done | bytes 8388624 | tf_op jit(solution)/shard_map/all_gather | solution.py:906
  231.5 6.8 %convolution_convert_fusion = bf16[2048,256]{1,0:T(8,128)(2,1)} fusion(bf16[2048,2048]{1,0:T(8,128)(2,1)} %all-gather.5.cloned.1.call-done.right_ref.g_ref, bf16[256,2048]{1,0:T(8,128)(2,1)S(1)} %copy-done.16), kind=kOutput, calls=%fused_computation.8 | convolution fusion | flops 2148007936 | bytes 10485760 | tf_op jit(solution)/shard_map/dot_general | solution.py:300
  238.3 3.8 all-to-all-start.2
  243.4 11.0 %contract.3 = bf16[2048,2048]{1,0:T(8,128)(2,1)} custom-call(bf16[2048,256]{1,0:T(8,128)(2,1)} %bitcast.137, bf16[256,2048]{1,0:T(8,128)(2,1)} %weight_ref.3, bf16[2048,2048]{1,0:T(8,128)(2,1)} %contract.2.refs_0_), custom_call_target="tpu_custom_call" | custom-call | flops 1 | bytes 1 | tf_op jit(solution)/shard_map/contract/pallas_call | solution.py:574
  254.4 7.0 %grad_pair.4 = (bf16[1,2,64,2048]{3,2,1,0:T(8,128)(2,1)}, bf16[1,2,64,2048]{3,2,1,0:T(8,128)(2,1)}) custom-call(s32[1]{0:T(128)} %bitcast.24.keep_ref.bit_ref, s32[1]{0:T(128)} %bitcast.25.send_ref, bf16[2048,256]{1,0:T(8,128)(2,1)} %bitcast.138, bf16[2048,256]{1,0:T(8,128)(2,1)} %bitcast.139, bf16[2048,2048]{1,0:T(8,128)(2,1)} %all-gather.5.cloned.1.call-done.right_ref.g_ref), custom_call_target="tpu_custom_call" | custom-call | flops 1 | bytes 1 | tf_op jit(solution)/shard_map/grad_pair/pallas_call | solution.py:629
  262.4 13.7 %attend_back.1 = bf16[4,2,256,768]{3,2,1,0:T(8,128)(2,1)} custom-call(s32[2,1,1024]{2,1,0:T(1,128)} %get-tuple-element.160.row_ref, s32[2,1024,1]{2,1,0:T(8,128)} %broadcast_in_dim_squeeze.4.col_ref, f32[2,1024,128]{2,1,0:T(8,128)} %bitcast.143, f32[2,1024,128]{2,1,0:T(8,128)} %bitcast.142, f32[2,1024,128]{2,1,0:T(8,128)} %bitcast.141, ...), custom_call_target="tpu_custom_call" | custom-call | flops 1 | bytes 1 | tf_op jit(solution)/shard_map/attend_back/pallas_call | solution.py:797
  276.2 4.2 all-to-all-start.3
  281.3 15.7 %hidden_back.1 = (bf16[2048,1024]{1,0:T(8,128)(2,1)}, f32[1,1024]{1,0:T(1,128)}) custom-call(bf16[2048,2048]{1,0:T(8,128)(2,1)} %all-gather.5.cloned.1.call-done.right_ref.g_ref, bf16[1024,2048]{1,0:T(8,128)(2,1)} %w_ref.1, bf16[2048,1024]{1,0:T(8,128)(2,1)} %get-tuple-element.88.s_ref), custom_call_target="tpu_custom_call" | custom-call | flops 1 | bytes 1 | tf_op jit(solution)/shard_map/hidden_back/pallas_call | solution.py:600
  297.0 15.1 %grad_pair.5 = (bf16[4,1,128,2048]{3,2,1,0:T(8,128)(2,1)}, bf16[4,1,128,2048]{3,2,1,0:T(8,128)(2,1)}) custom-call(s32[4]{0:T(128)} %get-tuple-element.186.keep_ref, s32[4]{0:T(128)} %get-tuple-element.187.send_ref, bf16[2048,1024]{1,0:T(8,128)(2,1)} %get-tuple-element.78.left_ref.a_ref.b_ref, bf16[2048,1024]{1,0:T(8,128)(2,1)} %get-tuple-element.78.left_ref.a_ref.b_ref, ...), custom_call_target="tpu_custom_call" | custom-call | flops 1 | bytes 1 | tf_op jit(solution)/shard_map/grad_pair/pallas_call | solution.py:629
  316.9 14.7 %grad_pair.6 = (bf16[8,2,64,1024]{3,2,1,0:T(8,128)(2,1)}, bf16[8,2,64,1024]{3,2,1,0:T(8,128)(2,1)}) custom-call(s32[8]{0:T(128)} %stack.213.keep_ref, s32[8]{0:T(128)} %stack.221.send_ref, bf16[2048,2048]{1,0:T(8,128)(2,1)} %get-tuple-element.77.s_ref.a_ref.b_ref, bf16[2048,2048]{1,0:T(8,128)(2,1)} %get-tuple-element.77.s_ref.a_ref.b_ref, ...), custom_call_target="tpu_custom_call" | custom-call | flops 1 | bytes 1 | tf_op jit(solution)/shard_map/grad_pair/pallas_call | solution.py:629
  335.1 13.1 %grad_pair.7 = (bf16[8,2,64,768]{3,2,1,0:T(8,128)(2,1)}, bf16[8,2,64,768]{3,2,1,0:T(8,128)(2,1)}) custom-call(s32[8]{0:T(128)} %stack.196.keep_ref, s32[8]{0:T(128)} %stack.205.send_ref, bf16[2048,2048]{1,0:T(8,128)(2,1)} %get-tuple-element.93.a_ref.b_ref, bf16[2048,2048]{1,0:T(8,128)(2,1)} %get-tuple-element.93.a_ref.b_ref, bf16[2048,768]{1,0:T(8,128)(2,1)} %bitcast.130), custom_call_target="tpu_custom_call" | custom-call | flops 1 | bytes 1 | tf_op jit(solution)/shard_map/grad_pair/pallas_call | solution.py:629
  348.2 14.8 %collective-permute-done.13.b_ref = bf16[1,2,256,2048]{3,2,1,0:T(8,128)(2,1)} collective-permute-done((bf16[1,2,256,2048]{3,2,1,0:T(8,128)(2,1)}, bf16[1,2,256,2048]{3,2,1,0:T(8,128)(2,1)}, u32[]{:S(2)}, u32[]{:S(2)}) %collective-permute-start.13) | collective-permute-done | bytes 2097184 | tf_op jit(solution)/shard_map/ppermute | solution.py:304
  363.0 4.0 add_split.2
  368.4 26.3 %norm_back.1 = (bf16[2048,2048]{1,0:T(8,128)(2,1)}, f32[4,2048]{1,0:T(4,128)}) custom-call(bf16[2048,2048]{1,0:T(8,128)(2,1)} %all-gather.3.cloned.1.call-done.x_ref, bf16[2048,768]{1,0:T(8,128)(2,1)} %bitcast.131, bf16[2048,1024]{1,0:T(8,128)(2,1)} %get-tuple-element.94.right_ref.h_ref, bf16[2048,768]{1,0:T(8,128)(2,1)} %bitcast.135, ...), custom_call_target="tpu_custom_call" | custom-call | flops 1 | bytes 1 | tf_op jit(solution)/shard_map/norm_back/pallas_call | solution.py:836
  394.7 4.5 add_split_two.1
  405.4 27.3 %collective-permute-done.19 = bf16[10,64,1024]{2,1,0:T(8,128)(2,1)S(1)} collective-permute-done((bf16[10,64,1024]{2,1,0:T(8,128)(2,1)}, bf16[10,64,1024]{2,1,0:T(8,128)(2,1)S(1)}, u32[]{:S(2)}, u32[]{:S(2)}) %collective-permute-start.19) | collective-permute-done | bytes 1310752 | tf_op jit(solution)/shard_map/ppermute | solution.py:304
  436.3 5.0 all-to-all-start.5
  441.3 3.1 add_convert_fusion.1.refs_0_
  448.5 21.8 %collective-permute-done.21.refs_2_ = bf16[1,256,2048]{2,1,0:T(8,128)(2,1)} collective-permute-done((bf16[1,256,2048]{2,1,0:T(8,128)(2,1)}, bf16[1,256,2048]{2,1,0:T(8,128)(2,1)}, u32[]{:S(2)}, u32[]{:S(2)}) %collective-permute-start.21) | collective-permute-done | bytes 1048608 | tf_op jit(solution)/shard_map/ppermute | solution.py:304
  474.8 10.4 %all-to-all-done.5 = bf16[8,64,1024]{2,1,0:T(8,128)(2,1)} async-done(((bf16[8,64,1024]{2,1,0:T(8,128)(2,1)}), bf16[8,64,1024]{2,1,0:T(8,128)(2,1)}, u32[]{:S(2)}, u32[]{:S(2)}) %all-to-all-start.5) | async-done | bytes 1048608 | tf_op jit(solution)/shard_map/all_to_all | solution.py:1028
  485.2 3.6 all-to-all-start.4
  488.8 6.7 %collective-permute-done.22.refs_3_ = bf16[1,256,2048]{2,1,0:T(8,128)(2,1)} collective-permute-done((bf16[1,256,2048]{2,1,0:T(8,128)(2,1)}, bf16[1,256,2048]{2,1,0:T(8,128)(2,1)}, u32[]{:S(2)}, u32[]{:S(2)}) %collective-permute-start.22) | collective-permute-done | bytes 1048608 | tf_op jit(solution)/shard_map/ppermute | solution.py:304
  498.2 27.3 %all-to-all-done.4 = bf16[8,72,768]{2,1,0:T(8,128)(2,1)S(1)} async-done(((bf16[8,72,768]{2,1,0:T(8,128)(2,1)}), bf16[8,72,768]{2,1,0:T(8,128)(2,1)S(1)}, u32[]{:S(2)}, u32[]{:S(2)}) %all-to-all-start.4) | async-done | bytes 884768 | tf_op jit(solution)/shard_map/all_to_all | solution.py:1030
  528.8 20.3 %collective-permute-done.25.refs_2_ = bf16[9,64,768]{2,1,0:T(8,128)(2,1)} collective-permute-done((bf16[9,64,768]{2,1,0:T(8,128)(2,1)S(1)}, bf16[9,64,768]{2,1,0:T(8,128)(2,1)}, u32[]{:S(2)}, u32[]{:S(2)}) %collective-permute-start.25) | collective-permute-done | bytes 884768 | tf_op jit(solution)/shard_map/ppermute | solution.py:304
  553.2 5.4 finish.4
  558.6 16.8 %collective-permute-done.28.refs_3_ = bf16[10,64,1024]{2,1,0:T(8,128)(2,1)} collective-permute-done((bf16[10,64,1024]{2,1,0:T(8,128)(2,1)}, bf16[10,64,1024]{2,1,0:T(8,128)(2,1)}, u32[]{:S(2)}, u32[]{:S(2)}) %collective-permute-start.28) | collective-permute-done | bytes 1310752 | tf_op jit(solution)/shard_map/ppermute | solution.py:304
  575.5 3.0 finish.5
  583.2 4.1 fusion.6
  587.3 5.4 finish.6
  592.8 5.3 finish.7
  (251 shorter events, 92.5 us)
Async XLA Ops:
  7.2 145.1 %all-gather.3.cloned.1.call-start = ((), (), s32[]{:S(2)}) async-start(), calls=%async_computation.8 | async-start | bytes 9437184 | tf_op jit(solution)/shard_map/all_gather | solution.py:904
  19.3 24.3 %collective-permute-start = (bf16[2,64,1920]{2,1,0:T(8,128)(2,1)}, bf16[2,64,1920]{2,1,0:T(8,128)(2,1)S(1)}, u32[]{:S(2)}, u32[]{:S(2)}) collective-permute-start(bf16[2,64,1920]{2,1,0:T(8,128)(2,1)} %get-tuple-element.70), channel_id=1, source_target_pairs={{0,2},{1,3},{2,0},{3,1},{4,6},{5,7},{6,4},{7,5},{8,10},{9,11},{10,... | collective-permute-start | bytes 1474568 | tf_op jit(solution)/shard_map/ppermute | solution.py:304
  22.4 36.3 %collective-permute-start.1 = (bf16[2,64,1920]{2,1,0:T(8,128)(2,1)}, bf16[2,64,1920]{2,1,0:T(8,128)(2,1)S(1)}, u32[]{:S(2)}, u32[]{:S(2)}) collective-permute-start(bf16[2,64,1920]{2,1,0:T(8,128)(2,1)} %get-tuple-element.71), channel_id=1, source_target_pairs={{0,4},{1,5},{2,6},{3,7},{4,0},{5,1},{6,2},{7,3},{8,12},{9,13},{10,... | collective-permute-start | bytes 1474568 | tf_op jit(solution)/shard_map/ppermute | solution.py:304
  25.0 33.7 %collective-permute-start.2 = (bf16[2,64,1920]{2,1,0:T(8,128)(2,1)}, bf16[2,64,1920]{2,1,0:T(8,128)(2,1)S(1)}, u32[]{:S(2)}, u32[]{:S(2)}) collective-permute-start(bf16[2,64,1920]{2,1,0:T(8,128)(2,1)} %get-tuple-element.72), channel_id=1, source_target_pairs={{0,6},{1,7},{2,4},{3,5},{4,2},{5,3},{6,0},{7,1},{8,14},{9,15},{10,... | collective-permute-start | bytes 1474568 | tf_op jit(solution)/shard_map/ppermute | solution.py:304
  58.8 172.7 %all-gather.5.cloned.1.call-start = ((), (), s32[]{:S(2)}) async-start(), calls=%async_computation.9 | async-start | bytes 9437184 | tf_op jit(solution)/shard_map/all_gather | solution.py:906
  62.9 2.6 collective-permute-start.3
  65.6 483.8 %copy-start.23 = (s32[4]{0:T(128)}, s32[4]{0:T(128)S(1)}, u32[]{:S(2)}) copy-start(s32[4]{0:T(128)S(1)} %get-tuple-element.185.rows_ref) | copy-start | bytes 52
  77.3 24.3 %copy-start.13 = (bf16[8,64,768]{2,1,0:T(8,128)(2,1)}, bf16[8,64,768]{2,1,0:T(8,128)(2,1)S(1)}, u32[]{:S(2)}) copy-start(bf16[8,64,768]{2,1,0:T(8,128)(2,1)S(1)} %slice.224.refs_0_) | copy-start | bytes 2359300
  77.3 33.4 %collective-permute-start.11 = (bf16[8,64,768]{2,1,0:T(8,128)(2,1)S(1)}, bf16[8,64,768]{2,1,0:T(8,128)(2,1)}, u32[]{:S(2)}, u32[]{:S(2)}) collective-permute-start(bf16[8,64,768]{2,1,0:T(8,128)(2,1)S(1)} %slice.224.refs_0_), channel_id=1, source_target_pairs={{0,16},{8,24},{16,0},{24,8},{1,17},{9,25},{17,1},{25,9},{2,18},{10... | collective-permute-start | bytes 2359304 | tf_op jit(solution)/shard_map/ppermute | solution.py:304
  78.8 50.6 %collective-permute-start.10 = (bf16[8,64,768]{2,1,0:T(8,128)(2,1)S(1)}, bf16[8,64,768]{2,1,0:T(8,128)(2,1)}, u32[]{:S(2)}, u32[]{:S(2)}) collective-permute-start(bf16[8,64,768]{2,1,0:T(8,128)(2,1)S(1)} %slice.224.refs_0_), channel_id=1, source_target_pairs={{0,8},{8,0},{16,24},{24,16},{1,9},{9,1},{17,25},{25,17},{2,10},{10... | collective-permute-start | bytes 2359304 | tf_op jit(solution)/shard_map/ppermute | solution.py:304
  81.4 16.8 %collective-permute-start.4 = (s32[2,2,256]{2,1,0:T(2,128)S(1)}, s32[2,2,256]{2,1,0:T(2,128)S(1)}, u32[]{:S(2)}, u32[]{:S(2)}) collective-permute-start(s32[2,2,256]{2,1,0:T(2,128)S(1)} %bitcast.163), channel_id=1, source_target_pairs={{0,8},{8,0},{16,24},{24,16},{1,9},{9,1},{17,25},{25,17},{2,10},{10... | collective-permute-start | bytes 12296 | tf_op jit(solution)/shard_map/ppermute | solution.py:304
  82.1 17.7 %collective-permute-start.5 = (s32[2,2,256]{2,1,0:T(2,128)S(1)}, s32[2,2,256]{2,1,0:T(2,128)S(1)}, u32[]{:S(2)}, u32[]{:S(2)}) collective-permute-start(s32[2,2,256]{2,1,0:T(2,128)S(1)} %bitcast.162), channel_id=1, source_target_pairs={{0,16},{8,24},{16,0},{24,8},{1,17},{9,25},{17,1},{25,9},{2,18},{10... | collective-permute-start | bytes 12296 | tf_op jit(solution)/shard_map/ppermute | solution.py:304
  82.7 17.6 %collective-permute-start.6 = (s32[2,2,256]{2,1,0:T(2,128)S(1)}, s32[2,2,256]{2,1,0:T(2,128)S(1)}, u32[]{:S(2)}, u32[]{:S(2)}) collective-permute-start(s32[2,2,256]{2,1,0:T(2,128)S(1)} %bitcast.161), channel_id=1, source_target_pairs={{0,24},{8,16},{16,8},{24,0},{1,25},{9,17},{17,9},{25,1},{2,26},{10... | collective-permute-start | bytes 12296 | tf_op jit(solution)/shard_map/ppermute | solution.py:304
  87.7 18.7 %copy-start.10 = (bf16[8,64,1024]{2,1,0:T(8,128)(2,1)}, bf16[8,64,1024]{2,1,0:T(8,128)(2,1)S(1)}, u32[]{:S(2)}) copy-start(bf16[8,64,1024]{2,1,0:T(8,128)(2,1)S(1)} %slice.223.refs_0_) | copy-start | bytes 3145732
  98.3 26.1 %collective-permute-start.7 = (bf16[8,64,1024]{2,1,0:T(8,128)(2,1)S(1)}, bf16[8,64,1024]{2,1,0:T(8,128)(2,1)S(1)}, u32[]{:S(2)}, u32[]{:S(2)}) collective-permute-start(bf16[8,64,1024]{2,1,0:T(8,128)(2,1)S(1)} %slice.223.refs_0_), channel_id=1, source_target_pairs={{0,8},{8,0},{16,24},{24,16},{1,9},{9,1},{17,25},{25,17},{2,10},{10... | collective-permute-start | bytes 3145736 | tf_op jit(solution)/shard_map/ppermute | solution.py:304
  99.7 44.5 %collective-permute-start.8 = (bf16[8,64,1024]{2,1,0:T(8,128)(2,1)S(1)}, bf16[8,64,1024]{2,1,0:T(8,128)(2,1)}, u32[]{:S(2)}, u32[]{:S(2)}) collective-permute-start(bf16[8,64,1024]{2,1,0:T(8,128)(2,1)S(1)} %slice.223.refs_0_), channel_id=1, source_target_pairs={{0,16},{8,24},{16,0},{24,8},{1,17},{9,25},{17,1},{25,9},{2,18},{10... | collective-permute-start | bytes 3145736 | tf_op jit(solution)/shard_map/ppermute | solution.py:304
  110.7 28.5 %collective-permute-start.12 = (bf16[8,64,768]{2,1,0:T(8,128)(2,1)}, bf16[8,64,768]{2,1,0:T(8,128)(2,1)S(1)}, u32[]{:S(2)}, u32[]{:S(2)}) collective-permute-start(bf16[8,64,768]{2,1,0:T(8,128)(2,1)} %collective-permute-done.11.refs_2_), channel_id=1, source_target_pairs={{0,8},{8,0},{16,24},{24,16},{1,9},{9,1},{17,25},{25,17},{2,10},{10... | collective-permute-start | bytes 2359304 | tf_op jit(solution)/shard_map/ppermute | solution.py:304
  124.4 21.6 %collective-permute-start.9 = (bf16[8,64,1024]{2,1,0:T(8,128)(2,1)S(1)}, bf16[8,64,1024]{2,1,0:T(8,128)(2,1)S(1)}, u32[]{:S(2)}, u32[]{:S(2)}) collective-permute-start(bf16[8,64,1024]{2,1,0:T(8,128)(2,1)S(1)} %collective-permute-done.7.refs_1_), channel_id=1, source_target_pairs={{0,16},{8,24},{16,0},{24,8},{1,17},{9,25},{17,1},{25,9},{2,18},{10... | collective-permute-start | bytes 3145736 | tf_op jit(solution)/shard_map/ppermute | solution.py:304
  170.0 38.0 %all-to-all-start = ((bf16[4,2,256,768]{3,2,1,0:T(8,128)(2,1)}), bf16[4,2,256,768]{3,2,1,0:T(8,128)(2,1)S(1)}, u32[]{:S(2)}, u32[]{:S(2)}) async-start(bf16[4,2,256,768]{3,2,1,0:T(8,128)(2,1)} %bitcast.144), calls=%async_computation | async-start | bytes 6291456 | tf_op jit(solution)/shard_map/all_to_all | solution.py:944
  217.9 20.4 %all-to-all-start.1 = ((bf16[4,2,256,256]{3,2,1,0:T(8,128)(2,1)}), bf16[4,2,256,256]{3,2,1,0:T(8,128)(2,1)S(1)}, u32[]{:S(2)}, u32[]{:S(2)}) async-start(bf16[4,2,256,256]{3,2,1,0:T(8,128)(2,1)} %attend.1), calls=%async_computation.1 | async-start | bytes 2097152 | tf_op jit(solution)/shard_map/all_to_all | solution.py:949
  238.3 23.1 %all-to-all-start.2 = ((bf16[4,2,256,256]{3,2,1,0:T(8,128)(2,1)}), bf16[4,2,256,256]{3,2,1,0:T(8,128)(2,1)S(1)}, u32[]{:S(2)}, u32[]{:S(2)}) async-start(bf16[4,2,256,256]{3,2,1,0:T(8,128)(2,1)} %bitcast.146), calls=%async_computation.2 | async-start | bytes 2097152 | tf_op jit(solution)/shard_map/all_to_all | solution.py:944
  242.1 162.1 %reduce-scatter.3.cloned.1.call-start = ((), (), s32[]{:S(2)}) async-start(), calls=%async_computation.10 | async-start | bytes 9437184 | tf_op jit(solution)/shard_map/reduce_scatter | solution.py:969
  276.2 57.3 %all-to-all-start.3 = ((bf16[4,2,256,768]{3,2,1,0:T(8,128)(2,1)}), bf16[4,2,256,768]{3,2,1,0:T(8,128)(2,1)S(1)}, u32[]{:S(2)}, u32[]{:S(2)}) async-start(bf16[4,2,256,768]{3,2,1,0:T(8,128)(2,1)} %attend_back.1), calls=%async_computation.4 | async-start | bytes 6291456 | tf_op jit(solution)/shard_map/all_to_all | solution.py:949
  280.4 300.8 %reduce-scatter.5.cloned.1.call-start = ((), (), s32[]{:S(2)}) async-start(), calls=%async_computation.11 | async-start | bytes 9437184 | tf_op jit(solution)/shard_map/reduce_scatter | solution.py:1016
  312.1 50.9 %collective-permute-start.13 = (bf16[1,2,256,2048]{3,2,1,0:T(8,128)(2,1)}, bf16[1,2,256,2048]{3,2,1,0:T(8,128)(2,1)}, u32[]{:S(2)}, u32[]{:S(2)}) collective-permute-start(bf16[1,2,256,2048]{3,2,1,0:T(8,128)(2,1)} %bitcast.164), channel_id=1, source_target_pairs={{0,8},{8,0},{16,24},{24,16},{1,9},{9,1},{17,25},{25,17},{2,10},{10... | collective-permute-start | bytes 6291464 | tf_op jit(solution)/shard_map/ppermute | solution.py:304
  315.4 18.1 %collective-permute-start.14 = (bf16[1,2,64,2048]{3,2,1,0:T(8,128)(2,1)}, bf16[1,2,64,2048]{3,2,1,0:T(8,128)(2,1)}, u32[]{:S(2)}, u32[]{:S(2)}) collective-permute-start(bf16[1,2,64,2048]{3,2,1,0:T(8,128)(2,1)} %get-tuple-element.84), channel_id=1, source_target_pairs={{0,16},{8,24},{16,0},{24,8},{1,17},{9,25},{17,1},{25,9},{2,18},{10... | collective-permute-start | bytes 1572872 | tf_op jit(solution)/shard_map/ppermute | solution.py:304
  331.6 63.2 %collective-permute-start.16 = (bf16[8,2,64,1024]{3,2,1,0:T(8,128)(2,1)}, bf16[8,2,64,1024]{3,2,1,0:T(8,128)(2,1)}, u32[]{:S(2)}, u32[]{:S(2)}) collective-permute-start(bf16[8,2,64,1024]{3,2,1,0:T(8,128)(2,1)} %get-tuple-element.95), channel_id=1, source_target_pairs={{0,16},{8,24},{16,0},{24,8},{1,17},{9,25},{17,1},{25,9},{2,18},{10... | collective-permute-start | bytes 6291464 | tf_op jit(solution)/shard_map/ppermute | solution.py:304
  348.2 52.0 %collective-permute-start.15 = (bf16[8,2,64,768]{3,2,1,0:T(8,128)(2,1)}, bf16[8,2,64,768]{3,2,1,0:T(8,128)(2,1)S(1)}, u32[]{:S(2)}, u32[]{:S(2)}) collective-permute-start(bf16[8,2,64,768]{3,2,1,0:T(8,128)(2,1)} %get-tuple-element.97), channel_id=1, source_target_pairs={{0,8},{8,0},{16,24},{24,16},{1,9},{9,1},{17,25},{25,17},{2,10},{10... | collective-permute-start | bytes 4718600 | tf_op jit(solution)/shard_map/ppermute | solution.py:304
  367.0 33.2 %collective-permute-start.17 = (bf16[1,256,2048]{2,1,0:T(8,128)(2,1)}, bf16[1,256,2048]{2,1,0:T(8,128)(2,1)S(1)}, u32[]{:S(2)}, u32[]{:S(2)}) collective-permute-start(bf16[1,256,2048]{2,1,0:T(8,128)(2,1)} %get-tuple-element.99), channel_id=1, source_target_pairs={{0,16},{8,24},{16,0},{24,8},{1,17},{9,25},{17,1},{25,9},{2,18},{10... | collective-permute-start | bytes 3145736 | tf_op jit(solution)/shard_map/ppermute | solution.py:304
  400.2 33.9 %copy-start.18 = (bf16[1,256,2048]{2,1,0:T(8,128)(2,1)}, bf16[1,256,2048]{2,1,0:T(8,128)(2,1)S(1)}, u32[]{:S(2)}) copy-start(bf16[1,256,2048]{2,1,0:T(8,128)(2,1)S(1)} %collective-permute-done.17) | copy-start | bytes 3145732
  404.2 29.4 %copy-start.15 = (bf16[10,64,1024]{2,1,0:T(8,128)(2,1)S(1)}, bf16[10,64,1024]{2,1,0:T(8,128)(2,1)}, u32[]{:S(2)}) copy-start(bf16[10,64,1024]{2,1,0:T(8,128)(2,1)} %get-tuple-element.117) | copy-start | bytes 3932164
  404.2 28.5 %collective-permute-start.19 = (bf16[10,64,1024]{2,1,0:T(8,128)(2,1)}, bf16[10,64,1024]{2,1,0:T(8,128)(2,1)S(1)}, u32[]{:S(2)}, u32[]{:S(2)}) collective-permute-start(bf16[10,64,1024]{2,1,0:T(8,128)(2,1)} %get-tuple-element.106), channel_id=1, source_target_pairs={{0,8},{8,0},{16,24},{24,16},{1,9},{9,1},{17,25},{25,17},{2,10},{10... | collective-permute-start | bytes 3932168 | tf_op jit(solution)/shard_map/ppermute | solution.py:304
  404.9 27.8 %collective-permute-start.18 = (bf16[8,64,768]{2,1,0:T(8,128)(2,1)}, bf16[8,64,768]{2,1,0:T(8,128)(2,1)S(1)}, u32[]{:S(2)}, u32[]{:S(2)}) collective-permute-start(bf16[8,64,768]{2,1,0:T(8,128)(2,1)} %get-tuple-element.108), channel_id=1, source_target_pairs={{0,16},{8,24},{16,0},{24,8},{1,17},{9,25},{17,1},{25,9},{2,18},{10... | collective-permute-start | bytes 2359304 | tf_op jit(solution)/shard_map/ppermute | solution.py:304
  436.3 48.9 %all-to-all-start.5 = ((bf16[8,64,1024]{2,1,0:T(8,128)(2,1)}), bf16[8,64,1024]{2,1,0:T(8,128)(2,1)}, u32[]{:S(2)}, u32[]{:S(2)}) async-start(bf16[8,64,1024]{2,1,0:T(8,128)(2,1)} %slice.244), calls=%async_computation.7 | async-start | bytes 2097152 | tf_op jit(solution)/shard_map/all_to_all | solution.py:1028
  444.4 25.9 %collective-permute-start.21 = (bf16[1,256,2048]{2,1,0:T(8,128)(2,1)}, bf16[1,256,2048]{2,1,0:T(8,128)(2,1)}, u32[]{:S(2)}, u32[]{:S(2)}) collective-permute-start(bf16[1,256,2048]{2,1,0:T(8,128)(2,1)} %add_convert_fusion.1.refs_0_), channel_id=1, source_target_pairs={{0,16},{8,24},{16,0},{24,8},{1,17},{9,25},{17,1},{25,9},{2,18},{10... | collective-permute-start | bytes 3145736 | tf_op jit(solution)/shard_map/ppermute | solution.py:304
  446.6 25.6 %collective-permute-start.20 = (bf16[1,256,2048]{2,1,0:T(8,128)(2,1)}, bf16[1,256,2048]{2,1,0:T(8,128)(2,1)}, u32[]{:S(2)}, u32[]{:S(2)}) collective-permute-start(bf16[1,256,2048]{2,1,0:T(8,128)(2,1)} %add_convert_fusion.1.refs_0_), channel_id=1, source_target_pairs={{0,8},{8,0},{16,24},{24,16},{1,9},{9,1},{17,25},{25,17},{2,10},{10... | collective-permute-start | bytes 3145736 | tf_op jit(solution)/shard_map/ppermute | solution.py:304
  470.3 25.1 %collective-permute-start.22 = (bf16[1,256,2048]{2,1,0:T(8,128)(2,1)}, bf16[1,256,2048]{2,1,0:T(8,128)(2,1)}, u32[]{:S(2)}, u32[]{:S(2)}) collective-permute-start(bf16[1,256,2048]{2,1,0:T(8,128)(2,1)} %collective-permute-done.21.refs_2_), channel_id=1, source_target_pairs={{0,8},{8,0},{16,24},{24,16},{1,9},{9,1},{17,25},{25,17},{2,10},{10... | collective-permute-start | bytes 3145736 | tf_op jit(solution)/shard_map/ppermute | solution.py:304
  473.8 21.6 %slice-start = ((bf16[10,64,1024]{2,1,0:T(8,128)(2,1)}), bf16[2,64,1024]{2,1,0:T(8,128)(2,1)S(1)}, s32[]{:S(2)}) async-start(bf16[10,64,1024]{2,1,0:T(8,128)(2,1)} %copy-done.7), calls=%async_computation.12 | async-start | bytes 524288 | tf_op jit(solution)/shard_map/slice | solution.py:1032
  485.2 40.3 %all-to-all-start.4 = ((bf16[8,72,768]{2,1,0:T(8,128)(2,1)}), bf16[8,72,768]{2,1,0:T(8,128)(2,1)S(1)}, u32[]{:S(2)}, u32[]{:S(2)}) async-start(bf16[8,72,768]{2,1,0:T(8,128)(2,1)} %fusion.18), calls=%async_computation.6 | async-start | bytes 1769472 | tf_op jit(solution)/shard_map/all_to_all | solution.py:1030
  496.8 55.4 %copy-start.5 = (bf16[10,64,1024]{2,1,0:T(8,128)(2,1)}, bf16[10,64,1024]{2,1,0:T(8,128)(2,1)S(1)}, u32[]{:S(2)}) copy-start(bf16[10,64,1024]{2,1,0:T(8,128)(2,1)S(1)} %pad_maximum_fusion.4.refs_0_) | copy-start | bytes 3932164
  496.8 55.2 %copy-start.3 = (bf16[1,256,2048]{2,1,0:T(8,128)(2,1)S(1)}, bf16[1,256,2048]{2,1,0:T(8,128)(2,1)}, u32[]{:S(2)}) copy-start(bf16[1,256,2048]{2,1,0:T(8,128)(2,1)} %param.17) | copy-start | bytes 3145732
  496.8 29.7 %collective-permute-start.23 = (bf16[10,64,1024]{2,1,0:T(8,128)(2,1)S(1)}, bf16[10,64,1024]{2,1,0:T(8,128)(2,1)}, u32[]{:S(2)}, u32[]{:S(2)}) collective-permute-start(bf16[10,64,1024]{2,1,0:T(8,128)(2,1)S(1)} %pad_maximum_fusion.4.refs_0_), channel_id=1, source_target_pairs={{0,16},{8,24},{16,0},{24,8},{1,17},{9,25},{17,1},{25,9},{2,18},{10... | collective-permute-start | bytes 3932168 | tf_op jit(solution)/shard_map/ppermute | solution.py:304
  497.7 30.0 %collective-permute-start.27 = (bf16[10,64,1024]{2,1,0:T(8,128)(2,1)S(1)}, bf16[10,64,1024]{2,1,0:T(8,128)(2,1)}, u32[]{:S(2)}, u32[]{:S(2)}) collective-permute-start(bf16[10,64,1024]{2,1,0:T(8,128)(2,1)S(1)} %pad_maximum_fusion.4.refs_0_), channel_id=1, source_target_pairs={{0,8},{8,0},{16,24},{24,16},{1,9},{9,1},{17,25},{25,17},{2,10},{10... | collective-permute-start | bytes 3932168 | tf_op jit(solution)/shard_map/ppermute | solution.py:304
  525.7 52.8 %copy-start.12 = (bf16[9,64,768]{2,1,0:T(8,128)(2,1)}, bf16[9,64,768]{2,1,0:T(8,128)(2,1)S(1)}, u32[]{:S(2)}) copy-start(bf16[9,64,768]{2,1,0:T(8,128)(2,1)S(1)} %pad_maximum_fusion.8.refs_0_) | copy-start | bytes 2654212
  526.5 22.7 %collective-permute-start.25 = (bf16[9,64,768]{2,1,0:T(8,128)(2,1)S(1)}, bf16[9,64,768]{2,1,0:T(8,128)(2,1)}, u32[]{:S(2)}, u32[]{:S(2)}) collective-permute-start(bf16[9,64,768]{2,1,0:T(8,128)(2,1)S(1)} %pad_maximum_fusion.8.refs_0_), channel_id=1, source_target_pairs={{0,16},{8,24},{16,0},{24,8},{1,17},{9,25},{17,1},{25,9},{2,18},{10... | collective-permute-start | bytes 2654216 | tf_op jit(solution)/shard_map/ppermute | solution.py:304
  527.7 47.7 %collective-permute-start.28 = (bf16[10,64,1024]{2,1,0:T(8,128)(2,1)}, bf16[10,64,1024]{2,1,0:T(8,128)(2,1)}, u32[]{:S(2)}, u32[]{:S(2)}) collective-permute-start(bf16[10,64,1024]{2,1,0:T(8,128)(2,1)} %collective-permute-done.27.refs_1_), channel_id=1, source_target_pairs={{0,16},{8,24},{16,0},{24,8},{1,17},{9,25},{17,1},{25,9},{2,18},{10... | collective-permute-start | bytes 3932168 | tf_op jit(solution)/shard_map/ppermute | solution.py:304
  528.5 50.0 %collective-permute-start.24 = (bf16[9,64,768]{2,1,0:T(8,128)(2,1)S(1)}, bf16[9,64,768]{2,1,0:T(8,128)(2,1)}, u32[]{:S(2)}, u32[]{:S(2)}) collective-permute-start(bf16[9,64,768]{2,1,0:T(8,128)(2,1)S(1)} %pad_maximum_fusion.8.refs_0_), channel_id=1, source_target_pairs={{0,8},{8,0},{16,24},{24,16},{1,9},{9,1},{17,25},{25,17},{2,10},{10... | collective-permute-start | bytes 2654216 | tf_op jit(solution)/shard_map/ppermute | solution.py:304
  549.2 29.4 %collective-permute-start.26 = (bf16[9,64,768]{2,1,0:T(8,128)(2,1)}, bf16[9,64,768]{2,1,0:T(8,128)(2,1)}, u32[]{:S(2)}, u32[]{:S(2)}) collective-permute-start(bf16[9,64,768]{2,1,0:T(8,128)(2,1)} %collective-permute-done.25.refs_2_), channel_id=1, source_target_pairs={{0,8},{8,0},{16,24},{24,16},{1,9},{9,1},{17,25},{25,17},{2,10},{10... | collective-permute-start | bytes 2654216 | tf_op jit(solution)/shard_map/ppermute | solution.py:304
  (20 other events, 87.1 us)
Sparse Core Ops, SparseCore 0:
  58.9 90.3 all-gather.2
  150.9 80.5 all-gather.4
  276.3 93.9 reduce-scatter.2
  404.4 121.6 reduce-scatter.4

commit v5 on v4

--- a/solution.py
+++ b/solution.py
@@ -815,13 +815,16 @@
     )(seg_row, seg_col, *tables, parts, d_parts)
 
 
-def norm_back(x_all, d_packed, d_hidden, w_qkv, w_in, gains, block):
+def norm_back(x_all, d_packed, d_hidden, w_qkv, w_in, gains, block, half, before=()):
     group, width = x_all.shape
-
-    def body(x_ref, p_ref, h_ref, w1_ref, w2_ref, g_ref, out_ref, sums_ref):
+    steps = group // block // 2
+
+    def body(x_ref, p_ref, h_ref, w1_ref, w2_ref, g_ref, *refs):
+        out_ref, sums_ref = refs[-2:]
+
         @pl.when(pl.program_id(0) == 0)
         def _():
-            sums_ref[...] = jnp.zeros_like(sums_ref)
+            sums_ref[...] = refs[1][...] if before else jnp.zeros_like(sums_ref)
 
         normal, _ = normalised(x_ref[...].astype(wide))
         one = dot(p_ref[...], w1_ref[...], 1, 1)
@@ -832,20 +835,22 @@
         sums_ref[2:3] += jnp.sum(two * normal, axis=0, keepdims=True)
         sums_ref[3:4] += jnp.sum(two, axis=0, keepdims=True)
 
-    row = lambda n: pl.BlockSpec((block, n), lambda i: (i, 0))
+    row = lambda n: pl.BlockSpec((block, n), lambda i: (i + half * steps, 0))
     return pl.pallas_call(
         body,
         name="norm_back",
-        grid=(group // block,),
-        in_specs=[row(width), row(d_packed.shape[1]), row(d_hidden.shape[1])] + [WHOLE] * 3,
+        grid=(steps,),
+        in_specs=[row(width), row(d_packed.shape[1]), row(d_hidden.shape[1])] + [WHOLE] * 3
+        + ([ANY, WHOLE] if before else []),
         out_specs=[row(width), pl.BlockSpec((4, width), lambda i: (0, 0))],
         out_shape=[
             jax.ShapeDtypeStruct((group, width), low),
             jax.ShapeDtypeStruct((4, width), wide),
         ],
-        compiler_params=FAST,
-        cost_estimate=SMALL,
-    )(x_all, d_packed, d_hidden, w_qkv, w_in, gains)
+        input_output_aliases={6: 0} if before else {},
+        compiler_params=FAST,
+        cost_estimate=SMALL,
+    )(x_all, d_packed, d_hidden, w_qkv, w_in, gains, *before)
 
 
 def local_by_head(
@@ -987,10 +992,11 @@
     to_x = [2 * f + x_bit for f in range(nf)], [2 * f + 1 - x_bit for f in range(nf)]
     qkv_kept, qkv_sent = grad_pair(first, then(d_packed, in_sent, dense_got), *to_x, 2)
     qkv_got = swap(qkv_sent, "ctx", 1)
-    rows_kept, rows_sent = add_split(out_kept, then(out_got, qkv_sent), y_bit)
+    d_half = norm_back(then(x_all, qkv_sent), d_packed, d_hidden, w_qkv, w_in, norms, block, 0)
+    rows_kept, rows_sent = add_split(out_kept, then(out_got, d_half[0]), y_bit)
     rows_got = swap(rows_sent, "ctx", 2)
     d_partial, sums = norm_back(
-        then(x_all, rows_sent), d_packed, d_hidden, w_qkv, w_in, norms, block
+        then(x_all, rows_sent), d_packed, d_hidden, w_qkv, w_in, norms, block, 1, d_half
     )
     def spread_out(values, parts):
         whole = jnp.zeros((parts, nf, values.shape[0] // parts), wide)
@@ -1011,10 +1017,10 @@
         in_kept, then(in_got, d_partial), dense_kept, dense_got, x_bit
     )
     both_got = swap(both_sent, "ctx", 1)
-    qkv_kept2, qkv_sent2 = add_split(qkv_kept, then(qkv_got, both_sent, rows_got), y_bit)
+    qkv_kept2, qkv_sent2 = add_split(qkv_kept, then(qkv_got, both_sent), y_bit)
     qkv_got2 = swap(qkv_sent2, "ctx", 2)
     d_normal = lax.psum_scatter(
-        then(d_partial, summed, qkv_sent2), "fsdp", scatter_dimension=0, tiled=True
+        then(d_partial, summed, qkv_sent2, rows_got), "fsdp", scatter_dimension=0, tiled=True
     )
 
     def with_totals(values):

time: 616 us -> 614 us (level)
  waiting for transfers between devices: 231 us -> 221 us
    ppermute x29, waiting for transfers between devices: 182 us -> 175 us  [swap(): lax.ppermute(values, axis, [(i, i ^ mask) for i in range(lax.axis_size(ax...]
    pallas_call x1 -> x2, Pallas kernels: 26.3 us -> 31.1 us  [norm_back(): pl.pallas_call(body, name='norm_back', grid=(steps,), in_specs=[row(width...]
  transfers between devices with their start and end apart: 39 -> 39, of which waited for: 20 -> 20; matrix products, arithmetic and copies ran while one was open for 9% -> 9% of each run, Pallas kernels for 31% -> 32%
where the time goes in v5:
time: 614 us; the launch traced here: 603 us
  Pallas kernels  222 us (36%)
  waiting for transfers between devices  221 us (36%)
  starting transfers between devices  55.5 us (9%)
  local copies, waits for them, and re-layouts  39.9 us (6%)
  other arithmetic  35.2 us (6%)
  between operations  22.9 us (4%)
  matrix products  6.96 us (1%)
    ppermute x29, waiting for transfers between devices, swap(): lax.ppermute(values, axis, [(i, i ^ mask) for i in range(lax.axis_size(ax...  175 us
    pallas_call x4, Pallas kernels, grad_pair(): pl.pallas_call(body, name='grad_pair', grid_spec=pltpu.PrefetchScalarGrid...  49.9 us
    pallas_call x2, Pallas kernels, norm_back(): pl.pallas_call(body, name='norm_back', grid=(steps,), in_specs=[row(width...  31.1 us
    ppermute x29, starting transfers between devices, swap(): lax.ppermute(values, axis, [(i, i ^ mask) for i in range(lax.axis_size(ax...  29.9 us
    all_to_all x1, waiting for transfers between devices, local_by_head(): qkv_rows = lax.all_to_all(with_totals(qkv_mine), 'fsdp', 0, 0, tiled=True)  25.8 us
    pallas_call x2, Pallas kernels, contract(): pl.pallas_call(body, name='contract', grid=(group // block,), in_specs=[r...  25.1 us
    pallas_call x4, Pallas kernels, finish(): pl.pallas_call(body, name='finish', out_shape=jax.ShapeDtypeStruct(shape,...  19.2 us
    pallas_call x1, Pallas kernels, project(): pl.pallas_call(body, name='project', grid=(group // block,), in_specs=[ro...  17.7 us
  transfers between devices with their start and end apart: 39, of which 20 were waited for; matrix products, arithmetic and copies ran while one was open for 9% of the time, Pallas kernels for 32%

profile of v5, /device:TPU:0, one launch (start us, length us, event | category | flops | bytes accessed | tf_op | source)
XLA Modules:
  0.0 603.5 jit_solution(7461389886417995705)
XLA Ops:
  15.6 3.8 cut_weights.1
  19.3 3.1 collective-permute-start
  25.0 18.6 %collective-permute-done = bf16[2,64,1920]{2,1,0:T(8,128)(2,1)S(1)} collective-permute-done((bf16[2,64,1920]{2,1,0:T(8,128)(2,1)}, bf16[2,64,1920]{2,1,0:T(8,128)(2,1)S(1)}, u32[]{:S(2)}, u32[]{:S(2)}) %collective-permute-start) | collective-permute-done | bytes 491552 | tf_op jit(solution)/shard_map/ppermute | solution.py:304
  43.6 15.1 %collective-permute-done.1 = bf16[2,64,1920]{2,1,0:T(8,128)(2,1)S(1)} collective-permute-done((bf16[2,64,1920]{2,1,0:T(8,128)(2,1)}, bf16[2,64,1920]{2,1,0:T(8,128)(2,1)S(1)}, u32[]{:S(2)}, u32[]{:S(2)}) %collective-permute-start.1) | collective-permute-done | bytes 491552 | tf_op jit(solution)/shard_map/ppermute | solution.py:304
  87.7 10.5 %collective-permute-done.4 = s32[2,2,256]{2,1,0:T(2,128)S(1)} collective-permute-done((s32[2,2,256]{2,1,0:T(2,128)S(1)}, s32[2,2,256]{2,1,0:T(2,128)S(1)}, u32[]{:S(2)}, u32[]{:S(2)}) %collective-permute-start.4) | collective-permute-done | bytes 4128 | tf_op jit(solution)/shard_map/ppermute | solution.py:304
  101.6 4.7 fusion.19
  106.3 4.0 fusion.21
  111.3 13.1 %collective-permute-done.7.refs_1_ = bf16[8,64,1024]{2,1,0:T(8,128)(2,1)S(1)} collective-permute-done((bf16[8,64,1024]{2,1,0:T(8,128)(2,1)S(1)}, bf16[8,64,1024]{2,1,0:T(8,128)(2,1)S(1)}, u32[]{:S(2)}, u32[]{:S(2)}) %collective-permute-start.7) | collective-permute-done | bytes 1048608 | tf_op jit(solution)/shard_map/ppermute | solution.py:304
  129.4 9.8 %collective-permute-done.12.refs_3_ = bf16[8,64,768]{2,1,0:T(8,128)(2,1)S(1)} collective-permute-done((bf16[8,64,768]{2,1,0:T(8,128)(2,1)}, bf16[8,64,768]{2,1,0:T(8,128)(2,1)S(1)}, u32[]{:S(2)}, u32[]{:S(2)}) %collective-permute-start.12) | collective-permute-done | bytes 786464 | tf_op jit(solution)/shard_map/ppermute | solution.py:304
  140.1 4.2 place.3
  147.0 5.3 place.2
  152.3 17.7 %project.1 = (bf16[2048,2048]{1,0:T(8,128)(2,1)}, bf16[2048,2048]{1,0:T(8,128)(2,1)}, bf16[2048,768]{1,0:T(8,128)(2,1)}) custom-call(bf16[2048,2048]{1,0:T(8,128)(2,1)} %all-gather.3.cloned.1.call-done.x_ref, bf16[2048,768]{1,0:T(8,128)(2,1)} %bitcast.136, f32[1,768]{1,0:T(1,128)} %bitcast.162, f32[4,2048]{1,0:T(4,128)} %pad_maximum_fusion.9.n_ref.g_ref, ...), custom_call_target="tpu_custom_call" | custom-call | flops 1 | bytes 1 | tf_op jit(solution)/shard_map/project/pallas_call | solution.py:523
  170.0 4.3 all-to-all-start
  176.2 16.8 %expand.1 = (bf16[2048,1024]{1,0:T(8,128)(2,1)}, bf16[2048,1024]{1,0:T(8,128)(2,1)}) custom-call(bf16[2048,2048]{1,0:T(8,128)(2,1)} %get-tuple-element.80.s_ref.a_ref.b_ref, bf16[2048,1024]{1,0:T(8,128)(2,1)} %bitcast.133, f32[1,1024]{1,0:T(1,128)} %bitcast.160), custom_call_target="tpu_custom_call" | custom-call | flops 1 | bytes 1 | tf_op jit(solution)/shard_map/expand/pallas_call | solution.py:551
  193.0 14.1 %contract.2.refs_0_ = bf16[2048,2048]{1,0:T(8,128)(2,1)} custom-call(bf16[2048,1024]{1,0:T(8,128)(2,1)} %get-tuple-element.81.left_ref.a_ref.b_ref, bf16[1024,2048]{1,0:T(8,128)(2,1)} %w_ref.1), custom_call_target="tpu_custom_call" | custom-call | flops 1 | bytes 1 | tf_op jit(solution)/shard_map/contract/pallas_call | solution.py:574
  209.6 8.3 %attend.1 = bf16[4,2,256,256]{3,2,1,0:T(8,128)(2,1)} custom-call(s32[2,1,1024]{2,1,0:T(1,128)} %get-tuple-element.166.row_ref, s32[2,1024,1]{2,1,0:T(8,128)} %broadcast_in_dim_squeeze.4.col_ref, bf16[4,2,256,768]{3,2,1,0:T(8,128)(2,1)} %copy-done.2), custom_call_target="tpu_custom_call" | custom-call | flops 1 | bytes 1 | tf_op jit(solution)/shard_map/attend/pallas_call | solution.py:737
  217.9 3.7 all-to-all-start.1
  221.5 10.0 %all-gather.5.cloned.1.call-done.right_ref.g_ref = bf16[2048,2048]{1,0:T(8,128)(2,1)} async-done(((bf16[256,2048]{1,0:T(8,128)(2,1)}), bf16[2048,2048]{1,0:T(8,128)(2,1)}) %all-gather.5.cloned.1.call-update) | async-done | bytes 8388624 | tf_op jit(solution)/shard_map/all_gather | solution.py:911
  231.5 6.8 %convolution_convert_fusion = bf16[2048,256]{1,0:T(8,128)(2,1)} fusion(bf16[2048,2048]{1,0:T(8,128)(2,1)} %all-gather.5.cloned.1.call-done.right_ref.g_ref, bf16[256,2048]{1,0:T(8,128)(2,1)S(1)} %copy-done.16), kind=kOutput, calls=%fused_computation.8 | convolution fusion | flops 2148007936 | bytes 10485760 | tf_op jit(solution)/shard_map/dot_general | solution.py:300
  238.3 3.8 all-to-all-start.2
  243.4 11.0 %contract.3 = bf16[2048,2048]{1,0:T(8,128)(2,1)} custom-call(bf16[2048,256]{1,0:T(8,128)(2,1)} %bitcast.140, bf16[256,2048]{1,0:T(8,128)(2,1)} %weight_ref.3, bf16[2048,2048]{1,0:T(8,128)(2,1)} %contract.2.refs_0_), custom_call_target="tpu_custom_call" | custom-call | flops 1 | bytes 1 | tf_op jit(solution)/shard_map/contract/pallas_call | solution.py:574
  254.4 7.0 %grad_pair.4 = (bf16[1,2,64,2048]{3,2,1,0:T(8,128)(2,1)}, bf16[1,2,64,2048]{3,2,1,0:T(8,128)(2,1)}) custom-call(s32[1]{0:T(128)} %bitcast.24.keep_ref.bit_ref, s32[1]{0:T(128)} %bitcast.25.send_ref, bf16[2048,256]{1,0:T(8,128)(2,1)} %bitcast.141, bf16[2048,256]{1,0:T(8,128)(2,1)} %bitcast.142, bf16[2048,2048]{1,0:T(8,128)(2,1)} %all-gather.5.cloned.1.call-done.right_ref.g_ref), custom_call_target="tpu_custom_call" | custom-call | flops 1 | bytes 1 | tf_op jit(solution)/shard_map/grad_pair/pallas_call | solution.py:629
  262.4 13.7 %attend_back.1 = bf16[4,2,256,768]{3,2,1,0:T(8,128)(2,1)} custom-call(s32[2,1,1024]{2,1,0:T(1,128)} %get-tuple-element.166.row_ref, s32[2,1024,1]{2,1,0:T(8,128)} %broadcast_in_dim_squeeze.4.col_ref, f32[2,1024,128]{2,1,0:T(8,128)} %bitcast.146, f32[2,1024,128]{2,1,0:T(8,128)} %bitcast.145, f32[2,1024,128]{2,1,0:T(8,128)} %bitcast.144, ...), custom_call_target="tpu_custom_call" | custom-call | flops 1 | bytes 1 | tf_op jit(solution)/shard_map/attend_back/pallas_call | solution.py:797
  276.2 4.2 all-to-all-start.3
  281.3 15.7 %hidden_back.1 = (bf16[2048,1024]{1,0:T(8,128)(2,1)}, f32[1,1024]{1,0:T(1,128)}) custom-call(bf16[2048,2048]{1,0:T(8,128)(2,1)} %all-gather.5.cloned.1.call-done.right_ref.g_ref, bf16[1024,2048]{1,0:T(8,128)(2,1)} %w_ref.1, bf16[2048,1024]{1,0:T(8,128)(2,1)} %get-tuple-element.91.s_ref), custom_call_target="tpu_custom_call" | custom-call | flops 1 | bytes 1 | tf_op jit(solution)/shard_map/hidden_back/pallas_call | solution.py:600
  297.0 15.1 %grad_pair.5 = (bf16[4,1,128,2048]{3,2,1,0:T(8,128)(2,1)}, bf16[4,1,128,2048]{3,2,1,0:T(8,128)(2,1)}) custom-call(s32[4]{0:T(128)} %get-tuple-element.192.keep_ref, s32[4]{0:T(128)} %get-tuple-element.193.send_ref, bf16[2048,1024]{1,0:T(8,128)(2,1)} %get-tuple-element.81.left_ref.a_ref.b_ref, bf16[2048,1024]{1,0:T(8,128)(2,1)} %get-tuple-element.81.left_ref.a_ref.b_ref, ...), custom_call_target="tpu_custom_call" | custom-call | flops 1 | bytes 1 | tf_op jit(solution)/shard_map/grad_pair/pallas_call | solution.py:629
  316.7 14.7 %grad_pair.6 = (bf16[8,2,64,1024]{3,2,1,0:T(8,128)(2,1)}, bf16[8,2,64,1024]{3,2,1,0:T(8,128)(2,1)}) custom-call(s32[8]{0:T(128)} %stack.213.keep_ref, s32[8]{0:T(128)} %stack.221.send_ref, bf16[2048,2048]{1,0:T(8,128)(2,1)} %get-tuple-element.80.s_ref.a_ref.b_ref, bf16[2048,2048]{1,0:T(8,128)(2,1)} %get-tuple-element.80.s_ref.a_ref.b_ref, ...), custom_call_target="tpu_custom_call" | custom-call | flops 1 | bytes 1 | tf_op jit(solution)/shard_map/grad_pair/pallas_call | solution.py:629
  334.9 13.1 %grad_pair.7 = (bf16[8,2,64,768]{3,2,1,0:T(8,128)(2,1)}, bf16[8,2,64,768]{3,2,1,0:T(8,128)(2,1)}) custom-call(s32[8]{0:T(128)} %stack.196.keep_ref, s32[8]{0:T(128)} %stack.205.send_ref, bf16[2048,2048]{1,0:T(8,128)(2,1)} %get-tuple-element.96.a_ref.b_ref, bf16[2048,2048]{1,0:T(8,128)(2,1)} %get-tuple-element.96.a_ref.b_ref, bf16[2048,768]{1,0:T(8,128)(2,1)} %bitcast.130), custom_call_target="tpu_custom_call" | custom-call | flops 1 | bytes 1 | tf_op jit(solution)/shard_map/grad_pair/pallas_call | solution.py:629
  348.1 15.6 %norm_back.2 = (bf16[2048,2048]{1,0:T(8,128)(2,1)}, f32[4,2048]{1,0:T(4,128)}) custom-call(bf16[2048,2048]{1,0:T(8,128)(2,1)} %all-gather.3.cloned.1.call-done.x_ref, bf16[2048,768]{1,0:T(8,128)(2,1)} %bitcast.131, bf16[2048,1024]{1,0:T(8,128)(2,1)} %get-tuple-element.97.right_ref.h_ref, bf16[2048,768]{1,0:T(8,128)(2,1)} %bitcast.137, ...), custom_call_target="tpu_custom_call" | custom-call | flops 1 | bytes 1 | tf_op jit(solution)/shard_map/norm_back/pallas_call | solution.py:839
  363.7 4.0 add_split.2
  369.7 15.6 %norm_back.3 = (bf16[2048,2048]{1,0:T(8,128)(2,1)}, f32[4,2048]{1,0:T(4,128)}) custom-call(bf16[2048,2048]{1,0:T(8,128)(2,1)} %all-gather.3.cloned.1.call-done.x_ref, bf16[2048,768]{1,0:T(8,128)(2,1)} %bitcast.132, bf16[2048,1024]{1,0:T(8,128)(2,1)} %get-tuple-element.97.right_ref.h_ref, ...), custom_call_target="tpu_custom_call", output_to_operand_aliasing={{0}: (6, {})} | custom-call | flops 1 | bytes 1 | tf_op jit(solution)/shard_map/norm_back/pallas_call | solution.py:839
  385.2 4.5 add_split_two.1
  389.7 5.5 collective-permute-done.15.b_ref
  402.4 27.6 %collective-permute-done.19 = bf16[10,64,1024]{2,1,0:T(8,128)(2,1)S(1)} collective-permute-done((bf16[10,64,1024]{2,1,0:T(8,128)(2,1)}, bf16[10,64,1024]{2,1,0:T(8,128)(2,1)S(1)}, u32[]{:S(2)}, u32[]{:S(2)}) %collective-permute-start.19) | collective-permute-done | bytes 1310752 | tf_op jit(solution)/shard_map/ppermute | solution.py:304
  433.6 5.6 all-to-all-start.5
  439.2 3.1 add_convert_fusion.1.refs_0_
  446.7 21.4 %collective-permute-done.21.refs_2_ = bf16[1,256,2048]{2,1,0:T(8,128)(2,1)} collective-permute-done((bf16[1,256,2048]{2,1,0:T(8,128)(2,1)}, bf16[1,256,2048]{2,1,0:T(8,128)(2,1)}, u32[]{:S(2)}, u32[]{:S(2)}) %collective-permute-start.21) | collective-permute-done | bytes 1048608 | tf_op jit(solution)/shard_map/ppermute | solution.py:304
  468.5 3.1 collective-permute-done.20.refs_1_
  474.2 8.9 %all-to-all-done.5 = bf16[8,64,1024]{2,1,0:T(8,128)(2,1)} async-done(((bf16[8,64,1024]{2,1,0:T(8,128)(2,1)}), bf16[8,64,1024]{2,1,0:T(8,128)(2,1)}, u32[]{:S(2)}, u32[]{:S(2)}) %all-to-all-start.5) | async-done | bytes 1048608 | tf_op jit(solution)/shard_map/all_to_all | solution.py:1034
  483.1 3.6 all-to-all-start.4
  486.7 7.0 %collective-permute-done.22.refs_3_ = bf16[1,256,2048]{2,1,0:T(8,128)(2,1)} collective-permute-done((bf16[1,256,2048]{2,1,0:T(8,128)(2,1)}, bf16[1,256,2048]{2,1,0:T(8,128)(2,1)}, u32[]{:S(2)}, u32[]{:S(2)}) %collective-permute-start.22) | collective-permute-done | bytes 1048608 | tf_op jit(solution)/shard_map/ppermute | solution.py:304
  496.8 25.8 %all-to-all-done.4 = bf16[8,72,768]{2,1,0:T(8,128)(2,1)S(1)} async-done(((bf16[8,72,768]{2,1,0:T(8,128)(2,1)}), bf16[8,72,768]{2,1,0:T(8,128)(2,1)S(1)}, u32[]{:S(2)}, u32[]{:S(2)}) %all-to-all-start.4) | async-done | bytes 884768 | tf_op jit(solution)/shard_map/all_to_all | solution.py:1036
  527.8 20.1 %collective-permute-done.25.refs_2_ = bf16[9,64,768]{2,1,0:T(8,128)(2,1)} collective-permute-done((bf16[9,64,768]{2,1,0:T(8,128)(2,1)S(1)}, bf16[9,64,768]{2,1,0:T(8,128)(2,1)}, u32[]{:S(2)}, u32[]{:S(2)}) %collective-permute-start.25) | collective-permute-done | bytes 884768 | tf_op jit(solution)/shard_map/ppermute | solution.py:304
  552.3 5.4 finish.4
  557.7 15.6 %collective-permute-done.28.refs_3_ = bf16[10,64,1024]{2,1,0:T(8,128)(2,1)} collective-permute-done((bf16[10,64,1024]{2,1,0:T(8,128)(2,1)}, bf16[10,64,1024]{2,1,0:T(8,128)(2,1)}, u32[]{:S(2)}, u32[]{:S(2)}) %collective-permute-start.28) | collective-permute-done | bytes 1310752 | tf_op jit(solution)/shard_map/ppermute | solution.py:304
  581.1 4.1 fusion.6
  585.2 5.4 finish.6
  590.6 5.3 finish.7
  (252 shorter events, 101.1 us)
Async XLA Ops:
  7.2 145.1 %all-gather.3.cloned.1.call-start = ((), (), s32[]{:S(2)}) async-start(), calls=%async_computation.8 | async-start | bytes 9437184 | tf_op jit(solution)/shard_map/all_gather | solution.py:909
  19.3 24.3 %collective-permute-start = (bf16[2,64,1920]{2,1,0:T(8,128)(2,1)}, bf16[2,64,1920]{2,1,0:T(8,128)(2,1)S(1)}, u32[]{:S(2)}, u32[]{:S(2)}) collective-permute-start(bf16[2,64,1920]{2,1,0:T(8,128)(2,1)} %get-tuple-element.73), channel_id=1, source_target_pairs={{0,2},{1,3},{2,0},{3,1},{4,6},{5,7},{6,4},{7,5},{8,10},{9,11},{10,... | collective-permute-start | bytes 1474568 | tf_op jit(solution)/shard_map/ppermute | solution.py:304
  22.4 36.3 %collective-permute-start.1 = (bf16[2,64,1920]{2,1,0:T(8,128)(2,1)}, bf16[2,64,1920]{2,1,0:T(8,128)(2,1)S(1)}, u32[]{:S(2)}, u32[]{:S(2)}) collective-permute-start(bf16[2,64,1920]{2,1,0:T(8,128)(2,1)} %get-tuple-element.74), channel_id=1, source_target_pairs={{0,4},{1,5},{2,6},{3,7},{4,0},{5,1},{6,2},{7,3},{8,12},{9,13},{10,... | collective-permute-start | bytes 1474568 | tf_op jit(solution)/shard_map/ppermute | solution.py:304
  25.0 33.7 %collective-permute-start.2 = (bf16[2,64,1920]{2,1,0:T(8,128)(2,1)}, bf16[2,64,1920]{2,1,0:T(8,128)(2,1)S(1)}, u32[]{:S(2)}, u32[]{:S(2)}) collective-permute-start(bf16[2,64,1920]{2,1,0:T(8,128)(2,1)} %get-tuple-element.75), channel_id=1, source_target_pairs={{0,6},{1,7},{2,4},{3,5},{4,2},{5,3},{6,0},{7,1},{8,14},{9,15},{10,... | collective-permute-start | bytes 1474568 | tf_op jit(solution)/shard_map/ppermute | solution.py:304
  58.8 172.7 %all-gather.5.cloned.1.call-start = ((), (), s32[]{:S(2)}) async-start(), calls=%async_computation.9 | async-start | bytes 9437184 | tf_op jit(solution)/shard_map/all_gather | solution.py:911
  62.9 2.6 collective-permute-start.3
  65.6 482.9 %copy-start.23 = (s32[4]{0:T(128)}, s32[4]{0:T(128)S(1)}, u32[]{:S(2)}) copy-start(s32[4]{0:T(128)S(1)} %get-tuple-element.191.rows_ref) | copy-start | bytes 52
  77.3 24.3 %copy-start.13 = (bf16[8,64,768]{2,1,0:T(8,128)(2,1)}, bf16[8,64,768]{2,1,0:T(8,128)(2,1)S(1)}, u32[]{:S(2)}) copy-start(bf16[8,64,768]{2,1,0:T(8,128)(2,1)S(1)} %slice.224.refs_0_) | copy-start | bytes 2359300
  77.3 33.4 %collective-permute-start.11 = (bf16[8,64,768]{2,1,0:T(8,128)(2,1)S(1)}, bf16[8,64,768]{2,1,0:T(8,128)(2,1)}, u32[]{:S(2)}, u32[]{:S(2)}) collective-permute-start(bf16[8,64,768]{2,1,0:T(8,128)(2,1)S(1)} %slice.224.refs_0_), channel_id=1, source_target_pairs={{0,16},{8,24},{16,0},{24,8},{1,17},{9,25},{17,1},{25,9},{2,18},{10... | collective-permute-start | bytes 2359304 | tf_op jit(solution)/shard_map/ppermute | solution.py:304
  78.8 50.6 %collective-permute-start.10 = (bf16[8,64,768]{2,1,0:T(8,128)(2,1)S(1)}, bf16[8,64,768]{2,1,0:T(8,128)(2,1)}, u32[]{:S(2)}, u32[]{:S(2)}) collective-permute-start(bf16[8,64,768]{2,1,0:T(8,128)(2,1)S(1)} %slice.224.refs_0_), channel_id=1, source_target_pairs={{0,8},{8,0},{16,24},{24,16},{1,9},{9,1},{17,25},{25,17},{2,10},{10... | collective-permute-start | bytes 2359304 | tf_op jit(solution)/shard_map/ppermute | solution.py:304
  81.4 16.8 %collective-permute-start.4 = (s32[2,2,256]{2,1,0:T(2,128)S(1)}, s32[2,2,256]{2,1,0:T(2,128)S(1)}, u32[]{:S(2)}, u32[]{:S(2)}) collective-permute-start(s32[2,2,256]{2,1,0:T(2,128)S(1)} %bitcast.166), channel_id=1, source_target_pairs={{0,8},{8,0},{16,24},{24,16},{1,9},{9,1},{17,25},{25,17},{2,10},{10... | collective-permute-start | bytes 12296 | tf_op jit(solution)/shard_map/ppermute | solution.py:304
  82.1 17.7 %collective-permute-start.5 = (s32[2,2,256]{2,1,0:T(2,128)S(1)}, s32[2,2,256]{2,1,0:T(2,128)S(1)}, u32[]{:S(2)}, u32[]{:S(2)}) collective-permute-start(s32[2,2,256]{2,1,0:T(2,128)S(1)} %bitcast.165), channel_id=1, source_target_pairs={{0,16},{8,24},{16,0},{24,8},{1,17},{9,25},{17,1},{25,9},{2,18},{10... | collective-permute-start | bytes 12296 | tf_op jit(solution)/shard_map/ppermute | solution.py:304
  82.7 17.6 %collective-permute-start.6 = (s32[2,2,256]{2,1,0:T(2,128)S(1)}, s32[2,2,256]{2,1,0:T(2,128)S(1)}, u32[]{:S(2)}, u32[]{:S(2)}) collective-permute-start(s32[2,2,256]{2,1,0:T(2,128)S(1)} %bitcast.164), channel_id=1, source_target_pairs={{0,24},{8,16},{16,8},{24,0},{1,25},{9,17},{17,9},{25,1},{2,26},{10... | collective-permute-start | bytes 12296 | tf_op jit(solution)/shard_map/ppermute | solution.py:304
  87.7 18.7 %copy-start.10 = (bf16[8,64,1024]{2,1,0:T(8,128)(2,1)}, bf16[8,64,1024]{2,1,0:T(8,128)(2,1)S(1)}, u32[]{:S(2)}) copy-start(bf16[8,64,1024]{2,1,0:T(8,128)(2,1)S(1)} %slice.223.refs_0_) | copy-start | bytes 3145732
  98.3 26.1 %collective-permute-start.7 = (bf16[8,64,1024]{2,1,0:T(8,128)(2,1)S(1)}, bf16[8,64,1024]{2,1,0:T(8,128)(2,1)S(1)}, u32[]{:S(2)}, u32[]{:S(2)}) collective-permute-start(bf16[8,64,1024]{2,1,0:T(8,128)(2,1)S(1)} %slice.223.refs_0_), channel_id=1, source_target_pairs={{0,8},{8,0},{16,24},{24,16},{1,9},{9,1},{17,25},{25,17},{2,10},{10... | collective-permute-start | bytes 3145736 | tf_op jit(solution)/shard_map/ppermute | solution.py:304
  99.7 44.5 %collective-permute-start.8 = (bf16[8,64,1024]{2,1,0:T(8,128)(2,1)S(1)}, bf16[8,64,1024]{2,1,0:T(8,128)(2,1)}, u32[]{:S(2)}, u32[]{:S(2)}) collective-permute-start(bf16[8,64,1024]{2,1,0:T(8,128)(2,1)S(1)} %slice.223.refs_0_), channel_id=1, source_target_pairs={{0,16},{8,24},{16,0},{24,8},{1,17},{9,25},{17,1},{25,9},{2,18},{10... | collective-permute-start | bytes 3145736 | tf_op jit(solution)/shard_map/ppermute | solution.py:304
  110.7 28.5 %collective-permute-start.12 = (bf16[8,64,768]{2,1,0:T(8,128)(2,1)}, bf16[8,64,768]{2,1,0:T(8,128)(2,1)S(1)}, u32[]{:S(2)}, u32[]{:S(2)}) collective-permute-start(bf16[8,64,768]{2,1,0:T(8,128)(2,1)} %collective-permute-done.11.refs_2_), channel_id=1, source_target_pairs={{0,8},{8,0},{16,24},{24,16},{1,9},{9,1},{17,25},{25,17},{2,10},{10... | collective-permute-start | bytes 2359304 | tf_op jit(solution)/shard_map/ppermute | solution.py:304
  124.4 21.6 %collective-permute-start.9 = (bf16[8,64,1024]{2,1,0:T(8,128)(2,1)S(1)}, bf16[8,64,1024]{2,1,0:T(8,128)(2,1)S(1)}, u32[]{:S(2)}, u32[]{:S(2)}) collective-permute-start(bf16[8,64,1024]{2,1,0:T(8,128)(2,1)S(1)} %collective-permute-done.7.refs_1_), channel_id=1, source_target_pairs={{0,16},{8,24},{16,0},{24,8},{1,17},{9,25},{17,1},{25,9},{2,18},{10... | collective-permute-start | bytes 3145736 | tf_op jit(solution)/shard_map/ppermute | solution.py:304
  170.0 38.0 %all-to-all-start = ((bf16[4,2,256,768]{3,2,1,0:T(8,128)(2,1)}), bf16[4,2,256,768]{3,2,1,0:T(8,128)(2,1)S(1)}, u32[]{:S(2)}, u32[]{:S(2)}) async-start(bf16[4,2,256,768]{3,2,1,0:T(8,128)(2,1)} %bitcast.147), calls=%async_computation | async-start | bytes 6291456 | tf_op jit(solution)/shard_map/all_to_all | solution.py:949
  217.9 20.4 %all-to-all-start.1 = ((bf16[4,2,256,256]{3,2,1,0:T(8,128)(2,1)}), bf16[4,2,256,256]{3,2,1,0:T(8,128)(2,1)S(1)}, u32[]{:S(2)}, u32[]{:S(2)}) async-start(bf16[4,2,256,256]{3,2,1,0:T(8,128)(2,1)} %attend.1), calls=%async_computation.1 | async-start | bytes 2097152 | tf_op jit(solution)/shard_map/all_to_all | solution.py:954
  238.3 23.1 %all-to-all-start.2 = ((bf16[4,2,256,256]{3,2,1,0:T(8,128)(2,1)}), bf16[4,2,256,256]{3,2,1,0:T(8,128)(2,1)S(1)}, u32[]{:S(2)}, u32[]{:S(2)}) async-start(bf16[4,2,256,256]{3,2,1,0:T(8,128)(2,1)} %bitcast.149), calls=%async_computation.2 | async-start | bytes 2097152 | tf_op jit(solution)/shard_map/all_to_all | solution.py:949
  242.1 158.0 %reduce-scatter.3.cloned.1.call-start = ((), (), s32[]{:S(2)}) async-start(), calls=%async_computation.10 | async-start | bytes 9437184 | tf_op jit(solution)/shard_map/reduce_scatter | solution.py:974
  276.2 57.1 %all-to-all-start.3 = ((bf16[4,2,256,768]{3,2,1,0:T(8,128)(2,1)}), bf16[4,2,256,768]{3,2,1,0:T(8,128)(2,1)S(1)}, u32[]{:S(2)}, u32[]{:S(2)}) async-start(bf16[4,2,256,768]{3,2,1,0:T(8,128)(2,1)} %attend_back.1), calls=%async_computation.4 | async-start | bytes 6291456 | tf_op jit(solution)/shard_map/all_to_all | solution.py:954
  280.4 298.6 %reduce-scatter.5.cloned.1.call-start = ((), (), s32[]{:S(2)}) async-start(), calls=%async_computation.11 | async-start | bytes 9437184 | tf_op jit(solution)/shard_map/reduce_scatter | solution.py:1022
  312.1 51.6 %collective-permute-start.13 = (bf16[1,2,256,2048]{3,2,1,0:T(8,128)(2,1)}, bf16[1,2,256,2048]{3,2,1,0:T(8,128)(2,1)}, u32[]{:S(2)}, u32[]{:S(2)}) collective-permute-start(bf16[1,2,256,2048]{3,2,1,0:T(8,128)(2,1)} %bitcast.167), channel_id=1, source_target_pairs={{0,8},{8,0},{16,24},{24,16},{1,9},{9,1},{17,25},{25,17},{2,10},{10... | collective-permute-start | bytes 6291464 | tf_op jit(solution)/shard_map/ppermute | solution.py:304
  315.3 18.1 %collective-permute-start.14 = (bf16[1,2,64,2048]{3,2,1,0:T(8,128)(2,1)}, bf16[1,2,64,2048]{3,2,1,0:T(8,128)(2,1)}, u32[]{:S(2)}, u32[]{:S(2)}) collective-permute-start(bf16[1,2,64,2048]{3,2,1,0:T(8,128)(2,1)} %get-tuple-element.87), channel_id=1, source_target_pairs={{0,16},{8,24},{16,0},{24,8},{1,17},{9,25},{17,1},{25,9},{2,18},{10... | collective-permute-start | bytes 1572872 | tf_op jit(solution)/shard_map/ppermute | solution.py:304
  331.4 53.8 %collective-permute-start.16 = (bf16[8,2,64,1024]{3,2,1,0:T(8,128)(2,1)}, bf16[8,2,64,1024]{3,2,1,0:T(8,128)(2,1)}, u32[]{:S(2)}, u32[]{:S(2)}) collective-permute-start(bf16[8,2,64,1024]{3,2,1,0:T(8,128)(2,1)} %get-tuple-element.98), channel_id=1, source_target_pairs={{0,16},{8,24},{16,0},{24,8},{1,17},{9,25},{17,1},{25,9},{2,18},{10... | collective-permute-start | bytes 6291464 | tf_op jit(solution)/shard_map/ppermute | solution.py:304
  348.1 47.1 %collective-permute-start.15 = (bf16[8,2,64,768]{3,2,1,0:T(8,128)(2,1)}, bf16[8,2,64,768]{3,2,1,0:T(8,128)(2,1)S(1)}, u32[]{:S(2)}, u32[]{:S(2)}) collective-permute-start(bf16[8,2,64,768]{3,2,1,0:T(8,128)(2,1)} %get-tuple-element.100), channel_id=1, source_target_pairs={{0,8},{8,0},{16,24},{24,16},{1,9},{9,1},{17,25},{25,17},{2,10},{10... | collective-permute-start | bytes 4718600 | tf_op jit(solution)/shard_map/ppermute | solution.py:304
  367.7 32.4 %collective-permute-start.17 = (bf16[1,256,2048]{2,1,0:T(8,128)(2,1)}, bf16[1,256,2048]{2,1,0:T(8,128)(2,1)S(1)}, u32[]{:S(2)}, u32[]{:S(2)}) collective-permute-start(bf16[1,256,2048]{2,1,0:T(8,128)(2,1)} %get-tuple-element.104), channel_id=1, source_target_pairs={{0,16},{8,24},{16,0},{24,8},{1,17},{9,25},{17,1},{25,9},{2,18},{10... | collective-permute-start | bytes 3145736 | tf_op jit(solution)/shard_map/ppermute | solution.py:304
  400.1 30.8 %copy-start.15 = (bf16[10,64,1024]{2,1,0:T(8,128)(2,1)S(1)}, bf16[10,64,1024]{2,1,0:T(8,128)(2,1)}, u32[]{:S(2)}) copy-start(bf16[10,64,1024]{2,1,0:T(8,128)(2,1)} %get-tuple-element.123) | copy-start | bytes 3932164
  401.1 29.0 %collective-permute-start.19 = (bf16[10,64,1024]{2,1,0:T(8,128)(2,1)}, bf16[10,64,1024]{2,1,0:T(8,128)(2,1)S(1)}, u32[]{:S(2)}, u32[]{:S(2)}) collective-permute-start(bf16[10,64,1024]{2,1,0:T(8,128)(2,1)} %get-tuple-element.112), channel_id=1, source_target_pairs={{0,8},{8,0},{16,24},{24,16},{1,9},{9,1},{17,25},{25,17},{2,10},{10... | collective-permute-start | bytes 3932168 | tf_op jit(solution)/shard_map/ppermute | solution.py:304
  401.7 28.4 %collective-permute-start.18 = (bf16[8,64,768]{2,1,0:T(8,128)(2,1)}, bf16[8,64,768]{2,1,0:T(8,128)(2,1)S(1)}, u32[]{:S(2)}, u32[]{:S(2)}) collective-permute-start(bf16[8,64,768]{2,1,0:T(8,128)(2,1)} %get-tuple-element.114), channel_id=1, source_target_pairs={{0,16},{8,24},{16,0},{24,8},{1,17},{9,25},{17,1},{25,9},{2,18},{10... | collective-permute-start | bytes 2359304 | tf_op jit(solution)/shard_map/ppermute | solution.py:304
  433.6 49.5 %all-to-all-start.5 = ((bf16[8,64,1024]{2,1,0:T(8,128)(2,1)}), bf16[8,64,1024]{2,1,0:T(8,128)(2,1)}, u32[]{:S(2)}, u32[]{:S(2)}) async-start(bf16[8,64,1024]{2,1,0:T(8,128)(2,1)} %slice.244), calls=%async_computation.7 | async-start | bytes 2097152 | tf_op jit(solution)/shard_map/all_to_all | solution.py:1034
  442.3 25.8 %collective-permute-start.21 = (bf16[1,256,2048]{2,1,0:T(8,128)(2,1)}, bf16[1,256,2048]{2,1,0:T(8,128)(2,1)}, u32[]{:S(2)}, u32[]{:S(2)}) collective-permute-start(bf16[1,256,2048]{2,1,0:T(8,128)(2,1)} %add_convert_fusion.1.refs_0_), channel_id=1, source_target_pairs={{0,16},{8,24},{16,0},{24,8},{1,17},{9,25},{17,1},{25,9},{2,18},{10... | collective-permute-start | bytes 3145736 | tf_op jit(solution)/shard_map/ppermute | solution.py:304
  445.6 26.0 %collective-permute-start.20 = (bf16[1,256,2048]{2,1,0:T(8,128)(2,1)}, bf16[1,256,2048]{2,1,0:T(8,128)(2,1)}, u32[]{:S(2)}, u32[]{:S(2)}) collective-permute-start(bf16[1,256,2048]{2,1,0:T(8,128)(2,1)} %add_convert_fusion.1.refs_0_), channel_id=1, source_target_pairs={{0,8},{8,0},{16,24},{24,16},{1,9},{9,1},{17,25},{25,17},{2,10},{10... | collective-permute-start | bytes 3145736 | tf_op jit(solution)/shard_map/ppermute | solution.py:304
  468.2 25.6 %collective-permute-start.22 = (bf16[1,256,2048]{2,1,0:T(8,128)(2,1)}, bf16[1,256,2048]{2,1,0:T(8,128)(2,1)}, u32[]{:S(2)}, u32[]{:S(2)}) collective-permute-start(bf16[1,256,2048]{2,1,0:T(8,128)(2,1)} %collective-permute-done.21.refs_2_), channel_id=1, source_target_pairs={{0,8},{8,0},{16,24},{24,16},{1,9},{9,1},{17,25},{25,17},{2,10},{10... | collective-permute-start | bytes 3145736 | tf_op jit(solution)/shard_map/ppermute | solution.py:304
  473.2 20.5 %slice-start = ((bf16[10,64,1024]{2,1,0:T(8,128)(2,1)}), bf16[2,64,1024]{2,1,0:T(8,128)(2,1)S(1)}, s32[]{:S(2)}) async-start(bf16[10,64,1024]{2,1,0:T(8,128)(2,1)} %copy-done.7), calls=%async_computation.12 | async-start | bytes 524288 | tf_op jit(solution)/shard_map/slice | solution.py:1038
  483.1 39.4 %all-to-all-start.4 = ((bf16[8,72,768]{2,1,0:T(8,128)(2,1)}), bf16[8,72,768]{2,1,0:T(8,128)(2,1)S(1)}, u32[]{:S(2)}, u32[]{:S(2)}) async-start(bf16[8,72,768]{2,1,0:T(8,128)(2,1)} %fusion.18), calls=%async_computation.6 | async-start | bytes 1769472 | tf_op jit(solution)/shard_map/all_to_all | solution.py:1036
  495.1 56.2 %copy-start.5 = (bf16[10,64,1024]{2,1,0:T(8,128)(2,1)}, bf16[10,64,1024]{2,1,0:T(8,128)(2,1)S(1)}, u32[]{:S(2)}) copy-start(bf16[10,64,1024]{2,1,0:T(8,128)(2,1)S(1)} %pad_maximum_fusion.4.refs_0_) | copy-start | bytes 3932164
  495.1 56.0 %copy-start.3 = (bf16[1,256,2048]{2,1,0:T(8,128)(2,1)S(1)}, bf16[1,256,2048]{2,1,0:T(8,128)(2,1)}, u32[]{:S(2)}) copy-start(bf16[1,256,2048]{2,1,0:T(8,128)(2,1)} %param.17) | copy-start | bytes 3145732
  495.1 30.1 %collective-permute-start.23 = (bf16[10,64,1024]{2,1,0:T(8,128)(2,1)S(1)}, bf16[10,64,1024]{2,1,0:T(8,128)(2,1)}, u32[]{:S(2)}, u32[]{:S(2)}) collective-permute-start(bf16[10,64,1024]{2,1,0:T(8,128)(2,1)S(1)} %pad_maximum_fusion.4.refs_0_), channel_id=1, source_target_pairs={{0,16},{8,24},{16,0},{24,8},{1,17},{9,25},{17,1},{25,9},{2,18},{10... | collective-permute-start | bytes 3932168 | tf_op jit(solution)/shard_map/ppermute | solution.py:304
  496.2 29.6 %collective-permute-start.27 = (bf16[10,64,1024]{2,1,0:T(8,128)(2,1)S(1)}, bf16[10,64,1024]{2,1,0:T(8,128)(2,1)}, u32[]{:S(2)}, u32[]{:S(2)}) collective-permute-start(bf16[10,64,1024]{2,1,0:T(8,128)(2,1)S(1)} %pad_maximum_fusion.4.refs_0_), channel_id=1, source_target_pairs={{0,8},{8,0},{16,24},{24,16},{1,9},{9,1},{17,25},{25,17},{2,10},{10... | collective-permute-start | bytes 3932168 | tf_op jit(solution)/shard_map/ppermute | solution.py:304
  522.8 53.6 %copy-start.12 = (bf16[9,64,768]{2,1,0:T(8,128)(2,1)}, bf16[9,64,768]{2,1,0:T(8,128)(2,1)S(1)}, u32[]{:S(2)}) copy-start(bf16[9,64,768]{2,1,0:T(8,128)(2,1)S(1)} %pad_maximum_fusion.8.refs_0_) | copy-start | bytes 2654212
  525.2 22.7 %collective-permute-start.25 = (bf16[9,64,768]{2,1,0:T(8,128)(2,1)S(1)}, bf16[9,64,768]{2,1,0:T(8,128)(2,1)}, u32[]{:S(2)}, u32[]{:S(2)}) collective-permute-start(bf16[9,64,768]{2,1,0:T(8,128)(2,1)S(1)} %pad_maximum_fusion.8.refs_0_), channel_id=1, source_target_pairs={{0,16},{8,24},{16,0},{24,8},{1,17},{9,25},{17,1},{25,9},{2,18},{10... | collective-permute-start | bytes 2654216 | tf_op jit(solution)/shard_map/ppermute | solution.py:304
  525.8 47.5 %collective-permute-start.28 = (bf16[10,64,1024]{2,1,0:T(8,128)(2,1)}, bf16[10,64,1024]{2,1,0:T(8,128)(2,1)}, u32[]{:S(2)}, u32[]{:S(2)}) collective-permute-start(bf16[10,64,1024]{2,1,0:T(8,128)(2,1)} %collective-permute-done.27.refs_1_), channel_id=1, source_target_pairs={{0,16},{8,24},{16,0},{24,8},{1,17},{9,25},{17,1},{25,9},{2,18},{10... | collective-permute-start | bytes 3932168 | tf_op jit(solution)/shard_map/ppermute | solution.py:304
  527.2 49.1 %collective-permute-start.24 = (bf16[9,64,768]{2,1,0:T(8,128)(2,1)S(1)}, bf16[9,64,768]{2,1,0:T(8,128)(2,1)}, u32[]{:S(2)}, u32[]{:S(2)}) collective-permute-start(bf16[9,64,768]{2,1,0:T(8,128)(2,1)S(1)} %pad_maximum_fusion.8.refs_0_), channel_id=1, source_target_pairs={{0,8},{8,0},{16,24},{24,16},{1,9},{9,1},{17,25},{25,17},{2,10},{10... | collective-permute-start | bytes 2654216 | tf_op jit(solution)/shard_map/ppermute | solution.py:304
  547.9 28.5 %collective-permute-start.26 = (bf16[9,64,768]{2,1,0:T(8,128)(2,1)}, bf16[9,64,768]{2,1,0:T(8,128)(2,1)}, u32[]{:S(2)}, u32[]{:S(2)}) collective-permute-start(bf16[9,64,768]{2,1,0:T(8,128)(2,1)} %collective-permute-done.25.refs_2_), channel_id=1, source_target_pairs={{0,8},{8,0},{16,24},{24,16},{1,9},{9,1},{17,25},{25,17},{2,10},{10... | collective-permute-start | bytes 2654216 | tf_op jit(solution)/shard_map/ppermute | solution.py:304
  579.0 16.9 %copy-start.24 = (f32[256]{0:T(256)}, f32[256]{0:T(256)S(1)}, u32[]{:S(2)}) copy-start(f32[256]{0:T(256)S(1)} %get-tuple-element.221) | copy-start | bytes 3076
  (20 other events, 73.9 us)
Sparse Core Ops, SparseCore 0:
  58.9 90.3 all-gather.2
  150.9 80.5 all-gather.4
  276.3 93.9 reduce-scatter.2
  400.2 121.9 reduce-scatter.4

commit v6 on v5

--- a/solution.py
+++ b/solution.py
@@ -958,13 +958,13 @@
     active, slope = expand(
         then(second, packed), w_in, fc_in_bias.astype(wide).reshape(1, -1), block
     )
-    mlp = contract(active, fc_out_weight, block)
+    mlp = contract(active, fc_out_weight, 2 * block)
     o = attend(then(parts, mlp), seg_row, seg_col, hd)
     o_back = to_group(o)
     x_bit, y_bit = me_c % 2, me_c // 2
     d_o = dot(then(g_all, o), dense_weight, 1, 1).astype(low)
     d_parts = to_sequences(d_o)
-    partial = contract(then(o_back, d_o), dense_weight, block, mlp)
+    partial = contract(then(o_back, d_o), dense_weight, 2 * block, mlp)
     dense_kept, dense_sent = grad_pair(o_back, then(g_all, partial), [y_bit], [1 - y_bit], 2)
     dense_got = swap(dense_sent, "ctx", 2)
     d_qkv = attend_back(
@@ -975,7 +975,7 @@
 
     rows_of = units // (nc * LANES)
     blocks = [((2 * y) * rows_of, s) for y in range(2) for s in range(rows_of)]
-    d_hidden, hidden_sum = hidden_back(then(g_all, d_qkv), fc_out_weight, slope, block)
+    d_hidden, hidden_sum = hidden_back(then(g_all, d_qkv), fc_out_weight, slope, 2 * block)
     out_kept, out_sent = grad_pair(
         active,
         then(g_all, d_hidden),

time: 614 us -> 611 us (level)
  no operation moved by 1% of the time
where the time goes in v6:
time: 611 us; the launch traced here: 601 us
  Pallas kernels  218 us (36%)
  waiting for transfers between devices  218 us (36%)
  starting transfers between devices  59.5 us (10%)
  local copies, waits for them, and re-layouts  39.8 us (7%)
  other arithmetic  35.2 us (6%)
  between operations  22.9 us (4%)
  matrix products  6.96 us (1%)
    ppermute x29, waiting for transfers between devices, swap(): lax.ppermute(values, axis, [(i, i ^ mask) for i in range(lax.axis_size(ax...  172 us
    pallas_call x4, Pallas kernels, grad_pair(): pl.pallas_call(body, name='grad_pair', grid_spec=pltpu.PrefetchScalarGrid...  50 us
    ppermute x29, starting transfers between devices, swap(): lax.ppermute(values, axis, [(i, i ^ mask) for i in range(lax.axis_size(ax...  34 us
    pallas_call x2, Pallas kernels, norm_back(): pl.pallas_call(body, name='norm_back', grid=(steps,), in_specs=[row(width...  31.2 us
    all_to_all x1, waiting for transfers between devices, local_by_head(): qkv_rows = lax.all_to_all(with_totals(qkv_mine), 'fsdp', 0, 0, tiled=True)  25.2 us
    pallas_call x2, Pallas kernels, contract(): pl.pallas_call(body, name='contract', grid=(group // block,), in_specs=[r...  21.9 us
    pallas_call x4, Pallas kernels, finish(): pl.pallas_call(body, name='finish', out_shape=jax.ShapeDtypeStruct(shape,...  19.2 us
    pallas_call x1, Pallas kernels, project(): pl.pallas_call(body, name='project', grid=(group // block,), in_specs=[ro...  17.7 us
  transfers between devices with their start and end apart: 39, of which 20 were waited for; matrix products, arithmetic and copies ran while one was open for 9% of the time, Pallas kernels for 32%

profile of v6, /device:TPU:0, one launch (start us, length us, event | category | flops | bytes accessed | tf_op | source)
XLA Modules:
  0.0 600.9 jit_solution(8361370946114368887)
XLA Ops:
  15.6 3.8 cut_weights.1
  19.3 3.1 collective-permute-start
  25.0 18.6 %collective-permute-done = bf16[2,64,1920]{2,1,0:T(8,128)(2,1)S(1)} collective-permute-done((bf16[2,64,1920]{2,1,0:T(8,128)(2,1)}, bf16[2,64,1920]{2,1,0:T(8,128)(2,1)S(1)}, u32[]{:S(2)}, u32[]{:S(2)}) %collective-permute-start) | collective-permute-done | bytes 491552 | tf_op jit(solution)/shard_map/ppermute | solution.py:304
  43.6 15.1 %collective-permute-done.1 = bf16[2,64,1920]{2,1,0:T(8,128)(2,1)S(1)} collective-permute-done((bf16[2,64,1920]{2,1,0:T(8,128)(2,1)}, bf16[2,64,1920]{2,1,0:T(8,128)(2,1)S(1)}, u32[]{:S(2)}, u32[]{:S(2)}) %collective-permute-start.1) | collective-permute-done | bytes 491552 | tf_op jit(solution)/shard_map/ppermute | solution.py:304
  87.7 10.5 %collective-permute-done.4 = s32[2,2,256]{2,1,0:T(2,128)S(1)} collective-permute-done((s32[2,2,256]{2,1,0:T(2,128)S(1)}, s32[2,2,256]{2,1,0:T(2,128)S(1)}, u32[]{:S(2)}, u32[]{:S(2)}) %collective-permute-start.4) | collective-permute-done | bytes 4128 | tf_op jit(solution)/shard_map/ppermute | solution.py:304
  101.6 4.7 fusion.19
  106.3 4.0 fusion.21
  111.3 13.1 %collective-permute-done.7.refs_1_ = bf16[8,64,1024]{2,1,0:T(8,128)(2,1)S(1)} collective-permute-done((bf16[8,64,1024]{2,1,0:T(8,128)(2,1)S(1)}, bf16[8,64,1024]{2,1,0:T(8,128)(2,1)S(1)}, u32[]{:S(2)}, u32[]{:S(2)}) %collective-permute-start.7) | collective-permute-done | bytes 1048608 | tf_op jit(solution)/shard_map/ppermute | solution.py:304
  129.4 9.8 %collective-permute-done.12.refs_3_ = bf16[8,64,768]{2,1,0:T(8,128)(2,1)S(1)} collective-permute-done((bf16[8,64,768]{2,1,0:T(8,128)(2,1)}, bf16[8,64,768]{2,1,0:T(8,128)(2,1)S(1)}, u32[]{:S(2)}, u32[]{:S(2)}) %collective-permute-start.12) | collective-permute-done | bytes 786464 | tf_op jit(solution)/shard_map/ppermute | solution.py:304
  140.1 4.2 place.3
  147.0 5.3 place.2
  152.3 17.7 %project.1 = (bf16[2048,2048]{1,0:T(8,128)(2,1)}, bf16[2048,2048]{1,0:T(8,128)(2,1)}, bf16[2048,768]{1,0:T(8,128)(2,1)}) custom-call(bf16[2048,2048]{1,0:T(8,128)(2,1)} %all-gather.3.cloned.1.call-done.x_ref, bf16[2048,768]{1,0:T(8,128)(2,1)} %bitcast.136, f32[1,768]{1,0:T(1,128)} %bitcast.162, f32[4,2048]{1,0:T(4,128)} %pad_maximum_fusion.9.n_ref.g_ref, ...), custom_call_target="tpu_custom_call" | custom-call | flops 1 | bytes 1 | tf_op jit(solution)/shard_map/project/pallas_call | solution.py:523
  170.0 4.3 all-to-all-start
  176.2 16.8 %expand.1 = (bf16[2048,1024]{1,0:T(8,128)(2,1)}, bf16[2048,1024]{1,0:T(8,128)(2,1)}) custom-call(bf16[2048,2048]{1,0:T(8,128)(2,1)} %get-tuple-element.80.s_ref.a_ref.b_ref, bf16[2048,1024]{1,0:T(8,128)(2,1)} %bitcast.133, f32[1,1024]{1,0:T(1,128)} %bitcast.160), custom_call_target="tpu_custom_call" | custom-call | flops 1 | bytes 1 | tf_op jit(solution)/shard_map/expand/pallas_call | solution.py:551
  193.0 13.2 %contract.2.refs_0_ = bf16[2048,2048]{1,0:T(8,128)(2,1)} custom-call(bf16[2048,1024]{1,0:T(8,128)(2,1)} %get-tuple-element.81.left_ref.a_ref.b_ref, bf16[1024,2048]{1,0:T(8,128)(2,1)} %w_ref.1), custom_call_target="tpu_custom_call" | custom-call | flops 1 | bytes 1 | tf_op jit(solution)/shard_map/contract/pallas_call | solution.py:574
  209.6 8.3 %attend.1 = bf16[4,2,256,256]{3,2,1,0:T(8,128)(2,1)} custom-call(s32[2,1,1024]{2,1,0:T(1,128)} %get-tuple-element.166.row_ref, s32[2,1024,1]{2,1,0:T(8,128)} %broadcast_in_dim_squeeze.4.col_ref, bf16[4,2,256,768]{3,2,1,0:T(8,128)(2,1)} %copy-done.2), custom_call_target="tpu_custom_call" | custom-call | flops 1 | bytes 1 | tf_op jit(solution)/shard_map/attend/pallas_call | solution.py:737
  217.9 3.7 all-to-all-start.1
  221.5 10.0 %all-gather.5.cloned.1.call-done.right_ref.g_ref = bf16[2048,2048]{1,0:T(8,128)(2,1)} async-done(((bf16[256,2048]{1,0:T(8,128)(2,1)}), bf16[2048,2048]{1,0:T(8,128)(2,1)}) %all-gather.5.cloned.1.call-update) | async-done | bytes 8388624 | tf_op jit(solution)/shard_map/all_gather | solution.py:911
  231.5 6.8 %convolution_convert_fusion = bf16[2048,256]{1,0:T(8,128)(2,1)} fusion(bf16[2048,2048]{1,0:T(8,128)(2,1)} %all-gather.5.cloned.1.call-done.right_ref.g_ref, bf16[256,2048]{1,0:T(8,128)(2,1)S(1)} %copy-done.16), kind=kOutput, calls=%fused_computation.8 | convolution fusion | flops 2148007936 | bytes 10485760 | tf_op jit(solution)/shard_map/dot_general | solution.py:300
  238.3 3.8 all-to-all-start.2
  243.4 8.6 %contract.3 = bf16[2048,2048]{1,0:T(8,128)(2,1)} custom-call(bf16[2048,256]{1,0:T(8,128)(2,1)} %bitcast.140, bf16[256,2048]{1,0:T(8,128)(2,1)} %weight_ref.3, bf16[2048,2048]{1,0:T(8,128)(2,1)} %contract.2.refs_0_), custom_call_target="tpu_custom_call" | custom-call | flops 1 | bytes 1 | tf_op jit(solution)/shard_map/contract/pallas_call | solution.py:574
  252.0 7.0 %grad_pair.4 = (bf16[1,2,64,2048]{3,2,1,0:T(8,128)(2,1)}, bf16[1,2,64,2048]{3,2,1,0:T(8,128)(2,1)}) custom-call(s32[1]{0:T(128)} %bitcast.24.keep_ref.bit_ref, s32[1]{0:T(128)} %bitcast.25.send_ref, bf16[2048,256]{1,0:T(8,128)(2,1)} %bitcast.141, bf16[2048,256]{1,0:T(8,128)(2,1)} %bitcast.142, bf16[2048,2048]{1,0:T(8,128)(2,1)} %all-gather.5.cloned.1.call-done.right_ref.g_ref), custom_call_target="tpu_custom_call" | custom-call | flops 1 | bytes 1 | tf_op jit(solution)/shard_map/grad_pair/pallas_call | solution.py:629
  260.0 13.7 %attend_back.1 = bf16[4,2,256,768]{3,2,1,0:T(8,128)(2,1)} custom-call(s32[2,1,1024]{2,1,0:T(1,128)} %get-tuple-element.166.row_ref, s32[2,1024,1]{2,1,0:T(8,128)} %broadcast_in_dim_squeeze.4.col_ref, f32[2,1024,128]{2,1,0:T(8,128)} %bitcast.146, f32[2,1024,128]{2,1,0:T(8,128)} %bitcast.145, f32[2,1024,128]{2,1,0:T(8,128)} %bitcast.144, ...), custom_call_target="tpu_custom_call" | custom-call | flops 1 | bytes 1 | tf_op jit(solution)/shard_map/attend_back/pallas_call | solution.py:797
  273.8 4.2 all-to-all-start.3
  278.8 14.7 %hidden_back.1 = (bf16[2048,1024]{1,0:T(8,128)(2,1)}, f32[1,1024]{1,0:T(1,128)}) custom-call(bf16[2048,2048]{1,0:T(8,128)(2,1)} %all-gather.5.cloned.1.call-done.right_ref.g_ref, bf16[1024,2048]{1,0:T(8,128)(2,1)} %w_ref.1, bf16[2048,1024]{1,0:T(8,128)(2,1)} %get-tuple-element.91.s_ref), custom_call_target="tpu_custom_call" | custom-call | flops 1 | bytes 1 | tf_op jit(solution)/shard_map/hidden_back/pallas_call | solution.py:600
  293.5 15.1 %grad_pair.5 = (bf16[4,1,128,2048]{3,2,1,0:T(8,128)(2,1)}, bf16[4,1,128,2048]{3,2,1,0:T(8,128)(2,1)}) custom-call(s32[4]{0:T(128)} %get-tuple-element.192.keep_ref, s32[4]{0:T(128)} %get-tuple-element.193.send_ref, bf16[2048,1024]{1,0:T(8,128)(2,1)} %get-tuple-element.81.left_ref.a_ref.b_ref, bf16[2048,1024]{1,0:T(8,128)(2,1)} %get-tuple-element.81.left_ref.a_ref.b_ref, ...), custom_call_target="tpu_custom_call" | custom-call | flops 1 | bytes 1 | tf_op jit(solution)/shard_map/grad_pair/pallas_call | solution.py:629
  313.3 14.7 %grad_pair.6 = (bf16[8,2,64,1024]{3,2,1,0:T(8,128)(2,1)}, bf16[8,2,64,1024]{3,2,1,0:T(8,128)(2,1)}) custom-call(s32[8]{0:T(128)} %stack.213.keep_ref, s32[8]{0:T(128)} %stack.221.send_ref, bf16[2048,2048]{1,0:T(8,128)(2,1)} %get-tuple-element.80.s_ref.a_ref.b_ref, bf16[2048,2048]{1,0:T(8,128)(2,1)} %get-tuple-element.80.s_ref.a_ref.b_ref, ...), custom_call_target="tpu_custom_call" | custom-call | flops 1 | bytes 1 | tf_op jit(solution)/shard_map/grad_pair/pallas_call | solution.py:629
  331.6 13.1 %grad_pair.7 = (bf16[8,2,64,768]{3,2,1,0:T(8,128)(2,1)}, bf16[8,2,64,768]{3,2,1,0:T(8,128)(2,1)}) custom-call(s32[8]{0:T(128)} %stack.196.keep_ref, s32[8]{0:T(128)} %stack.205.send_ref, bf16[2048,2048]{1,0:T(8,128)(2,1)} %get-tuple-element.96.a_ref.b_ref, bf16[2048,2048]{1,0:T(8,128)(2,1)} %get-tuple-element.96.a_ref.b_ref, bf16[2048,768]{1,0:T(8,128)(2,1)} %bitcast.130), custom_call_target="tpu_custom_call" | custom-call | flops 1 | bytes 1 | tf_op jit(solution)/shard_map/grad_pair/pallas_call | solution.py:629
  344.7 15.6 %norm_back.2 = (bf16[2048,2048]{1,0:T(8,128)(2,1)}, f32[4,2048]{1,0:T(4,128)}) custom-call(bf16[2048,2048]{1,0:T(8,128)(2,1)} %all-gather.3.cloned.1.call-done.x_ref, bf16[2048,768]{1,0:T(8,128)(2,1)} %bitcast.131, bf16[2048,1024]{1,0:T(8,128)(2,1)} %get-tuple-element.97.right_ref.h_ref, bf16[2048,768]{1,0:T(8,128)(2,1)} %bitcast.137, ...), custom_call_target="tpu_custom_call" | custom-call | flops 1 | bytes 1 | tf_op jit(solution)/shard_map/norm_back/pallas_call | solution.py:839
  360.6 4.0 add_split.2
  366.2 15.6 %norm_back.3 = (bf16[2048,2048]{1,0:T(8,128)(2,1)}, f32[4,2048]{1,0:T(4,128)}) custom-call(bf16[2048,2048]{1,0:T(8,128)(2,1)} %all-gather.3.cloned.1.call-done.x_ref, bf16[2048,768]{1,0:T(8,128)(2,1)} %bitcast.132, bf16[2048,1024]{1,0:T(8,128)(2,1)} %get-tuple-element.97.right_ref.h_ref, ...), custom_call_target="tpu_custom_call", output_to_operand_aliasing={{0}: (6, {})} | custom-call | flops 1 | bytes 1 | tf_op jit(solution)/shard_map/norm_back/pallas_call | solution.py:839
  381.8 4.5 add_split_two.1
  386.3 6.5 %collective-permute-done.15.b_ref = bf16[8,2,64,768]{3,2,1,0:T(8,128)(2,1)S(1)} collective-permute-done((bf16[8,2,64,768]{3,2,1,0:T(8,128)(2,1)}, bf16[8,2,64,768]{3,2,1,0:T(8,128)(2,1)S(1)}, u32[]{:S(2)}, u32[]{:S(2)}) %collective-permute-start.15) | collective-permute-done | bytes 1572896 | tf_op jit(solution)/shard_map/ppermute | solution.py:304
  393.9 3.1 add_split.3
  400.0 27.7 %collective-permute-done.19 = bf16[10,64,1024]{2,1,0:T(8,128)(2,1)S(1)} collective-permute-done((bf16[10,64,1024]{2,1,0:T(8,128)(2,1)}, bf16[10,64,1024]{2,1,0:T(8,128)(2,1)S(1)}, u32[]{:S(2)}, u32[]{:S(2)}) %collective-permute-start.19) | collective-permute-done | bytes 1310752 | tf_op jit(solution)/shard_map/ppermute | solution.py:304
  431.2 5.4 all-to-all-start.5
  436.7 3.1 add_convert_fusion.1.refs_0_
  445.0 20.6 %collective-permute-done.21.refs_2_ = bf16[1,256,2048]{2,1,0:T(8,128)(2,1)} collective-permute-done((bf16[1,256,2048]{2,1,0:T(8,128)(2,1)}, bf16[1,256,2048]{2,1,0:T(8,128)(2,1)}, u32[]{:S(2)}, u32[]{:S(2)}) %collective-permute-start.21) | collective-permute-done | bytes 1048608 | tf_op jit(solution)/shard_map/ppermute | solution.py:304
  471.6 8.9 %all-to-all-done.5 = bf16[8,64,1024]{2,1,0:T(8,128)(2,1)} async-done(((bf16[8,64,1024]{2,1,0:T(8,128)(2,1)}), bf16[8,64,1024]{2,1,0:T(8,128)(2,1)}, u32[]{:S(2)}, u32[]{:S(2)}) %all-to-all-start.5) | async-done | bytes 1048608 | tf_op jit(solution)/shard_map/all_to_all | solution.py:1034
  480.5 3.6 all-to-all-start.4
  484.1 7.0 %collective-permute-done.22.refs_3_ = bf16[1,256,2048]{2,1,0:T(8,128)(2,1)} collective-permute-done((bf16[1,256,2048]{2,1,0:T(8,128)(2,1)}, bf16[1,256,2048]{2,1,0:T(8,128)(2,1)}, u32[]{:S(2)}, u32[]{:S(2)}) %collective-permute-start.22) | collective-permute-done | bytes 1048608 | tf_op jit(solution)/shard_map/ppermute | solution.py:304
  494.9 25.2 %all-to-all-done.4 = bf16[8,72,768]{2,1,0:T(8,128)(2,1)S(1)} async-done(((bf16[8,72,768]{2,1,0:T(8,128)(2,1)}), bf16[8,72,768]{2,1,0:T(8,128)(2,1)S(1)}, u32[]{:S(2)}, u32[]{:S(2)}) %all-to-all-start.4) | async-done | bytes 884768 | tf_op jit(solution)/shard_map/all_to_all | solution.py:1036
  526.0 19.3 %collective-permute-done.25.refs_2_ = bf16[9,64,768]{2,1,0:T(8,128)(2,1)} collective-permute-done((bf16[9,64,768]{2,1,0:T(8,128)(2,1)S(1)}, bf16[9,64,768]{2,1,0:T(8,128)(2,1)}, u32[]{:S(2)}, u32[]{:S(2)}) %collective-permute-start.25) | collective-permute-done | bytes 884768 | tf_op jit(solution)/shard_map/ppermute | solution.py:304
  550.5 5.4 finish.4
  555.9 14.8 %collective-permute-done.28.refs_3_ = bf16[10,64,1024]{2,1,0:T(8,128)(2,1)} collective-permute-done((bf16[10,64,1024]{2,1,0:T(8,128)(2,1)}, bf16[10,64,1024]{2,1,0:T(8,128)(2,1)}, u32[]{:S(2)}, u32[]{:S(2)}) %collective-permute-start.28) | collective-permute-done | bytes 1310752 | tf_op jit(solution)/shard_map/ppermute | solution.py:304
  578.5 4.1 fusion.6
  582.6 5.4 finish.6
  588.0 5.3 finish.7
  (252 shorter events, 104.9 us)
Async XLA Ops:
  7.2 145.1 %all-gather.3.cloned.1.call-start = ((), (), s32[]{:S(2)}) async-start(), calls=%async_computation.8 | async-start | bytes 9437184 | tf_op jit(solution)/shard_map/all_gather | solution.py:909
  19.3 24.3 %collective-permute-start = (bf16[2,64,1920]{2,1,0:T(8,128)(2,1)}, bf16[2,64,1920]{2,1,0:T(8,128)(2,1)S(1)}, u32[]{:S(2)}, u32[]{:S(2)}) collective-permute-start(bf16[2,64,1920]{2,1,0:T(8,128)(2,1)} %get-tuple-element.73), channel_id=1, source_target_pairs={{0,2},{1,3},{2,0},{3,1},{4,6},{5,7},{6,4},{7,5},{8,10},{9,11},{10,... | collective-permute-start | bytes 1474568 | tf_op jit(solution)/shard_map/ppermute | solution.py:304
  22.4 36.3 %collective-permute-start.1 = (bf16[2,64,1920]{2,1,0:T(8,128)(2,1)}, bf16[2,64,1920]{2,1,0:T(8,128)(2,1)S(1)}, u32[]{:S(2)}, u32[]{:S(2)}) collective-permute-start(bf16[2,64,1920]{2,1,0:T(8,128)(2,1)} %get-tuple-element.74), channel_id=1, source_target_pairs={{0,4},{1,5},{2,6},{3,7},{4,0},{5,1},{6,2},{7,3},{8,12},{9,13},{10,... | collective-permute-start | bytes 1474568 | tf_op jit(solution)/shard_map/ppermute | solution.py:304
  25.0 33.7 %collective-permute-start.2 = (bf16[2,64,1920]{2,1,0:T(8,128)(2,1)}, bf16[2,64,1920]{2,1,0:T(8,128)(2,1)S(1)}, u32[]{:S(2)}, u32[]{:S(2)}) collective-permute-start(bf16[2,64,1920]{2,1,0:T(8,128)(2,1)} %get-tuple-element.75), channel_id=1, source_target_pairs={{0,6},{1,7},{2,4},{3,5},{4,2},{5,3},{6,0},{7,1},{8,14},{9,15},{10,... | collective-permute-start | bytes 1474568 | tf_op jit(solution)/shard_map/ppermute | solution.py:304
  58.8 172.7 %all-gather.5.cloned.1.call-start = ((), (), s32[]{:S(2)}) async-start(), calls=%async_computation.9 | async-start | bytes 9437184 | tf_op jit(solution)/shard_map/all_gather | solution.py:911
  62.9 2.6 collective-permute-start.3
  65.6 481.1 %copy-start.23 = (s32[4]{0:T(128)}, s32[4]{0:T(128)S(1)}, u32[]{:S(2)}) copy-start(s32[4]{0:T(128)S(1)} %get-tuple-element.191.rows_ref) | copy-start | bytes 52
  77.3 24.3 %copy-start.13 = (bf16[8,64,768]{2,1,0:T(8,128)(2,1)}, bf16[8,64,768]{2,1,0:T(8,128)(2,1)S(1)}, u32[]{:S(2)}) copy-start(bf16[8,64,768]{2,1,0:T(8,128)(2,1)S(1)} %slice.224.refs_0_) | copy-start | bytes 2359300
  77.3 33.4 %collective-permute-start.11 = (bf16[8,64,768]{2,1,0:T(8,128)(2,1)S(1)}, bf16[8,64,768]{2,1,0:T(8,128)(2,1)}, u32[]{:S(2)}, u32[]{:S(2)}) collective-permute-start(bf16[8,64,768]{2,1,0:T(8,128)(2,1)S(1)} %slice.224.refs_0_), channel_id=1, source_target_pairs={{0,16},{8,24},{16,0},{24,8},{1,17},{9,25},{17,1},{25,9},{2,18},{10... | collective-permute-start | bytes 2359304 | tf_op jit(solution)/shard_map/ppermute | solution.py:304
  78.8 50.6 %collective-permute-start.10 = (bf16[8,64,768]{2,1,0:T(8,128)(2,1)S(1)}, bf16[8,64,768]{2,1,0:T(8,128)(2,1)}, u32[]{:S(2)}, u32[]{:S(2)}) collective-permute-start(bf16[8,64,768]{2,1,0:T(8,128)(2,1)S(1)} %slice.224.refs_0_), channel_id=1, source_target_pairs={{0,8},{8,0},{16,24},{24,16},{1,9},{9,1},{17,25},{25,17},{2,10},{10... | collective-permute-start | bytes 2359304 | tf_op jit(solution)/shard_map/ppermute | solution.py:304
  81.4 16.8 %collective-permute-start.4 = (s32[2,2,256]{2,1,0:T(2,128)S(1)}, s32[2,2,256]{2,1,0:T(2,128)S(1)}, u32[]{:S(2)}, u32[]{:S(2)}) collective-permute-start(s32[2,2,256]{2,1,0:T(2,128)S(1)} %bitcast.166), channel_id=1, source_target_pairs={{0,8},{8,0},{16,24},{24,16},{1,9},{9,1},{17,25},{25,17},{2,10},{10... | collective-permute-start | bytes 12296 | tf_op jit(solution)/shard_map/ppermute | solution.py:304
  82.1 17.7 %collective-permute-start.5 = (s32[2,2,256]{2,1,0:T(2,128)S(1)}, s32[2,2,256]{2,1,0:T(2,128)S(1)}, u32[]{:S(2)}, u32[]{:S(2)}) collective-permute-start(s32[2,2,256]{2,1,0:T(2,128)S(1)} %bitcast.165), channel_id=1, source_target_pairs={{0,16},{8,24},{16,0},{24,8},{1,17},{9,25},{17,1},{25,9},{2,18},{10... | collective-permute-start | bytes 12296 | tf_op jit(solution)/shard_map/ppermute | solution.py:304
  82.7 17.6 %collective-permute-start.6 = (s32[2,2,256]{2,1,0:T(2,128)S(1)}, s32[2,2,256]{2,1,0:T(2,128)S(1)}, u32[]{:S(2)}, u32[]{:S(2)}) collective-permute-start(s32[2,2,256]{2,1,0:T(2,128)S(1)} %bitcast.164), channel_id=1, source_target_pairs={{0,24},{8,16},{16,8},{24,0},{1,25},{9,17},{17,9},{25,1},{2,26},{10... | collective-permute-start | bytes 12296 | tf_op jit(solution)/shard_map/ppermute | solution.py:304
  87.7 18.7 %copy-start.10 = (bf16[8,64,1024]{2,1,0:T(8,128)(2,1)}, bf16[8,64,1024]{2,1,0:T(8,128)(2,1)S(1)}, u32[]{:S(2)}) copy-start(bf16[8,64,1024]{2,1,0:T(8,128)(2,1)S(1)} %slice.223.refs_0_) | copy-start | bytes 3145732
  98.3 26.1 %collective-permute-start.7 = (bf16[8,64,1024]{2,1,0:T(8,128)(2,1)S(1)}, bf16[8,64,1024]{2,1,0:T(8,128)(2,1)S(1)}, u32[]{:S(2)}, u32[]{:S(2)}) collective-permute-start(bf16[8,64,1024]{2,1,0:T(8,128)(2,1)S(1)} %slice.223.refs_0_), channel_id=1, source_target_pairs={{0,8},{8,0},{16,24},{24,16},{1,9},{9,1},{17,25},{25,17},{2,10},{10... | collective-permute-start | bytes 3145736 | tf_op jit(solution)/shard_map/ppermute | solution.py:304
  99.7 44.5 %collective-permute-start.8 = (bf16[8,64,1024]{2,1,0:T(8,128)(2,1)S(1)}, bf16[8,64,1024]{2,1,0:T(8,128)(2,1)}, u32[]{:S(2)}, u32[]{:S(2)}) collective-permute-start(bf16[8,64,1024]{2,1,0:T(8,128)(2,1)S(1)} %slice.223.refs_0_), channel_id=1, source_target_pairs={{0,16},{8,24},{16,0},{24,8},{1,17},{9,25},{17,1},{25,9},{2,18},{10... | collective-permute-start | bytes 3145736 | tf_op jit(solution)/shard_map/ppermute | solution.py:304
  110.7 28.5 %collective-permute-start.12 = (bf16[8,64,768]{2,1,0:T(8,128)(2,1)}, bf16[8,64,768]{2,1,0:T(8,128)(2,1)S(1)}, u32[]{:S(2)}, u32[]{:S(2)}) collective-permute-start(bf16[8,64,768]{2,1,0:T(8,128)(2,1)} %collective-permute-done.11.refs_2_), channel_id=1, source_target_pairs={{0,8},{8,0},{16,24},{24,16},{1,9},{9,1},{17,25},{25,17},{2,10},{10... | collective-permute-start | bytes 2359304 | tf_op jit(solution)/shard_map/ppermute | solution.py:304
  124.4 21.6 %collective-permute-start.9 = (bf16[8,64,1024]{2,1,0:T(8,128)(2,1)S(1)}, bf16[8,64,1024]{2,1,0:T(8,128)(2,1)S(1)}, u32[]{:S(2)}, u32[]{:S(2)}) collective-permute-start(bf16[8,64,1024]{2,1,0:T(8,128)(2,1)S(1)} %collective-permute-done.7.refs_1_), channel_id=1, source_target_pairs={{0,16},{8,24},{16,0},{24,8},{1,17},{9,25},{17,1},{25,9},{2,18},{10... | collective-permute-start | bytes 3145736 | tf_op jit(solution)/shard_map/ppermute | solution.py:304
  170.0 38.0 %all-to-all-start = ((bf16[4,2,256,768]{3,2,1,0:T(8,128)(2,1)}), bf16[4,2,256,768]{3,2,1,0:T(8,128)(2,1)S(1)}, u32[]{:S(2)}, u32[]{:S(2)}) async-start(bf16[4,2,256,768]{3,2,1,0:T(8,128)(2,1)} %bitcast.147), calls=%async_computation | async-start | bytes 6291456 | tf_op jit(solution)/shard_map/all_to_all | solution.py:949
  217.9 20.4 %all-to-all-start.1 = ((bf16[4,2,256,256]{3,2,1,0:T(8,128)(2,1)}), bf16[4,2,256,256]{3,2,1,0:T(8,128)(2,1)S(1)}, u32[]{:S(2)}, u32[]{:S(2)}) async-start(bf16[4,2,256,256]{3,2,1,0:T(8,128)(2,1)} %attend.1), calls=%async_computation.1 | async-start | bytes 2097152 | tf_op jit(solution)/shard_map/all_to_all | solution.py:954
  238.3 20.7 %all-to-all-start.2 = ((bf16[4,2,256,256]{3,2,1,0:T(8,128)(2,1)}), bf16[4,2,256,256]{3,2,1,0:T(8,128)(2,1)S(1)}, u32[]{:S(2)}, u32[]{:S(2)}) async-start(bf16[4,2,256,256]{3,2,1,0:T(8,128)(2,1)} %bitcast.149), calls=%async_computation.2 | async-start | bytes 2097152 | tf_op jit(solution)/shard_map/all_to_all | solution.py:949
  242.1 154.9 %reduce-scatter.3.cloned.1.call-start = ((), (), s32[]{:S(2)}) async-start(), calls=%async_computation.10 | async-start | bytes 9437184 | tf_op jit(solution)/shard_map/reduce_scatter | solution.py:974
  273.8 56.1 %all-to-all-start.3 = ((bf16[4,2,256,768]{3,2,1,0:T(8,128)(2,1)}), bf16[4,2,256,768]{3,2,1,0:T(8,128)(2,1)S(1)}, u32[]{:S(2)}, u32[]{:S(2)}) async-start(bf16[4,2,256,768]{3,2,1,0:T(8,128)(2,1)} %attend_back.1), calls=%async_computation.4 | async-start | bytes 6291456 | tf_op jit(solution)/shard_map/all_to_all | solution.py:954
  278.0 298.4 %reduce-scatter.5.cloned.1.call-start = ((), (), s32[]{:S(2)}) async-start(), calls=%async_computation.11 | async-start | bytes 9437184 | tf_op jit(solution)/shard_map/reduce_scatter | solution.py:1022
  308.6 51.9 %collective-permute-start.13 = (bf16[1,2,256,2048]{3,2,1,0:T(8,128)(2,1)}, bf16[1,2,256,2048]{3,2,1,0:T(8,128)(2,1)}, u32[]{:S(2)}, u32[]{:S(2)}) collective-permute-start(bf16[1,2,256,2048]{3,2,1,0:T(8,128)(2,1)} %bitcast.167), channel_id=1, source_target_pairs={{0,8},{8,0},{16,24},{24,16},{1,9},{9,1},{17,25},{25,17},{2,10},{10... | collective-permute-start | bytes 6291464 | tf_op jit(solution)/shard_map/ppermute | solution.py:304
  311.8 18.1 %collective-permute-start.14 = (bf16[1,2,64,2048]{3,2,1,0:T(8,128)(2,1)}, bf16[1,2,64,2048]{3,2,1,0:T(8,128)(2,1)}, u32[]{:S(2)}, u32[]{:S(2)}) collective-permute-start(bf16[1,2,64,2048]{3,2,1,0:T(8,128)(2,1)} %get-tuple-element.87), channel_id=1, source_target_pairs={{0,16},{8,24},{16,0},{24,8},{1,17},{9,25},{17,1},{25,9},{2,18},{10... | collective-permute-start | bytes 1572872 | tf_op jit(solution)/shard_map/ppermute | solution.py:304
  328.0 53.8 %collective-permute-start.16 = (bf16[8,2,64,1024]{3,2,1,0:T(8,128)(2,1)}, bf16[8,2,64,1024]{3,2,1,0:T(8,128)(2,1)}, u32[]{:S(2)}, u32[]{:S(2)}) collective-permute-start(bf16[8,2,64,1024]{3,2,1,0:T(8,128)(2,1)} %get-tuple-element.98), channel_id=1, source_target_pairs={{0,16},{8,24},{16,0},{24,8},{1,17},{9,25},{17,1},{25,9},{2,18},{10... | collective-permute-start | bytes 6291464 | tf_op jit(solution)/shard_map/ppermute | solution.py:304
  344.7 48.1 %collective-permute-start.15 = (bf16[8,2,64,768]{3,2,1,0:T(8,128)(2,1)}, bf16[8,2,64,768]{3,2,1,0:T(8,128)(2,1)S(1)}, u32[]{:S(2)}, u32[]{:S(2)}) collective-permute-start(bf16[8,2,64,768]{3,2,1,0:T(8,128)(2,1)} %get-tuple-element.100), channel_id=1, source_target_pairs={{0,8},{8,0},{16,24},{24,16},{1,9},{9,1},{17,25},{25,17},{2,10},{10... | collective-permute-start | bytes 4718600 | tf_op jit(solution)/shard_map/ppermute | solution.py:304
  364.6 32.5 %collective-permute-start.17 = (bf16[1,256,2048]{2,1,0:T(8,128)(2,1)}, bf16[1,256,2048]{2,1,0:T(8,128)(2,1)S(1)}, u32[]{:S(2)}, u32[]{:S(2)}) collective-permute-start(bf16[1,256,2048]{2,1,0:T(8,128)(2,1)} %get-tuple-element.104), channel_id=1, source_target_pairs={{0,16},{8,24},{16,0},{24,8},{1,17},{9,25},{17,1},{25,9},{2,18},{10... | collective-permute-start | bytes 3145736 | tf_op jit(solution)/shard_map/ppermute | solution.py:304
  397.1 31.5 %copy-start.15 = (bf16[10,64,1024]{2,1,0:T(8,128)(2,1)S(1)}, bf16[10,64,1024]{2,1,0:T(8,128)(2,1)}, u32[]{:S(2)}) copy-start(bf16[10,64,1024]{2,1,0:T(8,128)(2,1)} %get-tuple-element.123) | copy-start | bytes 3932164
  398.0 29.6 %collective-permute-start.19 = (bf16[10,64,1024]{2,1,0:T(8,128)(2,1)}, bf16[10,64,1024]{2,1,0:T(8,128)(2,1)S(1)}, u32[]{:S(2)}, u32[]{:S(2)}) collective-permute-start(bf16[10,64,1024]{2,1,0:T(8,128)(2,1)} %get-tuple-element.112), channel_id=1, source_target_pairs={{0,8},{8,0},{16,24},{24,16},{1,9},{9,1},{17,25},{25,17},{2,10},{10... | collective-permute-start | bytes 3932168 | tf_op jit(solution)/shard_map/ppermute | solution.py:304
  398.6 29.0 %collective-permute-start.18 = (bf16[8,64,768]{2,1,0:T(8,128)(2,1)}, bf16[8,64,768]{2,1,0:T(8,128)(2,1)S(1)}, u32[]{:S(2)}, u32[]{:S(2)}) collective-permute-start(bf16[8,64,768]{2,1,0:T(8,128)(2,1)} %get-tuple-element.114), channel_id=1, source_target_pairs={{0,16},{8,24},{16,0},{24,8},{1,17},{9,25},{17,1},{25,9},{2,18},{10... | collective-permute-start | bytes 2359304 | tf_op jit(solution)/shard_map/ppermute | solution.py:304
  431.2 49.4 %all-to-all-start.5 = ((bf16[8,64,1024]{2,1,0:T(8,128)(2,1)}), bf16[8,64,1024]{2,1,0:T(8,128)(2,1)}, u32[]{:S(2)}, u32[]{:S(2)}) async-start(bf16[8,64,1024]{2,1,0:T(8,128)(2,1)} %slice.244), calls=%async_computation.7 | async-start | bytes 2097152 | tf_op jit(solution)/shard_map/all_to_all | solution.py:1034
  439.7 25.9 %collective-permute-start.21 = (bf16[1,256,2048]{2,1,0:T(8,128)(2,1)}, bf16[1,256,2048]{2,1,0:T(8,128)(2,1)}, u32[]{:S(2)}, u32[]{:S(2)}) collective-permute-start(bf16[1,256,2048]{2,1,0:T(8,128)(2,1)} %add_convert_fusion.1.refs_0_), channel_id=1, source_target_pairs={{0,16},{8,24},{16,0},{24,8},{1,17},{9,25},{17,1},{25,9},{2,18},{10... | collective-permute-start | bytes 3145736 | tf_op jit(solution)/shard_map/ppermute | solution.py:304
  443.0 26.0 %collective-permute-start.20 = (bf16[1,256,2048]{2,1,0:T(8,128)(2,1)}, bf16[1,256,2048]{2,1,0:T(8,128)(2,1)}, u32[]{:S(2)}, u32[]{:S(2)}) collective-permute-start(bf16[1,256,2048]{2,1,0:T(8,128)(2,1)} %add_convert_fusion.1.refs_0_), channel_id=1, source_target_pairs={{0,8},{8,0},{16,24},{24,16},{1,9},{9,1},{17,25},{25,17},{2,10},{10... | collective-permute-start | bytes 3145736 | tf_op jit(solution)/shard_map/ppermute | solution.py:304
  465.6 25.5 %collective-permute-start.22 = (bf16[1,256,2048]{2,1,0:T(8,128)(2,1)}, bf16[1,256,2048]{2,1,0:T(8,128)(2,1)}, u32[]{:S(2)}, u32[]{:S(2)}) collective-permute-start(bf16[1,256,2048]{2,1,0:T(8,128)(2,1)} %collective-permute-done.21.refs_2_), channel_id=1, source_target_pairs={{0,8},{8,0},{16,24},{24,16},{1,9},{9,1},{17,25},{25,17},{2,10},{10... | collective-permute-start | bytes 3145736 | tf_op jit(solution)/shard_map/ppermute | solution.py:304
  470.6 20.5 %slice-start = ((bf16[10,64,1024]{2,1,0:T(8,128)(2,1)}), bf16[2,64,1024]{2,1,0:T(8,128)(2,1)S(1)}, s32[]{:S(2)}) async-start(bf16[10,64,1024]{2,1,0:T(8,128)(2,1)} %copy-done.7), calls=%async_computation.12 | async-start | bytes 524288 | tf_op jit(solution)/shard_map/slice | solution.py:1038
  480.5 39.5 %all-to-all-start.4 = ((bf16[8,72,768]{2,1,0:T(8,128)(2,1)}), bf16[8,72,768]{2,1,0:T(8,128)(2,1)S(1)}, u32[]{:S(2)}, u32[]{:S(2)}) async-start(bf16[8,72,768]{2,1,0:T(8,128)(2,1)} %fusion.18), calls=%async_computation.6 | async-start | bytes 1769472 | tf_op jit(solution)/shard_map/all_to_all | solution.py:1036
  492.5 57.0 %copy-start.5 = (bf16[10,64,1024]{2,1,0:T(8,128)(2,1)}, bf16[10,64,1024]{2,1,0:T(8,128)(2,1)S(1)}, u32[]{:S(2)}) copy-start(bf16[10,64,1024]{2,1,0:T(8,128)(2,1)S(1)} %pad_maximum_fusion.4.refs_0_) | copy-start | bytes 3932164
  492.5 56.8 %copy-start.3 = (bf16[1,256,2048]{2,1,0:T(8,128)(2,1)S(1)}, bf16[1,256,2048]{2,1,0:T(8,128)(2,1)}, u32[]{:S(2)}) copy-start(bf16[1,256,2048]{2,1,0:T(8,128)(2,1)} %param.17) | copy-start | bytes 3145732
  492.5 30.1 %collective-permute-start.23 = (bf16[10,64,1024]{2,1,0:T(8,128)(2,1)S(1)}, bf16[10,64,1024]{2,1,0:T(8,128)(2,1)}, u32[]{:S(2)}, u32[]{:S(2)}) collective-permute-start(bf16[10,64,1024]{2,1,0:T(8,128)(2,1)S(1)} %pad_maximum_fusion.4.refs_0_), channel_id=1, source_target_pairs={{0,16},{8,24},{16,0},{24,8},{1,17},{9,25},{17,1},{25,9},{2,18},{10... | collective-permute-start | bytes 3932168 | tf_op jit(solution)/shard_map/ppermute | solution.py:304
  493.7 29.6 %collective-permute-start.27 = (bf16[10,64,1024]{2,1,0:T(8,128)(2,1)S(1)}, bf16[10,64,1024]{2,1,0:T(8,128)(2,1)}, u32[]{:S(2)}, u32[]{:S(2)}) collective-permute-start(bf16[10,64,1024]{2,1,0:T(8,128)(2,1)S(1)} %pad_maximum_fusion.4.refs_0_), channel_id=1, source_target_pairs={{0,8},{8,0},{16,24},{24,16},{1,9},{9,1},{17,25},{25,17},{2,10},{10... | collective-permute-start | bytes 3932168 | tf_op jit(solution)/shard_map/ppermute | solution.py:304
  520.3 53.5 %copy-start.12 = (bf16[9,64,768]{2,1,0:T(8,128)(2,1)}, bf16[9,64,768]{2,1,0:T(8,128)(2,1)S(1)}, u32[]{:S(2)}) copy-start(bf16[9,64,768]{2,1,0:T(8,128)(2,1)S(1)} %pad_maximum_fusion.8.refs_0_) | copy-start | bytes 2654212
  522.6 22.7 %collective-permute-start.25 = (bf16[9,64,768]{2,1,0:T(8,128)(2,1)S(1)}, bf16[9,64,768]{2,1,0:T(8,128)(2,1)}, u32[]{:S(2)}, u32[]{:S(2)}) collective-permute-start(bf16[9,64,768]{2,1,0:T(8,128)(2,1)S(1)} %pad_maximum_fusion.8.refs_0_), channel_id=1, source_target_pairs={{0,16},{8,24},{16,0},{24,8},{1,17},{9,25},{17,1},{25,9},{2,18},{10... | collective-permute-start | bytes 2654216 | tf_op jit(solution)/shard_map/ppermute | solution.py:304
  523.2 47.5 %collective-permute-start.28 = (bf16[10,64,1024]{2,1,0:T(8,128)(2,1)}, bf16[10,64,1024]{2,1,0:T(8,128)(2,1)}, u32[]{:S(2)}, u32[]{:S(2)}) collective-permute-start(bf16[10,64,1024]{2,1,0:T(8,128)(2,1)} %collective-permute-done.27.refs_1_), channel_id=1, source_target_pairs={{0,16},{8,24},{16,0},{24,8},{1,17},{9,25},{17,1},{25,9},{2,18},{10... | collective-permute-start | bytes 3932168 | tf_op jit(solution)/shard_map/ppermute | solution.py:304
  524.7 49.1 %collective-permute-start.24 = (bf16[9,64,768]{2,1,0:T(8,128)(2,1)S(1)}, bf16[9,64,768]{2,1,0:T(8,128)(2,1)}, u32[]{:S(2)}, u32[]{:S(2)}) collective-permute-start(bf16[9,64,768]{2,1,0:T(8,128)(2,1)S(1)} %pad_maximum_fusion.8.refs_0_), channel_id=1, source_target_pairs={{0,8},{8,0},{16,24},{24,16},{1,9},{9,1},{17,25},{25,17},{2,10},{10... | collective-permute-start | bytes 2654216 | tf_op jit(solution)/shard_map/ppermute | solution.py:304
  545.3 28.5 %collective-permute-start.26 = (bf16[9,64,768]{2,1,0:T(8,128)(2,1)}, bf16[9,64,768]{2,1,0:T(8,128)(2,1)}, u32[]{:S(2)}, u32[]{:S(2)}) collective-permute-start(bf16[9,64,768]{2,1,0:T(8,128)(2,1)} %collective-permute-done.25.refs_2_), channel_id=1, source_target_pairs={{0,8},{8,0},{16,24},{24,16},{1,9},{9,1},{17,25},{25,17},{2,10},{10... | collective-permute-start | bytes 2654216 | tf_op jit(solution)/shard_map/ppermute | solution.py:304
  576.4 16.9 %copy-start.24 = (f32[256]{0:T(256)}, f32[256]{0:T(256)S(1)}, u32[]{:S(2)}) copy-start(f32[256]{0:T(256)S(1)} %get-tuple-element.221) | copy-start | bytes 3076
  (20 other events, 74.7 us)
Sparse Core Ops, SparseCore 0:
  58.9 90.3 all-gather.2
  150.9 80.5 all-gather.4
  273.9 93.9 reduce-scatter.2
  397.2 122.5 reduce-scatter.4
